TPU v7x, 32 devices: a whole 2x2x4 slice. The times are simulated.
32 devices in a mesh: section: 2 (over core), dp: 4 (over z), tensor: 4 (over y, x).
Axes of the slice: x: 2, y: 2, z: 4, core: 2. Of those that a mesh axis runs over, the one named last changes fastest.
Arguments:
- latents: bfloat16 [4, 12, 256, 768], P(None, 'dp', 'tensor'), may hold values from -6 to 6
- cond: bfloat16 [4, 12, 768], P(None, 'dp'), may hold values from -6 to 6
- cotangent: bfloat16 [4, 12, 256, 768], P(None, 'dp', 'tensor'), may hold values from -6 to 6
- live: int32 [4, 4], P(None, 'dp'), may hold values from 1 to 3, as said below
- w_qkv: bfloat16 [2, 768, 3, 768], P('section', 'dp', None, 'tensor'), may hold values from -0.21650635 to 0.21650635
- w_proj: bfloat16 [2, 768, 768], P('section', 'tensor', 'dp'), may hold values from -0.625 to 0.625
- w_up: bfloat16 [2, 768, 3072], P('section', 'dp', 'tensor'), may hold values from -0.21875 to 0.21875
- w_down: bfloat16 [2, 3072, 768], P('section', 'tensor', 'dp'), may hold values from -0.109375 to 0.109375
- w_ada: bfloat16 [2, 768, 4608], P('section', 'dp', 'tensor'), may hold values from -0.21650635 to 0.21650635
- bias_qv: bfloat16 [2, 2, 768], P('section', None, ('dp', 'tensor')), may hold values from -3 to 3
- bias_proj: bfloat16 [2, 768], P('section', ('dp', 'tensor')), may hold values from -3 to 3
- bias_up: bfloat16 [2, 3072], P('section', ('dp', 'tensor')), may hold values from -3 to 3
- bias_down: bfloat16 [2, 768], P('section', ('dp', 'tensor')), may hold values from -3 to 3
- bias_ada: bfloat16 [2, 4608], P('section', ('dp', 'tensor')), may hold values from -3 to 3
Outputs:
- layer_out: bfloat16 [2, 4, 12, 256, 768], P('section', None, 'dp', 'tensor')
- input_grad: bfloat16 [2, 4, 12, 256, 768], P('section', None, 'dp', 'tensor')
- cond_grad: bfloat16 [4, 12, 768], P(None, 'dp')
- grad_qkv: float32 [2, 768, 3, 768], P('section', 'dp', None, 'tensor')
- grad_proj: float32 [2, 768, 768], P('section', 'tensor', 'dp')
- grad_up: float32 [2, 768, 3072], P('section', 'dp', 'tensor')
- grad_down: float32 [2, 3072, 768], P('section', 'tensor', 'dp')
- grad_ada: float32 [2, 768, 4608], P('section', 'dp', 'tensor')
- grad_bias_qv: float32 [2, 2, 768], P('section', None, ('dp', 'tensor'))
- grad_bias_proj: float32 [2, 768], P('section', ('dp', 'tensor'))
- grad_bias_up: float32 [2, 3072], P('section', ('dp', 'tensor'))
- grad_bias_down: float32 [2, 768], P('section', ('dp', 'tensor'))
- grad_bias_ada: float32 [2, 4608], P('section', ('dp', 'tensor'))
Inputs may be any that keep to these rules, and one draw needn't show every extreme that they name: live[m, d] latent slots of index d of dp in micro-batch m hold latents; in every micro-batch some index holds 3.
All inputs are finite; a program needn't handle non-finite values.
Results may differ from a plain program's by a relative error of at most 0.02.
Values may be sent and summed in bfloat16 or wider, within the bound.
No kernel may reach another device: no remote copies, remote signals or barrier semaphores. Data moves between devices by JAX's collectives and lax.ppermute only.
A program may use at most 192 MiB of HBM per device.

v0:
```python
import jax
import jax.numpy as jnp
from jax import lax
from jax.sharding import PartitionSpec as P

HEAD_DIM = 64


def shifted(shard, axis, by):
    peers = lax.axis_size(axis)
    pairs = [(i, i + by) for i in range(peers) if 0 <= i + by < peers]
    return lax.ppermute(shard, axis, pairs)


def layer_norm(features):
    centred = features - jnp.mean(features, axis=-1, keepdims=True)
    spread = jnp.mean(centred * centred, axis=-1, keepdims=True)
    return centred * lax.rsqrt(spread + 1e-06)


def gelu_tanh(features):
    return jax.nn.gelu(features, approximate=True)


def split_mod(modulate, model_width):
    return [
        modulate[:, None, column * model_width : (column + 1) * model_width] for column in range(6)
    ]


def gather_tokens(normed):
    return lax.all_gather(normed, "tensor", axis=1, tiled=True)


def gather_grads(grad_share):
    return lax.all_gather(grad_share, "tensor", axis=1, tiled=True)


def branch_terms(source, matrix):
    summed = lax.psum_scatter(
        jnp.einsum("gsd,de->sge", source, matrix, preferred_element_type=jnp.float32).astype(
            jnp.bfloat16
        ),
        "tensor",
        scatter_dimension=0,
        tiled=True,
    ).astype(jnp.float32)
    return jnp.transpose(summed, (1, 0, 2))


def input_terms(source, matrix):
    summed = lax.psum_scatter(
        jnp.einsum("gske,dke->sgd", source, matrix, preferred_element_type=jnp.float32).astype(
            jnp.bfloat16
        ),
        "tensor",
        scatter_dimension=0,
        tiled=True,
    ).astype(jnp.float32)
    return jnp.transpose(summed, (1, 0, 2))


def body(
    latents,
    cond,
    cotangent,
    live,
    w_qkv,
    w_proj,
    w_up,
    w_down,
    w_ada,
    bias_qv,
    bias_proj,
    bias_up,
    bias_down,
    bias_ada,
):
    micros = latents.shape[0]
    slot_count = latents.shape[1]
    model_width = latents.shape[3]
    column_pos = lax.axis_index("tensor")
    is_first = lax.axis_index("section") == 0
    head_scale = HEAD_DIM ** (-0.5)
    qkv_rows, proj_cols, up_rows, down_cols, ada_rows = (
        lax.all_gather(w_qkv[0], "dp", axis=0, tiled=True),
        lax.all_gather(w_proj[0], "dp", axis=1, tiled=True),
        lax.all_gather(w_up[0], "dp", axis=0, tiled=True),
        lax.all_gather(w_down[0], "dp", axis=1, tiled=True),
        lax.all_gather(w_ada[0], "dp", axis=0, tiled=True),
    )
    full_qv, full_proj, full_up, full_down, full_ada = (
        lax.all_gather(bias_qv[0], ("dp", "tensor"), axis=1, tiled=True),
        lax.all_gather(bias_proj[0], ("dp", "tensor"), axis=0, tiled=True),
        lax.all_gather(bias_up[0], ("dp", "tensor"), axis=0, tiled=True),
        lax.all_gather(bias_down[0], ("dp", "tensor"), axis=0, tiled=True),
        lax.all_gather(bias_ada[0], ("dp", "tensor"), axis=0, tiled=True),
    )
    local_width = qkv_rows.shape[2]
    hidden_width = up_rows.shape[1]
    mod_width = ada_rows.shape[1]
    head_local = local_width // HEAD_DIM
    up_rows3 = up_rows.reshape(model_width, 1, hidden_width)
    bias_query = lax.dynamic_slice_in_dim(full_qv[0], column_pos * local_width, local_width).astype(
        jnp.float32
    )
    bias_value = lax.dynamic_slice_in_dim(full_qv[1], column_pos * local_width, local_width).astype(
        jnp.float32
    )
    bias_pack = jnp.stack([bias_query, jnp.zeros_like(bias_query), bias_value], axis=0)
    bias_lift = lax.dynamic_slice_in_dim(full_up, column_pos * hidden_width, hidden_width).astype(
        jnp.float32
    )
    bias_mod = lax.dynamic_slice_in_dim(full_ada, column_pos * mod_width, mod_width).astype(
        jnp.float32
    )
    bias_branch = full_proj.astype(jnp.float32)
    bias_second = full_down.astype(jnp.float32)

    def split_heads(packed):
        seq_len = packed.shape[1]
        queries = packed[:, :, 0].reshape(slot_count, seq_len, head_local, HEAD_DIM)
        key_heads = packed[:, :, 1].reshape(slot_count, seq_len, head_local, HEAD_DIM)
        values = packed[:, :, 2].reshape(slot_count, seq_len, head_local, HEAD_DIM)
        return (queries, key_heads, values)

    def layer_backward(grad_out, saved_values):
        (
            incoming,
            act_cond,
            modulate,
            whole_a,
            packed,
            log_total,
            attended,
            branch,
            middle,
            whole_b,
            lifted,
            second,
        ) = saved_values
        residual_stream = incoming.astype(jnp.float32)
        shift_a, scale_a, gate_a, shift_b, scale_b, gate_b = split_mod(modulate, model_width)
        grad_gate_b = jnp.sum(grad_out * second, axis=1)
        grad_second = (gate_b * grad_out).astype(jnp.bfloat16)
        second_full = gather_grads(grad_second)
        hidden = gelu_tanh(lifted).astype(jnp.bfloat16)
        grad_down = jnp.einsum(
            "gsf,gsd->fd", hidden, second_full, preferred_element_type=jnp.float32
        )
        grad_hidden = jnp.einsum(
            "gsd,fd->gsf", second_full, down_cols, preferred_element_type=jnp.float32
        )
        gelu_unused, gelu_back = jax.vjp(gelu_tanh, lifted)
        grad_lifted = gelu_back(grad_hidden)[0].astype(jnp.bfloat16)
        grad_up = jnp.einsum(
            "gsd,gsf->df", whole_b, grad_lifted, preferred_element_type=jnp.float32
        )
        seq_full = grad_lifted.shape[1]
        grad_normed_b = input_terms(
            grad_lifted.reshape(slot_count, seq_full, 1, hidden_width), up_rows3
        )
        grad_shift_b = jnp.sum(grad_normed_b, axis=1)
        grad_scale_b = jnp.sum(grad_normed_b * layer_norm(middle), axis=1)
        norm_unused, norm_back_b = jax.vjp(layer_norm, middle)
        grad_middle = grad_out + norm_back_b(grad_normed_b * (1.0 + scale_b))[0]
        grad_gate_a = jnp.sum(grad_middle * branch, axis=1)
        grad_branch = (gate_a * grad_middle).astype(jnp.bfloat16)
        branch_full = gather_grads(grad_branch)
        grad_proj = jnp.einsum(
            "gsd,gse->de", attended, branch_full, preferred_element_type=jnp.float32
        )
        grad_attended = jnp.einsum(
            "gse,de->gsd", branch_full, proj_cols, preferred_element_type=jnp.float32
        ).astype(jnp.bfloat16)
        seq_len = grad_attended.shape[1]
        grad_heads = grad_attended.reshape(slot_count, seq_len, head_local, HEAD_DIM)
        queries, key_heads, values = split_heads(packed)
        scores = (
            jnp.einsum("gqhe,gkhe->ghqk", queries, key_heads, preferred_element_type=jnp.float32)
            * head_scale
        )
        probs_exact = jnp.exp(scores - log_total)
        attn_probs = probs_exact.astype(jnp.bfloat16)
        grad_values = jnp.einsum(
            "ghqk,gqhe->gkhe", attn_probs, grad_heads, preferred_element_type=jnp.float32
        )
        grad_probs = jnp.einsum(
            "gqhe,gkhe->ghqk", grad_heads, values, preferred_element_type=jnp.float32
        )
        row_total = jnp.sum(grad_probs * probs_exact, axis=-1, keepdims=True)
        grad_scores = (probs_exact * (grad_probs - row_total)).astype(jnp.bfloat16)
        grad_queries = (
            jnp.einsum(
                "ghqk,gkhe->gqhe", grad_scores, key_heads, preferred_element_type=jnp.float32
            )
            * head_scale
        )
        grad_keys = (
            jnp.einsum("ghqk,gqhe->gkhe", grad_scores, queries, preferred_element_type=jnp.float32)
            * head_scale
        )
        stacked = jnp.stack([grad_queries, grad_keys, grad_values], axis=2)
        grad_packed = stacked.reshape(slot_count, seq_len, 3, local_width).astype(jnp.bfloat16)
        grad_qkv = jnp.einsum(
            "gsd,gske->dke", whole_a, grad_packed, preferred_element_type=jnp.float32
        )
        packed_sums = jnp.sum(grad_packed.astype(jnp.float32), axis=(0, 1))
        grad_normed_a = input_terms(grad_packed, qkv_rows)
        grad_shift_a = jnp.sum(grad_normed_a, axis=1)
        grad_scale_a = jnp.sum(grad_normed_a * layer_norm(residual_stream), axis=1)
        norm_unused_a, norm_back_a = jax.vjp(layer_norm, residual_stream)
        grad_input = grad_middle + norm_back_a(grad_normed_a * (1.0 + scale_a))[0]
        grad_mod_full = jnp.concatenate(
            [grad_shift_a, grad_scale_a, grad_gate_a, grad_shift_b, grad_scale_b, grad_gate_b],
            axis=-1,
        )
        grad_mod = lax.psum_scatter(
            grad_mod_full.astype(jnp.bfloat16), "tensor", scatter_dimension=1, tiled=True
        )
        grad_ada = jnp.einsum("gd,gm->dm", act_cond, grad_mod, preferred_element_type=jnp.float32)
        grad_context = jnp.einsum(
            "gm,dm->gd", grad_mod, ada_rows, preferred_element_type=jnp.float32
        )
        bias_qv_grad = lax.dynamic_update_slice(
            jnp.zeros((2, model_width), jnp.float32),
            jnp.stack([packed_sums[0], packed_sums[2]], axis=0),
            (0, column_pos * local_width),
        )
        bias_up_grad = lax.dynamic_update_slice_in_dim(
            jnp.zeros((hidden_width * lax.axis_size("tensor"),), jnp.float32),
            jnp.sum(grad_lifted.astype(jnp.float32), axis=(0, 1)),
            column_pos * hidden_width,
            0,
        )
        bias_ada_grad = lax.dynamic_update_slice_in_dim(
            jnp.zeros((mod_width * lax.axis_size("tensor"),), jnp.float32),
            jnp.sum(grad_mod.astype(jnp.float32), axis=0),
            column_pos * mod_width,
            0,
        )
        bias_proj_grad = jnp.sum(grad_branch.astype(jnp.float32), axis=(0, 1))
        bias_down_grad = jnp.sum(grad_second.astype(jnp.float32), axis=(0, 1))
        slabs = (grad_qkv, grad_proj, grad_up, grad_down, grad_ada)
        bias_terms = (bias_qv_grad, bias_proj_grad, bias_up_grad, bias_down_grad, bias_ada_grad)
        return (grad_input, slabs, bias_terms, grad_context)

    def choose(early_val, late_val):
        return jnp.where(is_first, early_val, late_val)

    slot_mask = (lax.broadcasted_iota(jnp.int32, (micros, slot_count), 1) < live).astype(
        jnp.float32
    )
    forward_kept = []
    layer_outputs = []
    forwarded_output = None
    for moment in range(micros + 1):
        micro_index = jnp.clip(moment - lax.axis_index("section"), 0, micros - 1)
        own_input = latents[min(moment, micros - 1)]
        if moment > 0:
            arrived = shifted(forwarded_output, "section", 1)
            incoming = jnp.where(is_first, own_input, arrived)
        else:
            incoming = own_input
        context_vector = lax.dynamic_index_in_dim(cond, micro_index, 0, keepdims=False)
        layer_residual_stream = incoming.astype(jnp.float32)
        layer_act_cond = jax.nn.silu(context_vector.astype(jnp.float32)).astype(jnp.bfloat16)
        mod_part = jnp.dot(layer_act_cond, ada_rows, preferred_element_type=jnp.float32) + bias_mod
        layer_modulate = lax.all_gather(mod_part, "tensor", axis=1, tiled=True)
        layer_shift_a, layer_scale_a, layer_gate_a, layer_shift_b, layer_scale_b, layer_gate_b = (
            split_mod(layer_modulate, model_width)
        )
        normed_a = (
            layer_norm(layer_residual_stream) * (1.0 + layer_scale_a) + layer_shift_a
        ).astype(jnp.bfloat16)
        layer_whole_a = gather_tokens(normed_a)
        layer_seq_len = layer_whole_a.shape[1]
        layer_packed = (
            jnp.einsum("gsd,dke->gske", layer_whole_a, qkv_rows, preferred_element_type=jnp.float32)
            + bias_pack
        )
        layer_packed = layer_packed.astype(jnp.bfloat16)
        layer_queries, layer_key_heads, layer_values = split_heads(layer_packed)
        layer_scores = (
            jnp.einsum(
                "gqhe,gkhe->ghqk",
                layer_queries,
                layer_key_heads,
                preferred_element_type=jnp.float32,
            )
            * head_scale
        )
        score_top = jnp.max(layer_scores, axis=-1, keepdims=True)
        exp_scores = jnp.exp(layer_scores - score_top)
        score_sum = jnp.sum(exp_scores, axis=-1, keepdims=True)
        layer_attn_probs = (exp_scores / score_sum).astype(jnp.bfloat16)
        layer_log_total = score_top + jnp.log(score_sum)
        layer_attended = jnp.einsum(
            "ghqk,gkhe->gqhe", layer_attn_probs, layer_values, preferred_element_type=jnp.float32
        )
        layer_attended = layer_attended.reshape(slot_count, layer_seq_len, local_width).astype(
            jnp.bfloat16
        )
        layer_branch = branch_terms(layer_attended, proj_cols) + bias_branch
        layer_middle = layer_residual_stream + layer_gate_a * layer_branch
        normed_b = (layer_norm(layer_middle) * (1.0 + layer_scale_b) + layer_shift_b).astype(
            jnp.bfloat16
        )
        layer_whole_b = gather_tokens(normed_b)
        layer_lifted = (
            jnp.einsum("gsd,df->gsf", layer_whole_b, up_rows, preferred_element_type=jnp.float32)
            + bias_lift
        )
        layer_hidden = gelu_tanh(layer_lifted).astype(jnp.bfloat16)
        layer_second = branch_terms(layer_hidden, down_cols) + bias_second
        output = layer_middle + layer_gate_b * layer_second
        layer_saved_values = (
            incoming,
            layer_act_cond,
            layer_modulate,
            layer_whole_a,
            layer_packed,
            layer_log_total,
            layer_attended,
            layer_branch,
            layer_middle,
            layer_whole_b,
            layer_lifted,
            layer_second,
        )
        output, saved_values = (output, layer_saved_values)
        forwarded_output = output.astype(jnp.bfloat16)
        layer_outputs.append(forwarded_output)
        forward_kept.append(saved_values)
    zero_grad = jnp.zeros(latents.shape[1:], jnp.float32)
    grad_sent = None
    input_grads = []
    context_grads = jnp.zeros((micros, slot_count, model_width), jnp.float32)
    slab_sums = None
    bias_sums = None
    for moment in range(micros + 1):
        if moment > 0:
            back_arrived = shifted(grad_sent, "section", -1).astype(jnp.float32)
        else:
            back_arrived = zero_grad
        if moment < micros:
            from_loss = cotangent[moment].astype(jnp.float32) * slot_mask[moment][:, None, None]
        else:
            from_loss = zero_grad
        grad_out = jnp.where(is_first, back_arrived, from_loss)
        kept_first = forward_kept[max(moment - 1, 0)]
        kept_second = forward_kept[min(moment + 1, micros)]
        saved_values = jax.tree.map(choose, kept_first, kept_second)
        grad_input, slabs, bias_terms, grad_context = layer_backward(grad_out, saved_values)
        grad_sent = grad_input.astype(jnp.bfloat16)
        input_grads.append(grad_sent)
        micro_back = jnp.clip(jnp.where(is_first, moment - 1, moment), 0, micros - 1)
        current = lax.dynamic_index_in_dim(context_grads, micro_back, 0, keepdims=False)
        context_grads = lax.dynamic_update_index_in_dim(
            context_grads, current + grad_context, micro_back, 0
        )
        bias_sums = (
            bias_terms if bias_sums is None else jax.tree.map(jnp.add, bias_sums, bias_terms)
        )
        slab_sums = slabs if slab_sums is None else jax.tree.map(jnp.add, slab_sums, slabs)
    sum_qkv, sum_proj, sum_up, sum_down, sum_ada = slab_sums
    slab_sums = (
        lax.psum_scatter(
            sum_qkv.astype(jnp.bfloat16), "dp", scatter_dimension=0, tiled=True
        ).astype(jnp.float32),
        lax.psum_scatter(
            sum_proj.astype(jnp.bfloat16), "dp", scatter_dimension=1, tiled=True
        ).astype(jnp.float32),
        lax.psum_scatter(sum_up.astype(jnp.bfloat16), "dp", scatter_dimension=0, tiled=True).astype(
            jnp.float32
        ),
        lax.psum_scatter(
            sum_down.astype(jnp.bfloat16), "dp", scatter_dimension=1, tiled=True
        ).astype(jnp.float32),
        lax.psum_scatter(
            sum_ada.astype(jnp.bfloat16), "dp", scatter_dimension=0, tiled=True
        ).astype(jnp.float32),
    )
    shard_qkv, shard_proj, shard_up, shard_down, shard_ada = slab_sums
    sum_bqv, sum_bproj, sum_bup, sum_bdown, sum_bada = bias_sums
    bias_qv_out, bias_proj_out, bias_up_out, bias_down_out, bias_ada_out = (
        lax.psum_scatter(sum_bqv, ("dp", "tensor"), scatter_dimension=1, tiled=True),
        lax.psum_scatter(sum_bproj, ("dp", "tensor"), scatter_dimension=0, tiled=True),
        lax.psum_scatter(sum_bup, ("dp", "tensor"), scatter_dimension=0, tiled=True),
        lax.psum_scatter(sum_bdown, ("dp", "tensor"), scatter_dimension=0, tiled=True),
        lax.psum_scatter(sum_bada, ("dp", "tensor"), scatter_dimension=0, tiled=True),
    )
    total_context = lax.psum(context_grads.astype(jnp.bfloat16), ("section", "tensor")).astype(
        jnp.float32
    )
    silu_unused, silu_back = jax.vjp(jax.nn.silu, cond.astype(jnp.float32))
    cond_grad = silu_back(total_context)[0].astype(jnp.bfloat16)
    layer_out = jnp.stack(
        [choose(layer_outputs[micro], layer_outputs[micro + 1]) for micro in range(micros)], axis=0
    )
    input_grad = jnp.stack(
        [choose(input_grads[micro + 1], input_grads[micro]) for micro in range(micros)], axis=0
    )
    return (
        layer_out[None],
        input_grad[None],
        cond_grad,
        shard_qkv[None],
        shard_proj[None],
        shard_up[None],
        shard_down[None],
        shard_ada[None],
        bias_qv_out[None],
        bias_proj_out[None],
        bias_up_out[None],
        bias_down_out[None],
        bias_ada_out[None],
    )


def solution(mesh):
    return jax.shard_map(
        body,
        mesh=mesh,
        in_specs=(
            P(None, "dp", "tensor", None),
            P(None, "dp", None),
            P(None, "dp", "tensor", None),
            P(None, "dp"),
            P("section", "dp", None, "tensor"),
            P("section", "tensor", "dp"),
            P("section", "dp", "tensor"),
            P("section", "tensor", "dp"),
            P("section", "dp", "tensor"),
            P("section", None, ("dp", "tensor")),
            P("section", ("dp", "tensor")),
            P("section", ("dp", "tensor")),
            P("section", ("dp", "tensor")),
            P("section", ("dp", "tensor")),
        ),
        out_specs=(
            P("section", None, "dp", "tensor", None),
            P("section", None, "dp", "tensor", None),
            P(None, "dp", None),
            P("section", "dp", None, "tensor"),
            P("section", "tensor", "dp"),
            P("section", "dp", "tensor"),
            P("section", "tensor", "dp"),
            P("section", "dp", "tensor"),
            P("section", None, ("dp", "tensor")),
            P("section", ("dp", "tensor")),
            P("section", ("dp", "tensor")),
            P("section", ("dp", "tensor")),
            P("section", ("dp", "tensor")),
        ),
        check_vma=False,
    )
```

profile of v0, /device:TPU:0, one launch (start us, length us, event | category | flops | bytes accessed | tf_op | source)
XLA Modules:
  0.0 2123.4 jit_solution(16264890249895254866)
XLA Ops:
  14.8 79.5 %all-reduce.9 = (bf16[4608]{0:T(1024)(128)(2,1)S(1)}, bf16[768]{0:T(1024)(128)(2,1)S(1)}, bf16[3072]{0:T(1024)(128)(2,1)S(1)}, bf16[768]{0:T(1024)(128)(2,1)S(1)}) all-reduce(bf16[4608]{0:T(1024)(128)(2,1)S(1)} %dynamic-update-slice.12, ...), channel_id=3, replica_groups=mesh['section'=2,'dp'=4,'tensor'=4] {'dp','tensor'}, use_global_device_ids=true, to_apply=%add | all-reduce | flops 9216 | bytes 36864
  148.9 40.9 %all-gather.3 = bf16[1,2,768]{1,0,2:T(2,128)(2,1)S(1)} all-gather(bf16[1,2,48]{1,0,2:T(2,128)(2,1)S(1)} %copy.220), channel_id=5, replica_groups=mesh['section'=2,'dp'=4,'tensor'=4] {'dp','tensor'}, dimensions={2}, use_global_device_ids=true | all-gather | bytes 3264 | tf_op jit(solution)/shard_map/all_gather | solution.py:93
  255.0 29.1 %all-gather.36.cloned.1.call-done = bf16[3,256,768]{2,1,0:T(8,128)(2,1)} async-done(((bf16[3,64,768]{2,1,0:T(8,128)(2,1)}), bf16[3,256,768]{2,1,0:T(8,128)(2,1)}) %all-gather.36.cloned.1.call-update) | async-done | bytes 1179664 | tf_op jit(solution)/shard_map/all_gather | solution.py:32
  286.8 29.2 %all-gather.78.cloned.1.call-done = bf16[1,768,768]{1,2,0:T(8,128)(2,1)} async-done(((bf16[1,768,192]{1,2,0:T(8,128)(2,1)}), bf16[1,768,768]{1,2,0:T(8,128)(2,1)}) %all-gather.78.cloned.1.call-update) | async-done | bytes 1179664 | tf_op jit(solution)/shard_map/all_gather | solution.py:89
  320.0 27.8 %reduce-scatter.48.cloned.1.call-done = bf16[64,3,768]{2,0,1:T(8,128)(2,1)} async-done(((bf16[256,3,768]{2,0,1:T(8,128)(2,1)}), bf16[64,3,768]{2,0,1:T(8,128)(2,1)}) %reduce-scatter.48.cloned.1.call-update) | async-done | bytes 294928 | tf_op jit(solution)/shard_map/reduce_scatter | solution.py:40
  364.1 27.8 %all-gather.38.cloned.1.call-done = bf16[3,256,768]{2,1,0:T(8,128)(2,1)} async-done(((bf16[3,64,768]{2,1,0:T(8,128)(2,1)}), bf16[3,256,768]{2,1,0:T(8,128)(2,1)}) %all-gather.38.cloned.1.call-update) | async-done | bytes 1179664 | tf_op jit(solution)/shard_map/all_gather | solution.py:32
  397.9 28.6 %reduce-scatter.50.cloned.1.call-done = bf16[64,3,768]{2,0,1:T(8,128)(2,1)} async-done(((bf16[256,3,768]{2,0,1:T(8,128)(2,1)}), bf16[64,3,768]{2,0,1:T(8,128)(2,1)}) %reduce-scatter.50.cloned.1.call-update) | async-done | bytes 294928 | tf_op jit(solution)/shard_map/reduce_scatter | solution.py:40
  431.0 27.8 %all-gather.40.cloned.1.call-done = bf16[3,256,768]{2,1,0:T(8,128)(2,1)} async-done(((bf16[3,64,768]{2,1,0:T(8,128)(2,1)}), bf16[3,256,768]{2,1,0:T(8,128)(2,1)}) %all-gather.40.cloned.1.call-update) | async-done | bytes 1179664 | tf_op jit(solution)/shard_map/all_gather | solution.py:32
  465.7 28.6 %reduce-scatter.52.cloned.1.call-done = bf16[64,3,768]{2,0,1:T(8,128)(2,1)} async-done(((bf16[256,3,768]{2,0,1:T(8,128)(2,1)}), bf16[64,3,768]{2,0,1:T(8,128)(2,1)}) %reduce-scatter.52.cloned.1.call-update) | async-done | bytes 294928 | tf_op jit(solution)/shard_map/reduce_scatter | solution.py:40
  510.3 27.8 %all-gather.42.cloned.1.call-done = bf16[3,256,768]{2,1,0:T(8,128)(2,1)} async-done(((bf16[3,64,768]{2,1,0:T(8,128)(2,1)}), bf16[3,256,768]{2,1,0:T(8,128)(2,1)}) %all-gather.42.cloned.1.call-update) | async-done | bytes 1179664 | tf_op jit(solution)/shard_map/all_gather | solution.py:32
  544.7 28.6 %reduce-scatter.54.cloned.1.call-done = bf16[64,3,768]{2,0,1:T(8,128)(2,1)} async-done(((bf16[256,3,768]{2,0,1:T(8,128)(2,1)}), bf16[64,3,768]{2,0,1:T(8,128)(2,1)}) %reduce-scatter.54.cloned.1.call-update) | async-done | bytes 294928 | tf_op jit(solution)/shard_map/reduce_scatter | solution.py:40
  612.5 28.6 %reduce-scatter.56.cloned.1.call-done = bf16[64,3,768]{2,0,1:T(8,128)(2,1)} async-done(((bf16[256,3,768]{2,0,1:T(8,128)(2,1)}), bf16[64,3,768]{2,0,1:T(8,128)(2,1)}) %reduce-scatter.56.cloned.1.call-update) | async-done | bytes 294928 | tf_op jit(solution)/shard_map/reduce_scatter | solution.py:40
  659.2 27.8 %all-gather.46.cloned.1.call-done = bf16[3,256,768]{2,1,0:T(8,128)(2,1)} async-done(((bf16[3,64,768]{2,1,0:T(8,128)(2,1)}), bf16[3,256,768]{2,1,0:T(8,128)(2,1)}) %all-gather.46.cloned.1.call-update) | async-done | bytes 1179664 | tf_op jit(solution)/shard_map/all_gather | solution.py:32
  878.7 28.3 %all-gather.50.cloned.1.call-done = bf16[3,256,768]{2,1,0:T(8,128)(2,1)} async-done(((bf16[3,64,768]{2,1,0:T(8,128)(2,1)}), bf16[3,256,768]{2,1,0:T(8,128)(2,1)}) %all-gather.50.cloned.1.call-update) | async-done | bytes 1179664 | tf_op jit(solution)/shard_map/all_gather | solution.py:32
  921.5 28.0 %reduce-scatter.68.cloned.1.call-done = bf16[64,3,768]{2,0,1:T(8,128)(2,1)} async-done(((bf16[256,3,768]{2,0,1:T(8,128)(2,1)}), bf16[64,3,768]{2,0,1:T(8,128)(2,1)}) %reduce-scatter.68.cloned.1.call-update) | async-done | bytes 294928 | tf_op jit(solution)/shard_map/reduce_scatter | solution.py:52
  959.2 27.6 %all-gather.58.cloned.1.call-done = bf16[3,256,768]{2,1,0:T(8,128)(2,1)} async-done(((bf16[3,64,768]{2,1,0:T(8,128)(2,1)}), bf16[3,256,768]{2,1,0:T(8,128)(2,1)}) %all-gather.58.cloned.1.call-update) | async-done | bytes 1179664 | tf_op jit(solution)/shard_map/all_gather | solution.py:36
  996.4 28.6 %reduce-scatter.70.cloned.1.call-done = bf16[64,3,768]{2,0,1:T(8,128)(2,1)} async-done(((bf16[256,3,768]{2,0,1:T(8,128)(2,1)}), bf16[64,3,768]{2,0,1:T(8,128)(2,1)}) %reduce-scatter.70.cloned.1.call-update) | async-done | bytes 294928 | tf_op jit(solution)/shard_map/reduce_scatter | solution.py:52
  1067.5 27.9 %reduce-scatter.72.cloned.1.call-done = bf16[64,3,768]{2,0,1:T(8,128)(2,1)} async-done(((bf16[256,3,768]{2,0,1:T(8,128)(2,1)}), bf16[64,3,768]{2,0,1:T(8,128)(2,1)}) %reduce-scatter.72.cloned.1.call-update) | async-done | bytes 294928 | tf_op jit(solution)/shard_map/reduce_scatter | solution.py:52
  1338.3 28.6 %reduce-scatter.78.cloned.1.call-done = bf16[64,3,768]{2,0,1:T(8,128)(2,1)} async-done(((bf16[256,3,768]{2,0,1:T(8,128)(2,1)}), bf16[64,3,768]{2,0,1:T(8,128)(2,1)}) %reduce-scatter.78.cloned.1.call-update) | async-done | bytes 294928 | tf_op jit(solution)/shard_map/reduce_scatter | solution.py:52
  1641.1 28.2 %reduce-scatter.94.cloned.1.call-done = bf16[1152,3]{1,0:T(8,128)(2,1)} async-done(((bf16[4608,3]{1,0:T(8,128)(2,1)}), bf16[1152,3]{1,0:T(8,128)(2,1)}) %reduce-scatter.94.cloned.1.call-update) | async-done | bytes 6928
  1673.6 27.6 %reduce-scatter.84.cloned.1.call-done = bf16[64,3,768]{2,0,1:T(8,128)(2,1)} async-done(((bf16[256,3,768]{2,0,1:T(8,128)(2,1)}), bf16[64,3,768]{2,0,1:T(8,128)(2,1)}) %reduce-scatter.84.cloned.1.call-update) | async-done | bytes 294928 | tf_op jit(solution)/shard_map/reduce_scatter | solution.py:52
  1842.7 110.7 %reduce-scatter.106.cloned.1.call-done = f32[48,2]{1,0:T(8,128)} async-done(((f32[768,2]{1,0:T(8,128)}), f32[48,2]{1,0:T(8,128)}) %reduce-scatter.106.cloned.1.call-update) | async-done | bytes 400
  1977.8 27.9 %reduce-scatter.86.cloned.1.call-done = bf16[192,3,192]{2,0,1:T(8,128)(2,1)} async-done(((bf16[768,3,192]{2,0,1:T(8,128)(2,1)}), bf16[192,3,192]{2,0,1:T(8,128)(2,1)}) %reduce-scatter.86.cloned.1.call-update) | async-done | bytes 221200 | tf_op jit(solution)/shard_map/reduce_scatter | solution.py:368
  2010.9 75.9 %all-reduce.8 = (f32[768]{0:T(1024)S(1)}, f32[3072]{0:T(1024)S(1)}, f32[768]{0:T(1024)S(1)}, f32[4608]{0:T(1024)S(1)}) all-reduce(f32[768]{0:T(1024)S(1)} %copy-done.276, f32[3072]{0:T(1024)} %add_dynamic-update-slice_fusion.4, f32[768]{0:T(1024)S(1)} %add_add_fusion.14, ...), channel_id=43, replica_groups=mesh['section'=2,'dp'=4,'tensor'=4] {'dp','tensor'}, use_global_device_ids=true, to_apply=%region_147.148.clone | all-reduce | flops 9216 | bytes 73728
  (1239 shorter events, 1228.9 us)
Async XLA Ops:
  7.2 91.1 %all-gather.74.cloned.1.call-start = ((), (), s32[]{:S(2)}) async-start(), calls=%async_computation.75 | async-start | bytes 2211840 | tf_op jit(solution)/shard_map/all_gather | solution.py:90
  8.0 183.8 %all-gather.34.cloned.1.call-start = ((), (), s32[]{:S(2)}) async-start(), calls=%async_computation.31 | async-start | bytes 1474560 | tf_op jit(solution)/shard_map/all_gather | solution.py:32
  107.9 115.2 %reduce-scatter.46.cloned.1.call-start = ((), (), s32[]{:S(2)}) async-start(), calls=%async_computation.32 | async-start | bytes 1474560 | tf_op jit(solution)/shard_map/reduce_scatter | solution.py:40
  227.4 88.6 %all-gather.78.cloned.1.call-start = ((), (), s32[]{:S(2)}) async-start(), calls=%async_computation.77 | async-start | bytes 1474560 | tf_op jit(solution)/shard_map/all_gather | solution.py:89
  228.0 119.8 %reduce-scatter.48.cloned.1.call-start = ((), (), s32[]{:S(2)}) async-start(), calls=%async_computation.34 | async-start | bytes 1474560 | tf_op jit(solution)/shard_map/reduce_scatter | solution.py:40
  726.8 87.7 %reduce-scatter.66.cloned.1.call-start = ((), (), s32[]{:S(2)}) async-start(), calls=%async_computation.52 | async-start | bytes 1474560 | tf_op jit(solution)/shard_map/reduce_scatter | solution.py:52
  789.3 87.5 %all-gather.56.cloned.1.call-start = ((), (), s32[]{:S(2)}) async-start(), calls=%async_computation.53 | async-start | bytes 1474560 | tf_op jit(solution)/shard_map/all_gather | solution.py:36
  820.6 86.4 %all-gather.50.cloned.1.call-start = ((), (), s32[]{:S(2)}) async-start(), calls=%async_computation.47 | async-start | bytes 1474560 | tf_op jit(solution)/shard_map/all_gather | solution.py:32
  855.8 93.6 %reduce-scatter.68.cloned.1.call-start = ((), (), s32[]{:S(2)}) async-start(), calls=%async_computation.54 | async-start | bytes 1474560 | tf_op jit(solution)/shard_map/reduce_scatter | solution.py:52
  1110.9 88.0 %reduce-scatter.74.cloned.1.call-start = ((), (), s32[]{:S(2)}) async-start(), calls=%async_computation.60 | async-start | bytes 1474560 | tf_op jit(solution)/shard_map/reduce_scatter | solution.py:52
  1144.4 89.1 %all-gather.64.cloned.1.call-start = ((), (), s32[]{:S(2)}) async-start(), calls=%async_computation.61 | async-start | bytes 1474560 | tf_op jit(solution)/shard_map/all_gather | solution.py:36
  1241.1 87.7 %all-gather.66.cloned.1.call-start = ((), (), s32[]{:S(2)}) async-start(), calls=%async_computation.63 | async-start | bytes 1474560 | tf_op jit(solution)/shard_map/all_gather | solution.py:36
  1280.0 86.9 %reduce-scatter.78.cloned.1.call-start = ((), (), s32[]{:S(2)}) async-start(), calls=%async_computation.64 | async-start | bytes 1474560 | tf_op jit(solution)/shard_map/reduce_scatter | solution.py:52
  1489.5 104.7 %all-gather.72.cloned.1.call-start = ((), (), s32[]{:S(2)}) async-start(), calls=%async_computation.69 | async-start | bytes 1474560 | tf_op jit(solution)/shard_map/all_gather | solution.py:36
  1575.3 94.0 %reduce-scatter.94.cloned.1.call-start = ((), (), s32[]{:S(2)}) async-start(), calls=%async_computation.78 | async-start | bytes 1474560
  1594.2 107.0 %reduce-scatter.84.cloned.1.call-start = ((), (), s32[]{:S(2)}) async-start(), calls=%async_computation.70 | async-start | bytes 1474560 | tf_op jit(solution)/shard_map/reduce_scatter | solution.py:52
  1601.6 131.0 %reduce-scatter.96.cloned.1.call-start = ((), (), s32[]{:S(2)}) async-start(), calls=%async_computation.79 | async-start | bytes 1474560
  1613.0 150.9 %reduce-scatter.98.cloned.1.call-start = ((), (), s32[]{:S(2)}) async-start(), calls=%async_computation.80 | async-start | bytes 1474560
  1614.7 180.5 %reduce-scatter.100.cloned.1.call-start = ((), (), s32[]{:S(2)}) async-start(), calls=%async_computation.81 | async-start | bytes 1474560
  1616.3 211.0 %reduce-scatter.102.cloned.1.call-start = ((), (), s32[]{:S(2)}) async-start(), calls=%async_computation.82 | async-start | bytes 1474560
  1707.7 245.7 %reduce-scatter.106.cloned.1.call-start = ((), (), s32[]{:S(2)}) async-start(), calls=%async_computation.84 | async-start | bytes 417792
  1712.3 263.8 %reduce-scatter.104.cloned.1.call-start = ((), (), s32[]{:S(2)}) async-start(), calls=%async_computation.83 | async-start | bytes 491520
  1715.2 290.6 %reduce-scatter.86.cloned.1.call-start = ((), (), s32[]{:S(2)}) async-start(), calls=%async_computation.71 | async-start | bytes 1474560 | tf_op jit(solution)/shard_map/reduce_scatter | solution.py:368
  1722.0 392.1 %reduce-scatter.92.cloned.1.call-start = ((), (), s32[]{:S(2)}) async-start(), calls=%async_computation.74 | async-start | bytes 2211840 | tf_op jit(solution)/shard_map/reduce_scatter | solution.py:380
  (368 other events, 8774.9 us)
Sparse Core Ops, SparseCore 0:
  9.6 43.7 all-gather.73
  224.5 30.4 all-gather.75
  285.5 30.4 all-gather.77
  398.0 28.5 reduce-scatter.49
  465.8 28.5 reduce-scatter.51
  544.8 28.5 reduce-scatter.53
  612.6 28.5 reduce-scatter.55
  693.9 28.5 reduce-scatter.57
  786.0 28.5 reduce-scatter.65
  818.1 28.5 reduce-scatter.59
  920.8 28.5 reduce-scatter.67
  996.4 28.5 reduce-scatter.69
  1066.7 28.5 reduce-scatter.71
  1138.2 28.5 reduce-scatter.61
  1240.5 28.5 reduce-scatter.75
  1338.3 28.5 reduce-scatter.77
  1408.1 28.5 reduce-scatter.79
  1451.5 28.5 all-gather.69
  1483.6 28.5 reduce-scatter.63
  1579.8 29.1 reduce-scatter.89
  1672.6 28.5 reduce-scatter.83
  1766.7 28.5 reduce-scatter.99
  1831.8 121.6 reduce-scatter.105
  2008.1 37.7 reduce-scatter.91
  (30 shorter events, 819.0 us)
where the time goes:
time: 2140 us; the launch traced here: 2120 us
  waiting for transfers between devices  1310 us (61%)
  blocking collectives  298 us (14%)
  matrix products  225 us (11%)
  other arithmetic  172 us (8%)
  local copies, waits for them, and re-layouts  82.5 us (4%)
  between operations  22.7 us (1%)
    reduce_scatter x10, waiting for transfers between devices, input_terms(): lax.psum_scatter(jnp.einsum('gske,dke->sgd', source, matrix, preferred_el...  261 us
    unnamed x61, waiting for transfers between devices  254 us
    reduce_scatter x10, waiting for transfers between devices, branch_terms(): lax.psum_scatter(jnp.einsum('gsd,de->sge', source, matrix, preferred_elem...  245 us
    all_gather x10, waiting for transfers between devices, gather_tokens(): return lax.all_gather(normed, 'tensor', axis=1, tiled=True)  235 us
    all_gather x10, waiting for transfers between devices, gather_grads(): return lax.all_gather(grad_share, 'tensor', axis=1, tiled=True)  202 us
    unnamed x2, blocking collectives  155 us
    unnamed x713, local copies, waits for them, and re-layouts  54.2 us
  transfers between devices with their start and end apart: 62, of which 52 were waited for; matrix products, arithmetic and copies ran while one was open for 14% of the time, Pallas kernels for 0%

commit v1 on v0

v1 whole, which is shorter than its diff:
```python
import jax
import jax.numpy as jnp
from jax import lax
from jax.sharding import PartitionSpec as P

HEAD_DIM = 64
BF16 = jnp.bfloat16
F32 = jnp.float32


def layer_norm(features):
    centred = features - jnp.mean(features, axis=-1, keepdims=True)
    spread = jnp.mean(centred * centred, axis=-1, keepdims=True)
    return centred * lax.rsqrt(spread + 1e-06)


def gelu_tanh(features):
    return jax.nn.gelu(features, approximate=True)


def swap(shard, axis, step):
    peers = lax.axis_size(axis)
    return lax.ppermute(shard, axis, [(i, i ^ step) for i in range(peers)])


def turned(shard, axis, by):
    peers = lax.axis_size(axis)
    return lax.ppermute(shard, axis, [(i, (i + by) % peers) for i in range(peers)])


def pick(blocks, index):
    return lax.dynamic_index_in_dim(blocks, index, 0, keepdims=False)


def direct_dp():
    return lax.axis_size("dp") == 4


def gather_dp(shard):
    peers = lax.axis_size("dp")
    if not direct_dp():
        return lax.all_gather(shard, "dp", axis=0, tiled=True)
    place = lax.axis_index("dp")
    whole = jnp.zeros((peers,) + shard.shape, shard.dtype)
    for k in range(peers):
        piece = shard if k == 0 else turned(shard, "dp", k)
        whole = lax.dynamic_update_index_in_dim(whole, piece, (place - k) % peers, 0)
    return whole.reshape((peers * shard.shape[0],) + shard.shape[1:])


def scatter_dp(whole):
    peers = lax.axis_size("dp")
    if not direct_dp():
        return lax.psum_scatter(whole, "dp", scatter_dimension=0, tiled=True).astype(F32)
    place = lax.axis_index("dp")
    blocks = whole.reshape((peers, whole.shape[0] // peers) + whole.shape[1:])
    total = pick(blocks, place).astype(F32)
    for k in range(1, peers):
        total = total + turned(pick(blocks, (place + k) % peers), "dp", k).astype(F32)
    return total


def send_dp(blocks):
    peers = lax.axis_size("dp")
    if not direct_dp():
        return lax.all_to_all(blocks, "dp", 0, 0)
    place = lax.axis_index("dp")
    return jnp.stack(
        [pick(blocks, place)]
        + [turned(pick(blocks, (place + k) % peers), "dp", k) for k in range(1, peers)]
    )


def share_dp(shard):
    peers = lax.axis_size("dp")
    if not direct_dp():
        return lax.all_gather(shard, "dp")
    return jnp.stack([shard] + [turned(shard, "dp", k) for k in range(1, peers)])


def return_dp(blocks):
    peers = lax.axis_size("dp")
    if not direct_dp():
        return lax.all_to_all(blocks, "dp", 0, 0)
    place = lax.axis_index("dp")
    arrived = jnp.stack([blocks[0]] + [turned(blocks[k], "dp", -k) for k in range(1, peers)])
    return jnp.stack([pick(arrived, (a - place) % peers) for a in range(peers)])


def ordered(blocks):
    own = lax.axis_index("tensor")
    return jnp.stack([pick(blocks, b ^ own) for b in range(blocks.shape[0])])


def send_tensor(blocks):
    own = lax.axis_index("tensor")
    return [pick(blocks, own)] + [
        swap(pick(blocks, own ^ j), "tensor", j) for j in range(1, lax.axis_size("tensor"))
    ]


def spread_tensor(own, first, second):
    near = swap(own, "tensor", first)
    side = swap(own, "tensor", second)
    far = swap(near, "tensor", second)
    pieces = {0: own, first: near, second: side, first ^ second: far}
    return [pieces[j] for j in range(4)]


def collect_tensor(pieces, first, second):
    near = swap(pieces[first], "tensor", first)
    far = swap(pieces[first ^ second], "tensor", first)
    keep = pieces[0].astype(F32) + near.astype(F32)
    onward = (pieces[second].astype(F32) + far.astype(F32)).astype(BF16)
    return (keep + swap(onward, "tensor", second).astype(F32)).astype(BF16)


def dot(lhs, rhs, spec):
    return jnp.einsum(spec, lhs, rhs, preferred_element_type=F32)


def split_mod(modulate, width):
    return [modulate[:, None, i * width : (i + 1) * width] for i in range(6)]


def heads_of(packed):
    latents, tokens, width = packed.shape
    parts = packed.reshape(latents, tokens, 3, width // (3 * HEAD_DIM), HEAD_DIM)
    return parts[:, :, 0], parts[:, :, 1], parts[:, :, 2]


def layer_forward(incoming, modulate, weights, biases):
    w_pack, w_projt, w_up, w_downt = weights
    b_pack, b_proj, b_up, b_down = biases
    latents, tokens, width = incoming.shape
    shift_a, scale_a, gate_a, shift_b, scale_b, gate_b = split_mod(modulate, width)
    residual = incoming.astype(F32)
    normed_a = (layer_norm(residual) * (1.0 + scale_a) + shift_a).astype(BF16)
    packed = (dot(normed_a, w_pack, "gsd,dn->gsn") + b_pack).astype(BF16)
    queries, keys, values = heads_of(packed)
    scores = dot(queries, keys, "gqhe,gkhe->ghqk") * HEAD_DIM**-0.5
    top = jnp.max(scores, axis=-1, keepdims=True)
    raised = jnp.exp(scores - top)
    total = jnp.sum(raised, axis=-1, keepdims=True)
    probs = (raised / total).astype(BF16)
    log_total = top + jnp.log(total)
    attended = dot(probs, values, "ghqk,gkhe->gqhe").reshape(latents, tokens, width).astype(BF16)
    branch = dot(attended, w_projt, "gse,ne->gsn") + b_proj
    middle = residual + gate_a * branch
    normed_b = (layer_norm(middle) * (1.0 + scale_b) + shift_b).astype(BF16)
    lifted = dot(normed_b, w_up, "gsd,df->gsf") + b_up
    hidden = gelu_tanh(lifted).astype(BF16)
    second = dot(hidden, w_downt, "gsf,nf->gsn") + b_down
    output = (middle + gate_b * second).astype(BF16)
    saved = (
        normed_a,
        packed,
        log_total,
        attended,
        branch.astype(BF16),
        middle,
        normed_b,
        lifted.astype(BF16),
        hidden,
        second.astype(BF16),
    )
    return output, saved


def layer_backward(grad_out, incoming, modulate, weights, saved):
    w_pack, w_projt, w_up, w_downt = weights
    normed_a, packed, log_total, attended, branch, middle, normed_b, lifted, hidden, second = saved
    latents, tokens, width = incoming.shape
    shift_a, scale_a, gate_a, shift_b, scale_b, gate_b = split_mod(modulate, width)
    residual = incoming.astype(F32)
    grad_gate_b = jnp.sum(grad_out * second.astype(F32), axis=1)
    grad_second = (gate_b * grad_out).astype(BF16)
    grad_hidden = dot(grad_second, w_downt, "gsn,nf->gsf")
    gelu_back = jax.vjp(gelu_tanh, lifted.astype(F32))[1]
    grad_lifted = gelu_back(grad_hidden)[0].astype(BF16)
    grad_normed_b = dot(grad_lifted, w_up, "gsf,df->gsd")
    grad_shift_b = jnp.sum(grad_normed_b, axis=1)
    unit_b, norm_back_b = jax.vjp(layer_norm, middle)
    grad_scale_b = jnp.sum(grad_normed_b * unit_b, axis=1)
    grad_middle = grad_out + norm_back_b(grad_normed_b * (1.0 + scale_b))[0]
    grad_gate_a = jnp.sum(grad_middle * branch.astype(F32), axis=1)
    grad_branch = (gate_a * grad_middle).astype(BF16)
    grad_attended = dot(grad_branch, w_projt, "gsn,ne->gse").astype(BF16)
    grad_heads = grad_attended.reshape(latents, tokens, width // HEAD_DIM, HEAD_DIM)
    queries, keys, values = heads_of(packed)
    scores = dot(queries, keys, "gqhe,gkhe->ghqk") * HEAD_DIM**-0.5
    probs_exact = jnp.exp(scores - log_total)
    probs = probs_exact.astype(BF16)
    grad_values = dot(probs, grad_heads, "ghqk,gqhe->gkhe")
    grad_probs = dot(grad_heads, values, "gqhe,gkhe->ghqk")
    row_total = jnp.sum(grad_probs * probs_exact, axis=-1, keepdims=True)
    grad_scores = (probs_exact * (grad_probs - row_total)).astype(BF16)
    grad_queries = dot(grad_scores, keys, "ghqk,gkhe->gqhe") * HEAD_DIM**-0.5
    grad_keys = dot(grad_scores, queries, "ghqk,gqhe->gkhe") * HEAD_DIM**-0.5
    grad_packed = jnp.stack([grad_queries, grad_keys, grad_values], axis=2)
    grad_packed = grad_packed.reshape(latents, tokens, 3 * width).astype(BF16)
    grad_normed_a = dot(grad_packed, w_pack, "gsn,dn->gsd")
    grad_shift_a = jnp.sum(grad_normed_a, axis=1)
    unit_a, norm_back_a = jax.vjp(layer_norm, residual)
    grad_scale_a = jnp.sum(grad_normed_a * unit_a, axis=1)
    grad_input = grad_middle + norm_back_a(grad_normed_a * (1.0 + scale_a))[0]
    grad_mod = jnp.concatenate(
        [grad_shift_a, grad_scale_a, grad_gate_a, grad_shift_b, grad_scale_b, grad_gate_b], axis=-1
    ).astype(BF16)
    slabs = (
        dot(normed_a, grad_packed, "gsd,gsn->dn").astype(BF16),
        dot(grad_branch, attended, "gsn,gse->ne").astype(BF16),
        dot(normed_b, grad_lifted, "gsd,gsf->df").astype(BF16),
        dot(grad_second, hidden, "gsn,gsf->nf").astype(BF16),
    )
    bias_sums = tuple(
        jnp.sum(part.astype(F32), axis=(0, 1))
        for part in (grad_packed, grad_branch, grad_lifted, grad_second)
    )
    return grad_input.astype(BF16), grad_mod, slabs, bias_sums


def zeros_like_shapes(shapes):
    return jax.tree.map(lambda s: jnp.zeros(s.shape, s.dtype), shapes)


def body(
    latents,
    cond,
    cotangent,
    live,
    w_qkv,
    w_proj,
    w_up,
    w_down,
    w_ada,
    bias_qv,
    bias_proj,
    bias_up,
    bias_down,
    bias_ada,
):
    micros, slots, tokens_own, width = latents.shape
    ways = lax.axis_size("tensor")
    dps = lax.axis_size("dp")
    share = micros * slots // ways
    own_t = lax.axis_index("tensor")
    is_first = lax.axis_index("section") == 0
    qkv_cols = w_qkv.shape[3]
    hidden_cols = w_up.shape[2]
    mod_cols = w_ada.shape[2]
    mod_w = w_ada[0]

    pack_shard = jnp.concatenate(
        [w_qkv[0, :, 0], w_qkv[0, :, 1], w_qkv[0, :, 2], w_proj[0].T], axis=1
    )
    pack_own = gather_dp(pack_shard)
    up_own = gather_dp(w_up[0])
    down_own = gather_dp(w_down[0].T)
    qk_parts = spread_tensor(pack_own[:, : 2 * qkv_cols], 1, 2)
    vp_parts = spread_tensor(pack_own[:, 2 * qkv_cols :], 2, 1)
    up_parts = spread_tensor(up_own, 1, 2)
    down_parts = spread_tensor(down_own, 2, 1)

    source = jnp.where(is_first, latents, cotangent).reshape(ways, share, tokens_own, width)
    tokens_in = jnp.concatenate(send_tensor(source), axis=1)

    bias_shard = jnp.concatenate(
        [bias_qv[0, 0], bias_qv[0, 1], bias_proj[0], bias_up[0], bias_down[0], bias_ada[0]]
    )
    cuts = [bias_qv.shape[2]] * 2 + [b.shape[1] for b in (bias_proj, bias_up, bias_down, bias_ada)]
    bias_dp = gather_dp(bias_shard[None])
    bias_rel = jnp.stack(
        [bias_dp] + [swap(bias_dp, "tensor", j) for j in range(1, ways)]
    )
    bias_all = jnp.transpose(ordered(bias_rel), (1, 0, 2)).astype(F32)
    full, start = [], 0
    for cut in cuts:
        full.append(bias_all[:, :, start : start + cut].reshape(-1))
        start += cut
    full_q, full_v, full_proj, full_up, full_down, full_ada = full
    by_xor = lambda vector: ordered(vector.reshape(ways, -1)).reshape(-1)
    bias_pack = jnp.concatenate([by_xor(full_q), jnp.zeros_like(full_q), by_xor(full_v)])
    biases = (bias_pack, full_proj, by_xor(full_up), full_down)

    context = cond.reshape(micros * slots, width)
    act = jax.nn.silu(context.astype(F32)).astype(BF16)
    act_blocks = jnp.transpose(act.reshape(micros * slots, dps, width // dps), (1, 0, 2))
    act_all = send_dp(act_blocks)
    mod_terms = return_dp(dot(act_all, mod_w, "kgd,dm->kgm"))
    bias_mod = lax.dynamic_slice_in_dim(full_ada, own_t * mod_cols, mod_cols)
    mod_block = jnp.sum(mod_terms, axis=0) + bias_mod
    mod_rel = jnp.stack(send_tensor(mod_block.reshape(ways, share, mod_cols)))
    modulate = jnp.transpose(ordered(mod_rel), (1, 0, 2)).reshape(share, ways * mod_cols)

    weights = (
        jnp.concatenate(
            [part[:, :qkv_cols] for part in qk_parts]
            + [part[:, qkv_cols:] for part in qk_parts]
            + [part[:, :qkv_cols] for part in vp_parts],
            axis=1,
        ),
        jnp.concatenate([part[:, qkv_cols:] for part in vp_parts], axis=1),
        jnp.concatenate(up_parts, axis=1),
        jnp.concatenate(down_parts, axis=1),
    )

    slot_mask = (lax.broadcasted_iota(jnp.int32, (micros, slots), 1) < live).astype(F32)
    own_mask = pick(slot_mask.reshape(ways, share), own_t)

    def first_forward(args):
        tokens, modulate, weights, biases = args
        return layer_forward(tokens, modulate, weights, biases)

    args = (tokens_in, modulate, weights, biases)
    shapes = jax.eval_shape(first_forward, args)
    output_first, saved_first = lax.cond(
        is_first, first_forward, lambda args: zeros_like_shapes(shapes), args
    )
    arrived = lax.ppermute(output_first, "section", [(0, 1)])

    def second_both(args):
        arrived, tokens, own_mask, modulate, weights, biases = args
        output, saved = layer_forward(arrived, modulate, weights, biases)
        grad_out = tokens.astype(F32) * own_mask[:, None, None]
        return output, layer_backward(grad_out, arrived, modulate, weights, saved)

    args = (arrived, tokens_in, own_mask, modulate, weights, biases)
    shapes_both = jax.eval_shape(second_both, args)
    output_second, grads_second = lax.cond(
        is_first, lambda args: zeros_like_shapes(shapes_both), second_both, args
    )
    back = lax.ppermute(grads_second[0], "section", [(1, 0)])

    def first_backward(args):
        back, tokens, modulate, weights, saved, other = args
        return layer_backward(back.astype(F32), tokens, modulate, weights, saved)

    args = (back, tokens_in, modulate, weights, saved_first, grads_second)
    grad_input, grad_mod, slabs, bias_sums = lax.cond(
        is_first, first_backward, lambda args: args[-1], args
    )
    output = jnp.where(is_first, output_first, output_second)

    g_pack, g_projt, g_up, g_downt = slabs
    third = qkv_cols * ways
    g_qk = [
        jnp.concatenate(
            [
                g_pack[:, j * qkv_cols : (j + 1) * qkv_cols],
                g_pack[:, third + j * qkv_cols : third + (j + 1) * qkv_cols],
            ],
            axis=1,
        )
        for j in range(ways)
    ]
    g_vp = [
        jnp.concatenate(
            [
                g_pack[:, 2 * third + j * qkv_cols : 2 * third + (j + 1) * qkv_cols],
                g_projt[:, j * qkv_cols : (j + 1) * qkv_cols],
            ],
            axis=1,
        )
        for j in range(ways)
    ]
    blocks = lambda whole: [
        whole[:, j * hidden_cols : (j + 1) * hidden_cols] for j in range(ways)
    ]
    out_down = scatter_dp(collect_tensor(blocks(g_downt), 2, 1))
    out_up = scatter_dp(collect_tensor(blocks(g_up), 1, 2))
    out_pack = scatter_dp(
        jnp.concatenate([collect_tensor(g_qk, 1, 2), collect_tensor(g_vp, 2, 1)], axis=1)
    )
    shard_qkv = out_pack[:, : 3 * qkv_cols].reshape(-1, 3, qkv_cols)
    shard_proj = out_pack[:, 3 * qkv_cols :].T
    shard_up = out_up
    shard_down = out_down.T

    grad_groups = jnp.transpose(grad_mod.reshape(share, ways, mod_cols), (1, 0, 2))
    grad_block = ordered(jnp.stack(send_tensor(grad_groups)))
    grad_all = share_dp(grad_block.reshape(micros * slots, mod_cols))
    shard_ada = dot(act_all, grad_all, "kgd,kgm->dm")
    ctx_terms = return_dp(dot(grad_all, mod_w, "kgm,dm->kgd").astype(BF16))
    ctx = jnp.transpose(ctx_terms, (1, 0, 2)).reshape(micros * slots, width)
    for axis, step in (("tensor", 1), ("tensor", 2), ("section", 1)):
        ctx = (ctx.astype(F32) + swap(ctx, axis, step).astype(F32)).astype(BF16)
    silu_back = jax.vjp(jax.nn.silu, cond.astype(F32))[1]
    cond_grad = silu_back(ctx.astype(F32).reshape(cond.shape))[0].astype(BF16)

    sum_pack, sum_branch, sum_lifted, sum_second = bias_sums
    parts = [
        by_xor(sum_pack[:third]),
        by_xor(sum_pack[2 * third :]),
        sum_branch,
        by_xor(sum_lifted),
        sum_second,
        jnp.sum(grad_mod.astype(F32), axis=0),
    ]
    bias_terms = jnp.concatenate([part.reshape(dps, ways, -1) for part in parts], axis=2)
    bias_terms = scatter_dp(bias_terms)[0]
    bias_out = sum(send_tensor(bias_terms))
    pieces, start = [], 0
    for cut in cuts:
        pieces.append(bias_out[start : start + cut])
        start += cut

    def handed_back(whole):
        split = jnp.transpose(whole.reshape(share, ways, tokens_own, width), (1, 0, 2, 3))
        arrivals = [split[0]] + [swap(split[j], "tensor", j) for j in range(1, ways)]
        return ordered(jnp.stack(arrivals)).reshape(latents.shape)

    layer_out = handed_back(output)
    input_grad = handed_back(grad_input)
    return (
        layer_out[None],
        input_grad[None],
        cond_grad,
        shard_qkv[None],
        shard_proj[None],
        shard_up[None],
        shard_down[None],
        shard_ada[None],
        jnp.stack(pieces[:2])[None],
        pieces[2][None],
        pieces[3][None],
        pieces[4][None],
        pieces[5][None],
    )


def solution(mesh):
    both = ("dp", "tensor")
    return jax.shard_map(
        body,
        mesh=mesh,
        in_specs=(
            P(None, "dp", "tensor", None),
            P(None, "dp", None),
            P(None, "dp", "tensor", None),
            P(None, "dp"),
            P("section", "dp", None, "tensor"),
            P("section", "tensor", "dp"),
            P("section", "dp", "tensor"),
            P("section", "tensor", "dp"),
            P("section", "dp", "tensor"),
            P("section", None, both),
            P("section", both),
            P("section", both),
            P("section", both),
            P("section", both),
        ),
        out_specs=(
            P("section", None, "dp", "tensor", None),
            P("section", None, "dp", "tensor", None),
            P(None, "dp", None),
            P("section", "dp", None, "tensor"),
            P("section", "tensor", "dp"),
            P("section", "dp", "tensor"),
            P("section", "tensor", "dp"),
            P("section", "dp", "tensor"),
            P("section", None, both),
            P("section", both),
            P("section", both),
            P("section", both),
            P("section", both),
        ),
        check_vma=False,
    )
```

time: 2140 us -> 833 us (0.39)
  waiting for transfers between devices: 1310 us -> 363 us
  blocking collectives: 298 us -> 0 us
  starting transfers between devices: 16.8 us -> 146 us
  matrix products: 225 us -> 108 us
  other arithmetic: 172 us -> 84.9 us
  local copies, waits for them, and re-layouts: 82.5 us -> 111 us
    reduce_scatter x24 -> x0, waiting for transfers between devices: 554 us -> none  [the longest x10 261 us: input_terms(): lax.psum_scatter(jnp.einsum('gske,dke->sgd', source, matrix, preferred_el...]
    all_gather x23 -> x0, waiting for transfers between devices: 493 us -> none  [the longest x10 235 us: gather_tokens(): return lax.all_gather(normed, 'tensor', axis=1, tiled=True)]
    ppermute x8 -> x86, waiting for transfers between devices: 4.51 us -> 363 us  [the longest x48 166 us: swap(): return lax.ppermute(shard, axis, [(i, i ^ step) for i in range(peers)])]
    unnamed x61 -> x0, waiting for transfers between devices: 254 us -> none
    unnamed x2 -> x0, blocking collectives: 155 us -> none
    ppermute x8 -> x86, starting transfers between devices: 12.4 us -> 146 us  [the longest x36 85.1 us: turned(): lax.ppermute(shard, axis, [(i, (i + by) % peers) for i in range(peers)])]
    all_gather x8 -> x0, blocking collectives: 119 us -> none  [the longest x1 40.9 us: body(): lax.all_gather(bias_qv[0], ('dp', 'tensor'), axis=1, tiled=True)]
    dot_general x110 -> x22, matrix products: 225 us -> 108 us  [dot(): return jnp.einsum(spec, lhs, rhs, preferred_element_type=F32)]
  transfers between devices with their start and end apart: 62 -> 86, of which waited for: 52 -> 33; matrix products, arithmetic and copies ran while one was open for 14% -> 14% of each run, Pallas kernels for 0% -> 0%
where the time goes in v1:
time: 833 us; the launch traced here: 821 us
  waiting for transfers between devices  363 us (44%)
  starting transfers between devices  146 us (18%)
  local copies, waits for them, and re-layouts  111 us (13%)
  matrix products  108 us (13%)
  other arithmetic  84.9 us (10%)
    ppermute x48, waiting for transfers between devices, swap(): return lax.ppermute(shard, axis, [(i, i ^ step) for i in range(peers)])  166 us
    ppermute x1, waiting for transfers between devices, body(): back = lax.ppermute(grads_second[0], 'section', [(1, 0)])  114 us
    dot_general x22, matrix products, dot(): return jnp.einsum(spec, lhs, rhs, preferred_element_type=F32)  108 us
    ppermute x36, starting transfers between devices, turned(): lax.ppermute(shard, axis, [(i, (i + by) % peers) for i in range(peers)])  85.1 us
    ppermute x36, waiting for transfers between devices, turned(): lax.ppermute(shard, axis, [(i, (i + by) % peers) for i in range(peers)])  80 us
    ppermute x48, starting transfers between devices, swap(): return lax.ppermute(shard, axis, [(i, i ^ step) for i in range(peers)])  58.7 us
    another operation x19, local copies, waits for them, and re-layouts  16.8 us
  transfers between devices with their start and end apart: 86, of which 33 were waited for; matrix products, arithmetic and copies ran while one was open for 14% of the time, Pallas kernels for 0%

profile of v1, /device:TPU:0, one launch (start us, length us, event | category | flops | bytes accessed | tf_op | source)
XLA Modules:
  0.0 821.0 jit_solution(11648290364787784851)
XLA Ops:
  41.3 8.5 %collective-permute-done.7 = f32[12,1152]{1,0:T(8,128)S(1)} collective-permute-done((f32[12,1152]{1,0:T(8,128)}, f32[12,1152]{1,0:T(8,128)S(1)}, u32[]{:S(2)}, u32[]{:S(2)}) %collective-permute-start.7) | collective-permute-done | bytes 55328 | tf_op jit(solution)/shard_map/ppermute | solution.py:28
  63.3 25.9 %collective-permute-done.19 = bf16[192,768]{0,1:T(8,128)(2,1)S(1)} collective-permute-done((bf16[192,768]{0,1:T(8,128)(2,1)}, bf16[192,768]{0,1:T(8,128)(2,1)S(1)}, u32[]{:S(2)}, u32[]{:S(2)}) %collective-permute-start.19) | collective-permute-done | bytes 294944 | tf_op jit(solution)/shard_map/ppermute | solution.py:28
  96.5 13.9 %collective-permute-start.33 = (bf16[192,768]{1,0:T(8,128)(2,1)}, bf16[192,768]{1,0:T(8,128)(2,1)}, u32[]{:S(2)}, u32[]{:S(2)}) collective-permute-start(bf16[192,768]{1,0:T(8,128)(2,1)} %bitcast.516), channel_id=1, source_target_pairs={{0,4},{4,8},{8,12},{12,0},{1,5},{5,9},{9,13},{13,1},{2,6},{6,10},{... | collective-permute-start | bytes 884744 | tf_op jit(solution)/shard_map/ppermute | solution.py:28
  135.2 32.0 %collective-permute-done.25 = bf16[768,384]{1,0:T(8,128)(2,1)S(1)} collective-permute-done((bf16[768,384]{1,0:T(8,128)(2,1)S(1)}, bf16[768,384]{1,0:T(8,128)(2,1)S(1)}, u32[]{:S(2)}, u32[]{:S(2)}) %collective-permute-start.25) | collective-permute-done | bytes 589856 | tf_op jit(solution)/shard_map/ppermute | solution.py:23
  171.4 12.3 %collective-permute-done.21 = bf16[768,384]{1,0:T(8,128)(2,1)S(1)} collective-permute-done((bf16[768,384]{1,0:T(8,128)(2,1)S(1)}, bf16[768,384]{1,0:T(8,128)(2,1)S(1)}, u32[]{:S(2)}, u32[]{:S(2)}) %collective-permute-start.21) | collective-permute-done | bytes 589856 | tf_op jit(solution)/shard_map/ppermute | solution.py:23
  211.2 10.5 %collective-permute-done.36 = bf16[768,768]{1,0:T(8,128)(2,1)} collective-permute-done((bf16[768,768]{1,0:T(8,128)(2,1)}, bf16[768,768]{1,0:T(8,128)(2,1)}, u32[]{:S(2)}, u32[]{:S(2)}) %collective-permute-start.36) | collective-permute-done | bytes 1179680 | tf_op jit(solution)/shard_map/ppermute | solution.py:23
  221.7 22.8 %collective-permute-done.38 = bf16[768,768]{1,0:T(8,128)(2,1)} collective-permute-done((bf16[768,768]{1,0:T(8,128)(2,1)}, bf16[768,768]{1,0:T(8,128)(2,1)}, u32[]{:S(2)}, u32[]{:S(2)}) %collective-permute-start.38) | collective-permute-done | bytes 1179680 | tf_op jit(solution)/shard_map/ppermute | solution.py:23
  255.0 52.8 %conditional.3 = (bf16[3,256,768]{2,1,0:T(8,128)(2,1)}, bf16[3,256,768]{2,1,0:T(8,128)(2,1)S(1)}, bf16[3,256,2304]{2,1,0:T(8,128)(2,1)}, f32[3,12,256,1]{2,1,0,3...) conditional(s32[]{:T(128)} %convert_element_type.481, () %tuple.53, ...), branch_computations={%region_0.1_spmd, %region_1.8_spmd} | conditional | flops 11545211904 | bytes 138612000 | solution.py:317
  289.9 9.7 %add_convert_fusion = (bf16[3,256,3072]{2,1,0:T(8,128)(2,1)}, bf16[3,256,3072]{2,1,0:T(8,128)(2,1)}) fusion(f32[3072]{0:T(1024)S(1)} %add.540, bf16[3,256,768]{2,1,0:T(8,128)(2,1)} %add_convert_fusion.3, bf16[768,3072]{1,0:T(8,128)(2,1)S(1)} %bitcast.487), kind=kOutput, calls=%fused_computation.11 | convolution fusion | flops 3649830912 | bytes 15347712 | tf_op jit(solution)/shard_map/cond/branch_1_fun/gsd,df->gsf/dot_general | solution.py:119
  299.6 8.0 add_convert_fusion.4
  312.8 15.6 %conditional.4 = (bf16[3,256,768]{2,1,0:T(8,128)(2,1)}, bf16[3,256,768]{2,1,0:T(8,128)(2,1)}, bf16[3,4608]{1,0:T(4,128)(2,1)}, bf16[768,2304]{1,0:T(8,128)(2,1)S...) conditional(s32[]{:T(128)} %convert_element_type.481, ...), branch_computations={%region_8.30_spmd, %region_30.31_spmd} | conditional | flops 34672779264 | bytes 465949312 | solution.py:330
  345.2 113.6 %collective-permute-done.43 = bf16[3,256,768]{2,1,0:T(8,128)(2,1)} collective-permute-done((bf16[3,256,768]{2,1,0:T(8,128)(2,1)}, bf16[3,256,768]{2,1,0:T(8,128)(2,1)}, u32[]{:S(2)}, u32[]{:S(2)}) %collective-permute-start.43) | collective-permute-done | bytes 1179680 | tf_op jit(solution)/shard_map/ppermute | solution.py:333
  458.8 111.3 %conditional.5 = (bf16[3,256,768]{2,1,0:T(8,128)(2,1)}, bf16[768,2304]{0,1:T(8,128)(2,1)}, bf16[768,768]{1,0:T(8,128)(2,1)}, bf16[768,3072]{0,1:T(8,128)(2,1)}, ...) conditional(s32[]{:T(128)} %convert_element_type.481, ...), branch_computations={%region_31.32_spmd, %region_32.52_spmd} | conditional | flops 23397711872 | bytes 328553824 | solution.py:340
  463.1 12.0 %convert_reduce_fusion.6 = (f32[3072]{0:T(1024)S(1)}, bf16[3,256,3072]{2,1,0:T(8,128)(2,1)S(1)}) fusion(bf16[3,256,3072]{2,1,0:T(8,128)(2,1)} %get-tuple-element.247, bf16[768,3072]{1,0:T(8,128)(2,1)} %get-tuple-element.246, bf16[3,256,768]{2,1,0:T(8,128)(2,1)} %get-tuple-element.244, f32[3,768]{1,0:T(4,128)S(1)} %get-tuple-element.619), kind=kOutput, calls=%fused_computation.188 | convolution fusion | flops 3679908864 | bytes 15356928 | tf_op jit(solution)/shard_map/cond/branch_1_fun/gsn,nf->gsf/dot_general | solution.py:119
  490.8 9.6 %bitcast_convert_fusion.4 = bf16[768,3072]{1,0:T(8,128)(2,1)} fusion(bf16[3,256,3072]{2,1,0:T(8,128)(2,1)} %get-tuple-element.258, bf16[3,256,768]{2,1,0:T(8,128)(2,1)} %get-tuple-element.244, f32[3,768]{1,0:T(4,128)S(1)} %get-tuple-element.619), kind=kOutput, calls=%fused_computation.186 | convolution fusion | flops 3628007424 | bytes 10626048 | tf_op jit(solution)/shard_map/cond/branch_1_fun/gsn,gsf->nf/dot_general | solution.py:119
  529.2 11.5 %multiply_convert_fusion.5 = bf16[3,12,256,256]{2,3,1,0:T(8,128)(2,1)} fusion(f32[3,12,256,256]{2,3,1,0:T(8,128)} %get-tuple-element.626, f32[3,12,256,256]{2,3,1,0:T(8,128)} %copy-done.2, f32[3,12,256]{2,1,0:T(8,128)S(1)} %get-tuple-element.625, f32[3,12,256]{2,1,0:T(8,128)S(1)} %bitcast.507), kind=kLoop, calls=%fused_computation.189 | loop fusion | flops 11796480 | bytes 23666688 | tf_op jit(solution)/shard_map/cond/branch_1_fun/convert_element_type | solution.py:197
  577.2 9.8 %collective-permute-start.80 = (f32[1,4,672]{2,1,0:T(4,128)}, f32[1,4,672]{2,1,0:T(4,128)}, u32[]{:S(2)}, u32[]{:S(2)}) collective-permute-start(f32[1,4,672]{2,1,0:T(4,128)} %get-tuple-element.715), channel_id=1, source_target_pairs={{0,4},{4,8},{8,12},{12,0},{1,5},{5,9},{9,13},{13,1},{2,6},{6,10},{... | collective-permute-start | bytes 32264 | tf_op jit(solution)/shard_map/ppermute | solution.py:28
  673.8 25.0 %collective-permute-done.61 = bf16[768,384]{1,0:T(8,128)(2,1)S(1)} collective-permute-done((bf16[768,384]{1,0:T(8,128)(2,1)S(1)}, bf16[768,384]{1,0:T(8,128)(2,1)S(1)}, u32[]{:S(2)}, u32[]{:S(2)}) %collective-permute-start.61) | collective-permute-done | bytes 589856 | tf_op jit(solution)/shard_map/ppermute | solution.py:23
  700.7 10.8 %collective-permute-done.62 = bf16[768,384]{1,0:T(8,128)(2,1)S(1)} collective-permute-done((bf16[768,384]{1,0:T(8,128)(2,1)S(1)}, bf16[768,384]{1,0:T(8,128)(2,1)S(1)}, u32[]{:S(2)}, u32[]{:S(2)}) %collective-permute-start.62) | collective-permute-done | bytes 589856 | tf_op jit(solution)/shard_map/ppermute | solution.py:23
  735.1 7.8 collective-permute-done.66
  743.0 21.0 %collective-permute-done.76 = bf16[768,768]{1,0:T(8,128)(2,1)S(1)} collective-permute-done((bf16[768,768]{1,0:T(8,128)(2,1)S(1)}, bf16[768,768]{1,0:T(8,128)(2,1)S(1)}, u32[]{:S(2)}, u32[]{:S(2)}) %collective-permute-start.76) | collective-permute-done | bytes 1179680 | tf_op jit(solution)/shard_map/ppermute | solution.py:23
  778.8 10.8 %collective-permute-start.72 = (bf16[192,768]{1,0:T(8,128)(2,1)}, bf16[192,768]{1,0:T(8,128)(2,1)}, u32[]{:S(2)}, u32[]{:S(2)}) collective-permute-start(bf16[192,768]{1,0:T(8,128)(2,1)} %get-tuple-element.652), channel_id=1, source_target_pairs={{0,8},{4,12},{8,0},{12,4},{1,9},{5,13},{9,1},{13,5},{2,10},{6,14},... | collective-permute-start | bytes 884744 | tf_op jit(solution)/shard_map/ppermute | solution.py:28
  795.3 8.9 %collective-permute-done.78 = bf16[192,768]{1,0:T(8,128)(2,1)} collective-permute-done((bf16[192,768]{1,0:T(8,128)(2,1)}, bf16[192,768]{1,0:T(8,128)(2,1)}, u32[]{:S(2)}, u32[]{:S(2)}) %collective-permute-start.78) | collective-permute-done | bytes 294944 | tf_op jit(solution)/shard_map/ppermute | solution.py:28
  806.3 12.5 %collective-permute-done.72 = bf16[192,768]{1,0:T(8,128)(2,1)} collective-permute-done((bf16[192,768]{1,0:T(8,128)(2,1)}, bf16[192,768]{1,0:T(8,128)(2,1)}, u32[]{:S(2)}, u32[]{:S(2)}) %collective-permute-start.72) | collective-permute-done | bytes 294944 | tf_op jit(solution)/shard_map/ppermute | solution.py:28
  (521 shorter events, 415.4 us)
Async XLA Ops:
  23.2 104.7 %collective-permute-start.29 = (bf16[192,768]{1,0:T(8,128)(2,1)}, bf16[192,768]{1,0:T(8,128)(2,1)}, u32[]{:S(2)}, u32[]{:S(2)}) collective-permute-start(bf16[192,768]{1,0:T(8,128)(2,1)} %bitcast.104), channel_id=1, source_target_pairs={{0,12},{4,0},{8,4},{12,8},{1,13},{5,1},{9,5},{13,9},{2,14},{6,2},{... | collective-permute-start | bytes 884744 | tf_op jit(solution)/shard_map/ppermute | solution.py:28
  26.1 99.2 %collective-permute-start.28 = (bf16[192,768]{1,0:T(8,128)(2,1)}, bf16[192,768]{1,0:T(8,128)(2,1)}, u32[]{:S(2)}, u32[]{:S(2)}) collective-permute-start(bf16[192,768]{1,0:T(8,128)(2,1)} %bitcast.104), channel_id=1, source_target_pairs={{0,8},{4,12},{8,0},{12,4},{1,9},{5,13},{9,1},{13,5},{2,10},{6,14},... | collective-permute-start | bytes 884744 | tf_op jit(solution)/shard_map/ppermute | solution.py:28
  125.3 59.1 %collective-permute-start.37 = (bf16[768,768]{1,0:T(8,128)(2,1)}, bf16[768,768]{1,0:T(8,128)(2,1)}, u32[]{:S(2)}, u32[]{:S(2)}) collective-permute-start(bf16[768,768]{1,0:T(8,128)(2,1)} %bitcast.116), channel_id=1, source_target_pairs={{0,2},{1,3},{2,0},{3,1},{4,6},{5,7},{6,4},{7,5},{8,10},{9,11},{10,... | collective-permute-start | bytes 3538952 | tf_op jit(solution)/shard_map/ppermute | solution.py:23
  129.4 39.4 %collective-permute-start.24 = (bf16[768,384]{1,0:T(8,128)(2,1)S(1)}, bf16[768,384]{1,0:T(8,128)(2,1)S(1)}, u32[]{:S(2)}, u32[]{:S(2)}) collective-permute-start(bf16[768,384]{1,0:T(8,128)(2,1)S(1)} %get-tuple-element.680), channel_id=1, source_target_pairs={{0,1},{1,0},{2,3},{3,2},{4,5},{5,4},{6,7},{7,6},{8,9},{9,8},{10,11... | collective-permute-start | bytes 1769480 | tf_op jit(solution)/shard_map/ppermute | solution.py:23
  130.0 67.8 %collective-permute-start.30 = (bf16[768,768]{1,0:T(8,128)(2,1)S(1)}, bf16[768,768]{1,0:T(8,128)(2,1)}, u32[]{:S(2)}, u32[]{:S(2)}) collective-permute-start(bf16[768,768]{1,0:T(8,128)(2,1)S(1)} %bitcast.475), channel_id=1, source_target_pairs={{0,1},{1,0},{2,3},{3,2},{4,5},{5,4},{6,7},{7,6},{8,9},{9,8},{10,11... | collective-permute-start | bytes 3538952 | tf_op jit(solution)/shard_map/ppermute | solution.py:23
  132.2 51.5 %collective-permute-start.21 = (bf16[768,384]{1,0:T(8,128)(2,1)S(1)}, bf16[768,384]{1,0:T(8,128)(2,1)S(1)}, u32[]{:S(2)}, u32[]{:S(2)}) collective-permute-start(bf16[768,384]{1,0:T(8,128)(2,1)S(1)} %get-tuple-element.681), channel_id=1, source_target_pairs={{0,1},{1,0},{2,3},{3,2},{4,5},{5,4},{6,7},{7,6},{8,9},{9,8},{10,11... | collective-permute-start | bytes 1769480 | tf_op jit(solution)/shard_map/ppermute | solution.py:23
  184.4 60.1 %collective-permute-start.38 = (bf16[768,768]{1,0:T(8,128)(2,1)}, bf16[768,768]{1,0:T(8,128)(2,1)}, u32[]{:S(2)}, u32[]{:S(2)}) collective-permute-start(bf16[768,768]{1,0:T(8,128)(2,1)} %collective-permute-done.37), channel_id=1, source_target_pairs={{0,1},{1,0},{2,3},{3,2},{4,5},{5,4},{6,7},{7,6},{8,9},{9,8},{10,11... | collective-permute-start | bytes 3538952 | tf_op jit(solution)/shard_map/ppermute | solution.py:23
  196.3 53.7 %collective-permute-start.31 = (bf16[768,768]{1,0:T(8,128)(2,1)S(1)}, bf16[768,768]{1,0:T(8,128)(2,1)}, u32[]{:S(2)}, u32[]{:S(2)}) collective-permute-start(bf16[768,768]{1,0:T(8,128)(2,1)S(1)} %bitcast.476), channel_id=1, source_target_pairs={{0,2},{1,3},{2,0},{3,1},{4,6},{5,7},{6,4},{7,5},{8,10},{9,11},{10,... | collective-permute-start | bytes 3538952 | tf_op jit(solution)/shard_map/ppermute | solution.py:23
  197.8 52.2 %collective-permute-start.32 = (bf16[768,768]{1,0:T(8,128)(2,1)}, bf16[768,768]{1,0:T(8,128)(2,1)}, u32[]{:S(2)}, u32[]{:S(2)}) collective-permute-start(bf16[768,768]{1,0:T(8,128)(2,1)} %collective-permute-done.30), channel_id=1, source_target_pairs={{0,2},{1,3},{2,0},{3,1},{4,6},{5,7},{6,4},{7,5},{8,10},{9,11},{10,... | collective-permute-start | bytes 3538952 | tf_op jit(solution)/shard_map/ppermute | solution.py:23
  328.4 130.4 %collective-permute-start.43 = (bf16[3,256,768]{2,1,0:T(8,128)(2,1)}, bf16[3,256,768]{2,1,0:T(8,128)(2,1)}, u32[]{:S(2)}, u32[]{:S(2)}) collective-permute-start(bf16[3,256,768]{2,1,0:T(8,128)(2,1)} %get-tuple-element.312), channel_id=1, source_target_pairs={{16,0},{17,1},{18,2},{19,3},{20,4},{21,5},{22,6},{23,7},{24,8},{25... | collective-permute-start | bytes 3538952 | tf_op jit(solution)/shard_map/ppermute | solution.py:333
  575.4 39.5 %collective-permute-start.48 = (bf16[3,1152]{1,0:T(4,128)(2,1)}, bf16[3,1152]{1,0:T(4,128)(2,1)S(1)}, u32[]{:S(2)}, u32[]{:S(2)}) collective-permute-start(bf16[3,1152]{1,0:T(4,128)(2,1)} %get-tuple-element.728), channel_id=1, source_target_pairs={{0,2},{1,3},{2,0},{3,1},{4,6},{5,7},{6,4},{7,5},{8,10},{9,11},{10,... | collective-permute-start | bytes 20744 | tf_op jit(solution)/shard_map/ppermute | solution.py:23
  575.9 40.5 %collective-permute-start.47 = (bf16[3,1152]{1,0:T(4,128)(2,1)}, bf16[3,1152]{1,0:T(4,128)(2,1)}, u32[]{:S(2)}, u32[]{:S(2)}) collective-permute-start(bf16[3,1152]{1,0:T(4,128)(2,1)} %get-tuple-element.729), channel_id=1, source_target_pairs={{0,1},{1,0},{2,3},{3,2},{4,5},{5,4},{6,7},{7,6},{8,9},{9,8},{10,11... | collective-permute-start | bytes 20744 | tf_op jit(solution)/shard_map/ppermute | solution.py:23
  577.2 41.8 %collective-permute-start.80 = (f32[1,4,672]{2,1,0:T(4,128)}, f32[1,4,672]{2,1,0:T(4,128)}, u32[]{:S(2)}, u32[]{:S(2)}) collective-permute-start(f32[1,4,672]{2,1,0:T(4,128)} %get-tuple-element.715), channel_id=1, source_target_pairs={{0,4},{4,8},{8,12},{12,0},{1,5},{5,9},{9,13},{13,1},{2,6},{6,10},{... | collective-permute-start | bytes 32264 | tf_op jit(solution)/shard_map/ppermute | solution.py:28
  616.4 43.1 %collective-permute-start.46 = (bf16[3,64,768]{2,1,0:T(8,128)(2,1)}, bf16[3,64,768]{2,1,0:T(8,128)(2,1)}, u32[]{:S(2)}, u32[]{:S(2)}) collective-permute-start(bf16[3,64,768]{2,1,0:T(8,128)(2,1)} %get-tuple-element.666), channel_id=1, source_target_pairs={{0,3},{1,2},{2,1},{3,0},{4,7},{5,6},{6,5},{7,4},{8,11},{9,10},{10,... | collective-permute-start | bytes 884744 | tf_op jit(solution)/shard_map/ppermute | solution.py:23
  653.9 59.5 %collective-permute-start.75 = (bf16[768,768]{1,0:T(8,128)(2,1)}, bf16[768,768]{1,0:T(8,128)(2,1)S(1)}, u32[]{:S(2)}, u32[]{:S(2)}) collective-permute-start(bf16[768,768]{1,0:T(8,128)(2,1)} %get-tuple-element.632), channel_id=1, source_target_pairs={{0,2},{1,3},{2,0},{3,1},{4,6},{5,7},{6,4},{7,5},{8,10},{9,11},{10,... | collective-permute-start | bytes 3538952 | tf_op jit(solution)/shard_map/ppermute | solution.py:23
  657.4 41.5 %collective-permute-start.61 = (bf16[768,384]{1,0:T(8,128)(2,1)S(1)}, bf16[768,384]{1,0:T(8,128)(2,1)S(1)}, u32[]{:S(2)}, u32[]{:S(2)}) collective-permute-start(bf16[768,384]{1,0:T(8,128)(2,1)S(1)} %add_convert_fusion.23), channel_id=1, source_target_pairs={{0,2},{1,3},{2,0},{3,1},{4,6},{5,7},{6,4},{7,5},{8,10},{9,11},{10,... | collective-permute-start | bytes 1769480 | tf_op jit(solution)/shard_map/ppermute | solution.py:23
  659.4 52.1 %collective-permute-start.62 = (bf16[768,384]{1,0:T(8,128)(2,1)S(1)}, bf16[768,384]{1,0:T(8,128)(2,1)S(1)}, u32[]{:S(2)}, u32[]{:S(2)}) collective-permute-start(bf16[768,384]{1,0:T(8,128)(2,1)S(1)} %copy-done.32), channel_id=1, source_target_pairs={{0,2},{1,3},{2,0},{3,1},{4,6},{5,7},{6,4},{7,5},{8,10},{9,11},{10,... | collective-permute-start | bytes 1769480 | tf_op jit(solution)/shard_map/ppermute | solution.py:23
  661.1 52.0 %collective-permute-start.64 = (bf16[768,384]{1,0:T(8,128)(2,1)S(1)}, bf16[768,384]{1,0:T(8,128)(2,1)S(1)}, u32[]{:S(2)}, u32[]{:S(2)}) collective-permute-start(bf16[768,384]{1,0:T(8,128)(2,1)S(1)} %add_convert_fusion.21), channel_id=1, source_target_pairs={{0,1},{1,0},{2,3},{3,2},{4,5},{5,4},{6,7},{7,6},{8,9},{9,8},{10,11... | collective-permute-start | bytes 1769480 | tf_op jit(solution)/shard_map/ppermute | solution.py:23
  671.0 45.1 %collective-permute-start.69 = (bf16[768,768]{0,1:T(8,128)(2,1)S(1)}, bf16[768,768]{0,1:T(8,128)(2,1)S(1)}, u32[]{:S(2)}, u32[]{:S(2)}) collective-permute-start(bf16[768,768]{0,1:T(8,128)(2,1)S(1)} %copy-done.30), channel_id=1, source_target_pairs={{0,1},{1,0},{2,3},{3,2},{4,5},{5,4},{6,7},{7,6},{8,9},{9,8},{10,11... | collective-permute-start | bytes 3538952 | tf_op jit(solution)/shard_map/ppermute | solution.py:23
  698.9 44.1 %collective-permute-start.74 = (bf16[768,768]{1,0:T(8,128)(2,1)S(1)}, bf16[768,768]{1,0:T(8,128)(2,1)S(1)}, u32[]{:S(2)}, u32[]{:S(2)}) collective-permute-start(bf16[768,768]{1,0:T(8,128)(2,1)S(1)} %copy-done.29), channel_id=1, source_target_pairs={{0,2},{1,3},{2,0},{3,1},{4,6},{5,7},{6,4},{7,5},{8,10},{9,11},{10,... | collective-permute-start | bytes 3538952 | tf_op jit(solution)/shard_map/ppermute | solution.py:23
  711.5 59.0 %collective-permute-start.68 = (bf16[768,768]{0,1:T(8,128)(2,1)S(1)}, bf16[768,768]{0,1:T(8,128)(2,1)S(1)}, u32[]{:S(2)}, u32[]{:S(2)}) collective-permute-start(bf16[768,768]{0,1:T(8,128)(2,1)S(1)} %copy-done.28), channel_id=1, source_target_pairs={{0,1},{1,0},{2,3},{3,2},{4,5},{5,4},{6,7},{7,6},{8,9},{9,8},{10,11... | collective-permute-start | bytes 3538952 | tf_op jit(solution)/shard_map/ppermute | solution.py:23
  715.2 48.8 %collective-permute-start.76 = (bf16[768,768]{1,0:T(8,128)(2,1)S(1)}, bf16[768,768]{1,0:T(8,128)(2,1)S(1)}, u32[]{:S(2)}, u32[]{:S(2)}) collective-permute-start(bf16[768,768]{1,0:T(8,128)(2,1)S(1)} %add_convert_fusion.17), channel_id=1, source_target_pairs={{0,1},{1,0},{2,3},{3,2},{4,5},{5,4},{6,7},{7,6},{8,9},{9,8},{10,11... | collective-permute-start | bytes 3538952 | tf_op jit(solution)/shard_map/ppermute | solution.py:23
  731.0 39.6 %collective-permute-start.70 = (bf16[768,768]{0,1:T(8,128)(2,1)S(1)}, bf16[768,768]{0,1:T(8,128)(2,1)S(1)}, u32[]{:S(2)}, u32[]{:S(2)}) collective-permute-start(bf16[768,768]{0,1:T(8,128)(2,1)S(1)} %add_convert_fusion.19), channel_id=1, source_target_pairs={{0,2},{1,3},{2,0},{3,1},{4,6},{5,7},{6,4},{7,5},{8,10},{9,11},{10,... | collective-permute-start | bytes 3538952 | tf_op jit(solution)/shard_map/ppermute | solution.py:23
  778.8 40.0 %collective-permute-start.72 = (bf16[192,768]{1,0:T(8,128)(2,1)}, bf16[192,768]{1,0:T(8,128)(2,1)}, u32[]{:S(2)}, u32[]{:S(2)}) collective-permute-start(bf16[192,768]{1,0:T(8,128)(2,1)} %get-tuple-element.652), channel_id=1, source_target_pairs={{0,8},{4,12},{8,0},{12,4},{1,9},{5,13},{9,1},{13,5},{2,10},{6,14},... | collective-permute-start | bytes 884744 | tf_op jit(solution)/shard_map/ppermute | solution.py:28
  (119 other events, 1667.2 us)

commit v2 on v1

v2 whole, which is shorter than its diff:
```python
import functools
import math

import jax
import jax.numpy as jnp
from jax import lax
from jax.experimental import pallas as pl
from jax.experimental.pallas import tpu as pltpu
from jax.sharding import PartitionSpec as P

HEAD_DIM = 64
BF16 = jnp.bfloat16
F32 = jnp.float32


def swap(shard, axis, step):
    peers = lax.axis_size(axis)
    return lax.ppermute(shard, axis, [(i, i ^ step) for i in range(peers)])


def turned(shard, axis, by):
    peers = lax.axis_size(axis)
    return lax.ppermute(shard, axis, [(i, (i + by) % peers) for i in range(peers)])


def pick(blocks, index):
    return lax.dynamic_index_in_dim(blocks, index, 0, keepdims=False)


def direct_dp():
    return lax.axis_size("dp") == 4


def gather_dp(shard):
    peers = lax.axis_size("dp")
    if not direct_dp():
        return lax.all_gather(shard, "dp", axis=0, tiled=True)
    place = lax.axis_index("dp")
    whole = jnp.zeros((peers,) + shard.shape, shard.dtype)
    for k in range(peers):
        piece = shard if k == 0 else turned(shard, "dp", k)
        whole = lax.dynamic_update_index_in_dim(whole, piece, (place - k) % peers, 0)
    return whole.reshape((peers * shard.shape[0],) + shard.shape[1:])


def scatter_dp(whole):
    peers = lax.axis_size("dp")
    if not direct_dp():
        return lax.psum_scatter(whole, "dp", scatter_dimension=0, tiled=True).astype(F32)
    place = lax.axis_index("dp")
    blocks = whole.reshape((peers, whole.shape[0] // peers) + whole.shape[1:])
    total = pick(blocks, place).astype(F32)
    for k in range(1, peers):
        total = total + turned(pick(blocks, (place + k) % peers), "dp", k).astype(F32)
    return total


def send_dp(blocks):
    peers = lax.axis_size("dp")
    if not direct_dp():
        return lax.all_to_all(blocks, "dp", 0, 0)
    place = lax.axis_index("dp")
    return jnp.stack(
        [pick(blocks, place)]
        + [turned(pick(blocks, (place + k) % peers), "dp", k) for k in range(1, peers)]
    )


def share_dp(shard):
    peers = lax.axis_size("dp")
    if not direct_dp():
        return lax.all_gather(shard, "dp")
    return jnp.stack([shard] + [turned(shard, "dp", k) for k in range(1, peers)])


def return_dp(blocks):
    peers = lax.axis_size("dp")
    if not direct_dp():
        return lax.all_to_all(blocks, "dp", 0, 0)
    place = lax.axis_index("dp")
    arrived = jnp.stack([blocks[0]] + [turned(blocks[k], "dp", -k) for k in range(1, peers)])
    return jnp.stack([pick(arrived, (a - place) % peers) for a in range(peers)])


def ordered(blocks):
    own = lax.axis_index("tensor")
    return jnp.stack([pick(blocks, b ^ own) for b in range(blocks.shape[0])])


def send_tensor(blocks):
    own = lax.axis_index("tensor")
    return [pick(blocks, own)] + [
        swap(pick(blocks, own ^ j), "tensor", j) for j in range(1, lax.axis_size("tensor"))
    ]


def spread_tensor(own, first, second):
    near = swap(own, "tensor", first)
    side = swap(own, "tensor", second)
    far = swap(near, "tensor", second)
    pieces = {0: own, first: near, second: side, first ^ second: far}
    return [pieces[j] for j in range(4)]


def collect_tensor(pieces, first, second):
    near = swap(pieces[first], "tensor", first)
    far = swap(pieces[first ^ second], "tensor", first)
    keep = pieces[0].astype(F32) + near.astype(F32)
    onward = (pieces[second].astype(F32) + far.astype(F32)).astype(BF16)
    return (keep + swap(onward, "tensor", second).astype(F32)).astype(BF16)


VMEM_BYTES = 50 * 1024 * 1024
GELU_A = 0.7978845608028654
GELU_B = 0.044715


def dot(lhs, rhs, spec):
    return jnp.einsum(spec, lhs, rhs, preferred_element_type=F32)


def mm(lhs, rhs):
    return jnp.dot(lhs, rhs, preferred_element_type=F32)


def mm_nt(lhs, rhs):
    return lax.dot_general(lhs, rhs, (((1,), (1,)), ((), ())), preferred_element_type=F32)


def mm_tn(lhs, rhs):
    return lax.dot_general(lhs, rhs, (((0,), (0,)), ((), ())), preferred_element_type=F32)


def norm_parts(features):
    centred = features - jnp.mean(features, axis=-1, keepdims=True)
    spread = jnp.mean(centred * centred, axis=-1, keepdims=True)
    rate = lax.rsqrt(spread + 1e-06)
    return centred * rate, rate


def norm_back(unit, rate, grad):
    lean = jnp.mean(grad, axis=-1, keepdims=True)
    tilt = jnp.mean(grad * unit, axis=-1, keepdims=True)
    return rate * (grad - lean - unit * tilt)


def token_sum(part):
    return jnp.sum(part, axis=0, keepdims=True)


def head_cols(block, start, head):
    return block[:, start + head * HEAD_DIM : start + (head + 1) * HEAD_DIM]


def attend_kernel(ways, heads, refs):
    x_ref, mod_ref, bqk_ref, bv_ref, bproj_ref = refs[:5]
    qk_w, vp_w = refs[5 : 5 + ways], refs[5 + ways : 5 + 2 * ways]
    na_ref, qk_ref, v_ref, att_ref, branch_ref, middle_ref, nb_ref = refs[5 + 2 * ways :]
    cols = heads * HEAD_DIM
    scale = HEAD_DIM**-0.5
    x = x_ref[0].astype(F32)
    shift_a, scale_a, gate_a = (mod_ref[0, i : i + 1, :] for i in range(3))
    shift_b, scale_b = (mod_ref[0, i : i + 1, :] for i in (3, 4))
    normed = (norm_parts(x)[0] * (1.0 + scale_a) + shift_a).astype(BF16)
    na_ref[0] = normed
    branch = jnp.zeros_like(x) + bproj_ref[...]
    for j in range(ways):
        qk = (mm(normed, qk_w[j][...]) + bqk_ref[j : j + 1, :]).astype(BF16)
        value = (mm(normed, vp_w[j][:, :cols]) + bv_ref[j : j + 1, :]).astype(BF16)
        qk_ref[0, j] = qk
        v_ref[0, j] = value
        outs = [jnp.zeros((x.shape[0], cols), F32)]
        for h in range(heads):
            scores = mm_nt(head_cols(qk, 0, h), head_cols(qk, cols, h)) * scale
            raised = jnp.exp(scores - jnp.max(scores, axis=-1, keepdims=True))
            probs = raised / jnp.sum(raised, axis=-1, keepdims=True)
            outs.append(mm(probs.astype(BF16), head_cols(value, 0, h)))
        padded = jnp.concatenate(outs, axis=1).astype(BF16)
        att_ref[0, j] = padded
        branch = branch + mm_nt(padded, vp_w[j][...])
    branch_ref[0] = branch.astype(BF16)
    middle = x + gate_a * branch
    middle_ref[0] = middle
    nb_ref[0] = (norm_parts(middle)[0] * (1.0 + scale_b) + shift_b).astype(BF16)


def lift_kernel(pieces, refs):
    nb_ref, middle_ref, mod_ref, bup_ref, bdown_ref = refs[:5]
    up_w, down_w = refs[5 : 5 + pieces], refs[5 + pieces : 5 + 2 * pieces]
    lifted_ref, hidden_ref, second_ref, out_ref = refs[5 + 2 * pieces :]
    normed = nb_ref[0]
    middle = middle_ref[0]
    gate_b = mod_ref[0, 5:6, :]
    second = jnp.zeros_like(middle) + bdown_ref[...]
    for c in range(pieces):
        part = up_w[c].shape[1]
        lifted = mm(normed, up_w[c][...]) + bup_ref[c : c + 1, :]
        turn = jnp.tanh(GELU_A * (lifted + GELU_B * lifted * lifted * lifted))
        hidden = (0.5 * lifted * (1.0 + turn)).astype(BF16)
        lifted_ref[0, :, c * part : (c + 1) * part] = lifted.astype(BF16)
        hidden_ref[0, :, c * part : (c + 1) * part] = hidden
        second = second + mm_nt(hidden, down_w[c][...])
    second_ref[0] = second.astype(BF16)
    out_ref[0] = (middle + gate_b * second).astype(BF16)


def lift_back_kernel(pieces, refs):
    g_ref, second_ref, lifted_ref, middle_ref, mod_ref = refs[:5]
    up_w, down_w = refs[5 : 5 + pieces], refs[5 + pieces : 5 + 2 * pieces]
    gs_ref, gl_ref, gm_ref, sums_ref, lift_sums_ref = refs[5 + 2 * pieces :]
    grad = g_ref[0].astype(F32)
    scale_b, gate_b = mod_ref[0, 4:5, :], mod_ref[0, 5:6, :]
    grad_second = (gate_b * grad).astype(BF16)
    gs_ref[0] = grad_second
    normed = jnp.zeros_like(grad)
    for c in range(pieces):
        part = up_w[c].shape[1]
        grad_hidden = mm(grad_second, down_w[c][...])
        v = lifted_ref[0, :, c * part : (c + 1) * part].astype(F32)
        square = v * v
        turn = jnp.tanh(GELU_A * v * (1.0 + GELU_B * square))
        slope = 0.5 * (1.0 + turn) + (0.5 * GELU_A) * v * (1.0 - turn * turn) * (
            1.0 + (3.0 * GELU_B) * square
        )
        grad_lifted = (grad_hidden * slope).astype(BF16)
        gl_ref[0, :, c * part : (c + 1) * part] = grad_lifted
        lift_sums_ref[0, c : c + 1, :] = token_sum(grad_lifted.astype(F32))
        normed = normed + mm_nt(grad_lifted, up_w[c][...])
    unit, rate = norm_parts(middle_ref[0])
    gm_ref[0] = grad + norm_back(unit, rate, normed * (1.0 + scale_b))
    sums_ref[0, 0:1, :] = token_sum(normed)
    sums_ref[0, 1:2, :] = token_sum(normed * unit)
    sums_ref[0, 2:3, :] = token_sum(grad * second_ref[0].astype(F32))
    sums_ref[0, 3:4, :] = token_sum(grad_second.astype(F32))


def attend_back_kernel(ways, heads, refs):
    gm_ref, branch_ref, qk_ref, v_ref, x_ref, mod_ref = refs[:6]
    qk_w, vp_w = refs[6 : 6 + ways], refs[6 + ways : 6 + 2 * ways]
    gb_ref, gqk_ref, gv_ref, gi_ref, sums_ref, pack_sums_ref = refs[6 + 2 * ways :]
    cols = heads * HEAD_DIM
    scale = HEAD_DIM**-0.5
    middle = gm_ref[0]
    scale_a, gate_a = mod_ref[0, 1:2, :], mod_ref[0, 2:3, :]
    grad_branch = (gate_a * middle).astype(BF16)
    gb_ref[0] = grad_branch
    normed = jnp.zeros_like(middle)
    for j in range(ways):
        grad_att = mm(grad_branch, vp_w[j][...]).astype(BF16)
        qk = qk_ref[0, j]
        value = v_ref[0, j]
        grads_q, grads_k, grads_v = [], [], []
        for h in range(heads):
            query, key = head_cols(qk, 0, h), head_cols(qk, cols, h)
            grad_head = head_cols(grad_att, cols, h)
            scores = mm_nt(key, query) * scale
            raised = jnp.exp(scores - jnp.max(scores, axis=0, keepdims=True))
            probs = raised / jnp.sum(raised, axis=0, keepdims=True)
            grads_v.append(mm(probs.astype(BF16), grad_head))
            grad_probs = mm_nt(head_cols(value, 0, h), grad_head)
            total = jnp.sum(grad_probs * probs, axis=0, keepdims=True)
            grad_scores = (probs * (grad_probs - total)).astype(BF16)
            grads_k.append(mm(grad_scores, query) * scale)
            grads_q.append(mm_tn(grad_scores, key) * scale)
        grad_qk = jnp.concatenate(grads_q + grads_k, axis=1).astype(BF16)
        grads_v.append(jnp.zeros((middle.shape[0], cols), F32))
        grad_v = jnp.concatenate(grads_v, axis=1).astype(BF16)
        gqk_ref[0, j] = grad_qk
        gv_ref[0, j] = grad_v
        pack_sums_ref[0, j : j + 1, :] = token_sum(grad_qk.astype(F32))
        pack_sums_ref[0, ways + j : ways + j + 1, :] = token_sum(grad_v.astype(F32))
        normed = normed + mm_nt(grad_qk, qk_w[j][...]) + mm_nt(grad_v, vp_w[j][...])
    unit, rate = norm_parts(x_ref[0].astype(F32))
    gi_ref[0] = (middle + norm_back(unit, rate, normed * (1.0 + scale_a))).astype(BF16)
    sums_ref[0, 0:1, :] = token_sum(normed)
    sums_ref[0, 1:2, :] = token_sum(normed * unit)
    sums_ref[0, 2:3, :] = token_sum(middle * branch_ref[0].astype(F32))
    sums_ref[0, 3:4, :] = token_sum(grad_branch.astype(F32))


def flat_tokens(ref):
    return ref[...].reshape(ref.shape[0] * ref.shape[1], ref.shape[2])


def lift_weights_kernel(pieces, refs):
    nb_ref, gl_ref, gs_ref, hidden_ref = refs[:4]
    up_out, down_out = refs[4 : 4 + pieces], refs[4 + pieces : 4 + 2 * pieces]
    for left_ref, right_ref, outs in ((gs_ref, hidden_ref, down_out), (nb_ref, gl_ref, up_out)):
        left = flat_tokens(left_ref).T
        for c in range(pieces):
            part = outs[c].shape[1]
            right = right_ref[:, :, c * part : (c + 1) * part]
            right = right.reshape(right.shape[0] * right.shape[1], part)
            outs[c][...] = mm(left, right).astype(BF16)


def attend_weights_kernel(ways, refs):
    na_ref, gqk_ref, gv_ref, gb_ref, att_ref = refs[:5]
    qk_out, vp_out = refs[5 : 5 + ways], refs[5 + ways : 5 + 2 * ways]
    latents, tokens = na_ref.shape[:2]
    left_n = flat_tokens(na_ref).T
    left_b = flat_tokens(gb_ref).T
    for j in range(ways):
        over = lambda ref: jnp.concatenate([ref[g, j] for g in range(latents)], axis=0)
        qk_out[j][...] = mm(left_n, over(gqk_ref)).astype(BF16)
        vp_out[j][...] = (mm(left_n, over(gv_ref)) + mm(left_b, over(att_ref))).astype(BF16)


def per_latent(shape):
    rank = len(shape)
    return pl.BlockSpec((1,) + tuple(shape[1:]), lambda g: (g,) + (0,) * (rank - 1))


def constant(shape):
    rank = len(shape)
    return pl.BlockSpec(tuple(shape), lambda g: (0,) * rank, pipeline_mode=pl.Buffered(1))


def over_latents(kernel, name, varying, fixed, outs, flops):
    return pl.pallas_call(
        lambda *refs: kernel(refs),
        grid=(varying[0].shape[0],),
        in_specs=[per_latent(a.shape) for a in varying] + [constant(a.shape) for a in fixed],
        out_specs=[per_latent(shape) for shape, _ in outs],
        out_shape=[jax.ShapeDtypeStruct(shape, dtype) for shape, dtype in outs],
        compiler_params=pltpu.CompilerParams(vmem_limit_bytes=VMEM_BYTES),
        cost_estimate=pl.CostEstimate(
            flops=flops,
            bytes_accessed=sum(a.size * a.dtype.itemsize for a in varying + fixed)
            + sum(4 * math.prod(shape) for shape, _ in outs),
            transcendentals=0,
        ),
        name=name,
    )(*varying, *fixed)


def at_once(kernel, name, inputs, out_shapes, flops):
    return pl.pallas_call(
        lambda *refs: kernel(refs),
        in_specs=[pl.BlockSpec(memory_space=pltpu.VMEM)] * len(inputs),
        out_specs=[pl.BlockSpec(memory_space=pltpu.VMEM)] * len(out_shapes),
        out_shape=[jax.ShapeDtypeStruct(shape, BF16) for shape in out_shapes],
        compiler_params=pltpu.CompilerParams(vmem_limit_bytes=VMEM_BYTES),
        cost_estimate=pl.CostEstimate(
            flops=flops,
            bytes_accessed=sum(a.size * a.dtype.itemsize for a in inputs)
            + sum(2 * math.prod(shape) for shape in out_shapes),
            transcendentals=0,
        ),
        name=name,
    )(*inputs)


def attend_forward(tokens_in, mod6, weights, biases):
    qk_w, vp_w = weights[:2]
    b_qk, b_v, b_proj = biases[:3]
    ways, cols = len(qk_w), b_v.shape[1]
    latents, tokens, width = tokens_in.shape
    whole = (latents, tokens, width)
    return over_latents(
        functools.partial(attend_kernel, ways, cols // HEAD_DIM),
        "attend_forward",
        [tokens_in, mod6],
        [b_qk, b_v, b_proj, *qk_w, *vp_w],
        [
            (whole, BF16),
            ((latents, ways, tokens, 2 * cols), BF16),
            ((latents, ways, tokens, cols), BF16),
            ((latents, ways, tokens, 2 * cols), BF16),
            (whole, BF16),
            (whole, F32),
            (whole, BF16),
        ],
        10 * latents * tokens * width * width,
    )


def lift_forward(normed_b, middle, mod6, weights, biases):
    up_w, down_w = weights[2:]
    b_up, b_down = biases[3:]
    whole = middle.shape
    wide = whole[:2] + (b_up.size,)
    return over_latents(
        functools.partial(lift_kernel, len(up_w)),
        "lift_forward",
        [normed_b, middle, mod6],
        [b_up, b_down, *up_w, *down_w],
        [(wide, BF16), (wide, BF16), (whole, BF16), (whole, BF16)],
        4 * math.prod(whole) * b_up.size,
    )


def layer_forward(tokens_in, mod6, weights, biases):
    normed_a, qk, value, attended, branch, middle, normed_b = attend_forward(
        tokens_in, mod6, weights, biases
    )
    lifted, hidden, second, output = lift_forward(normed_b, middle, mod6, weights, biases)
    saved_a = (normed_a, qk, value, attended, branch)
    saved_b = (middle, normed_b, lifted, hidden, second)
    return output, saved_a, saved_b


def lift_backward(grad_out, mod6, weights, saved_b):
    up_w, down_w = weights[2:]
    middle, normed_b, lifted, hidden, second = saved_b
    latents, tokens, width = middle.shape
    grad_second, grad_lifted, grad_middle, sums, lift_sums = over_latents(
        functools.partial(lift_back_kernel, len(up_w)),
        "lift_backward",
        [grad_out, second, lifted, middle, mod6],
        [*up_w, *down_w],
        [
            (middle.shape, BF16),
            (lifted.shape, BF16),
            (middle.shape, F32),
            ((latents, 4, width), F32),
            ((latents, len(up_w), up_w[0].shape[1]), F32),
        ],
        4 * middle.size * lifted.shape[2],
    )
    return grad_middle, (normed_b, grad_lifted, grad_second, hidden), (sums, lift_sums)


def attend_backward(grad_middle, tokens_in, mod6, weights, saved_a):
    qk_w, vp_w = weights[:2]
    normed_a, qk, value, attended, branch = saved_a
    latents, tokens, width = grad_middle.shape
    cols = value.shape[3]
    grad_branch, grad_qk, grad_v, grad_input, sums, pack_sums = over_latents(
        functools.partial(attend_back_kernel, len(qk_w), cols // HEAD_DIM),
        "attend_backward",
        [grad_middle, branch, qk, value, tokens_in, mod6],
        [*qk_w, *vp_w],
        [
            (grad_middle.shape, BF16),
            (qk.shape, BF16),
            (qk.shape, BF16),
            (grad_middle.shape, BF16),
            ((latents, 4, width), F32),
            ((latents, 2 * len(qk_w), 2 * cols), F32),
        ],
        12 * grad_middle.size * width,
    )
    return grad_input, (normed_a, grad_qk, grad_v, grad_branch, attended), (sums, pack_sums)


def lift_weights(kept, pieces):
    normed_b, grad_lifted = kept[:2]
    width, wide = normed_b.shape[2], grad_lifted.shape[2]
    return at_once(
        functools.partial(lift_weights_kernel, pieces),
        "lift_weights",
        kept,
        [(width, wide // pieces)] * (2 * pieces),
        4 * normed_b.size * wide,
    )


def attend_weights(kept):
    normed_a, grad_qk = kept[:2]
    ways, part = grad_qk.shape[1], grad_qk.shape[3]
    return at_once(
        functools.partial(attend_weights_kernel, ways),
        "attend_weights",
        kept,
        [(normed_a.shape[2], part)] * (2 * ways),
        6 * normed_a.size * ways * part,
    )


def zeros_like_shapes(shapes):
    return jax.tree.map(lambda s: jnp.zeros(s.shape, s.dtype), shapes)


def after(value, *others):
    return lax.optimization_barrier((value,) + others)[0]


def body(
    latents,
    cond,
    cotangent,
    live,
    w_qkv,
    w_proj,
    w_up,
    w_down,
    w_ada,
    bias_qv,
    bias_proj,
    bias_up,
    bias_down,
    bias_ada,
):
    micros, slots, tokens_own, width = latents.shape
    ways = lax.axis_size("tensor")
    dps = lax.axis_size("dp")
    share = micros * slots // ways
    own_t = lax.axis_index("tensor")
    is_first = lax.axis_index("section") == 0
    qkv_cols = w_qkv.shape[3]
    hidden_cols = w_up.shape[2]
    mod_cols = w_ada.shape[2]
    mod_w = w_ada[0]

    source = jnp.where(is_first, latents, cotangent).reshape(ways, share, tokens_own, width)
    tokens_in = jnp.concatenate(send_tensor(source), axis=1)

    bias_shard = jnp.concatenate(
        [bias_qv[0, 0], bias_qv[0, 1], bias_proj[0], bias_up[0], bias_down[0], bias_ada[0]]
    )
    cuts = [bias_qv.shape[2]] * 2 + [b.shape[1] for b in (bias_proj, bias_up, bias_down, bias_ada)]
    bias_dp = gather_dp(bias_shard[None])
    bias_rel = jnp.stack(
        [bias_dp] + [swap(bias_dp, "tensor", j) for j in range(1, ways)]
    )
    bias_all = jnp.transpose(ordered(bias_rel), (1, 0, 2)).astype(F32)
    full, start = [], 0
    for cut in cuts:
        full.append(bias_all[:, :, start : start + cut].reshape(-1))
        start += cut
    full_q, full_v, full_proj, full_up, full_down, full_ada = full
    by_xor = lambda vector: ordered(vector.reshape(ways, -1)).reshape(-1)
    bias_qk = by_xor(full_q).reshape(ways, -1)
    bias_qk = jnp.concatenate([bias_qk, jnp.zeros_like(bias_qk)], axis=1)
    biases = (
        bias_qk,
        by_xor(full_v).reshape(ways, -1),
        full_proj[None],
        by_xor(full_up).reshape(2 * ways, -1),
        full_down[None],
    )

    context = cond.reshape(micros * slots, width)
    act = jax.nn.silu(context.astype(F32)).astype(BF16)
    act_blocks = jnp.transpose(act.reshape(micros * slots, dps, width // dps), (1, 0, 2))
    act_all = send_dp(act_blocks)
    mod_terms = return_dp(dot(act_all, mod_w, "kgd,dm->kgm"))
    bias_mod = lax.dynamic_slice_in_dim(full_ada, own_t * mod_cols, mod_cols)
    mod_block = jnp.sum(mod_terms, axis=0) + bias_mod
    mod_rel = jnp.stack(send_tensor(mod_block.reshape(ways, share, mod_cols)))
    modulate = jnp.transpose(ordered(mod_rel), (1, 0, 2)).reshape(share, ways * mod_cols)

    mod6 = modulate.reshape(share, 6, width)

    half = hidden_cols // 2
    pack_shard = jnp.concatenate(
        [w_qkv[0, :, 0], w_qkv[0, :, 1], w_qkv[0, :, 2], w_proj[0].T], axis=1
    )
    pack_own = gather_dp(pack_shard)
    up_own = gather_dp(after(w_up[0], pack_own, tokens_in))
    qk_w = spread_tensor(pack_own[:, : 2 * qkv_cols], 1, 2)
    vp_w = spread_tensor(pack_own[:, 2 * qkv_cols :], 2, 1)
    down_own = gather_dp(after(w_down[0].T, up_own, mod6, qk_w[1], vp_w[2], bias_qk))
    up_a = spread_tensor(after(up_own[:, :half], qk_w[3], qk_w[2]), 1, 2)
    up_b = spread_tensor(after(up_own[:, half:], vp_w[3], vp_w[1]), 2, 1)
    down_a = spread_tensor(after(down_own[:, :half], up_a[1]), 1, 2)
    down_b = spread_tensor(after(down_own[:, half:], up_b[2]), 2, 1)
    interleave = lambda first, second: [piece for pair in zip(first, second) for piece in pair]
    up_w, down_w = interleave(up_a, up_b), interleave(down_a, down_b)
    weights = (qk_w, vp_w, up_w, down_w)

    slot_mask = (lax.broadcasted_iota(jnp.int32, (micros, slots), 1) < live).astype(F32)
    own_mask = pick(slot_mask.reshape(ways, share), own_t)

    def on_first(run, args, otherwise=None):
        shapes = jax.eval_shape(run, args)
        rest = (lambda args: zeros_like_shapes(shapes)) if otherwise is None else otherwise
        return lax.cond(is_first, run, rest, args)

    ahead = on_first(
        lambda args: attend_forward(*args), (tokens_in, mod6, (qk_w, vp_w), biases)
    )
    normed_a, qk, value, attended, branch, middle, normed_b = ahead
    lifted, hidden, second, output_first = on_first(
        lambda args: lift_forward(*args), (normed_b, middle, mod6, weights, biases)
    )
    saved_a = (normed_a, qk, value, attended, branch)
    saved_b = (middle, normed_b, lifted, hidden, second)
    arrived = lax.ppermute(output_first, "section", [(0, 1)])

    def second_layer(args):
        arrived, tokens, mask, mod6, weights, biases = args
        output, saved_a, saved_b = layer_forward(arrived, mod6, weights, biases)
        grad_out = tokens * mask[:, None, None].astype(BF16)
        grad_middle, kept_b, sums_b = lift_backward(grad_out, mod6, weights, saved_b)
        grad_input, kept_a, sums_a = attend_backward(grad_middle, arrived, mod6, weights, saved_a)
        return output, grad_input, kept_a, kept_b, sums_a, sums_b

    args = (arrived, tokens_in, own_mask, mod6, weights, biases)
    shapes = jax.eval_shape(second_layer, args)
    output_second, grad_second_in, kept_a1, kept_b1, sums_a1, sums_b1 = lax.cond(
        is_first, lambda args: zeros_like_shapes(shapes), second_layer, args
    )
    back = lax.ppermute(grad_second_in, "section", [(1, 0)])

    pieces = len(up_w)

    def first_lift(args):
        back, mod6, weights, saved_b = args[:4]
        grad_middle, kept_b, sums_b = lift_backward(back, mod6, weights, saved_b)
        return grad_middle, sums_b, lift_weights(kept_b, pieces)

    def second_lift(args):
        kept_b1, sums_b1, saved_b = args[4], args[5], args[3]
        return jnp.zeros_like(saved_b[0]), sums_b1, lift_weights(kept_b1, pieces)

    args = (back, mod6, weights, saved_b, kept_b1, sums_b1)
    grad_middle, sums_b, lift_slabs = on_first(first_lift, args, second_lift)

    def first_attend(args):
        grad_middle, tokens, mod6, weights, saved_a = args[:5]
        grad_input, kept_a, sums_a = attend_backward(grad_middle, tokens, mod6, weights, saved_a)
        return grad_input, sums_a, attend_weights(kept_a)

    def second_attend(args):
        kept_a1, sums_a1, grad_second_in = args[5:]
        return grad_second_in, sums_a1, attend_weights(kept_a1)

    args = (grad_middle, tokens_in, mod6, weights, saved_a, kept_a1, sums_a1, grad_second_in)
    grad_input, sums_a, attend_slabs = on_first(first_attend, args, second_attend)
    output = jnp.where(is_first, output_first, output_second)

    g_up, g_down = lift_slabs[:pieces], lift_slabs[pieces:]
    g_qk, g_vp = attend_slabs[:ways], attend_slabs[ways:]
    pair = lambda first, second: jnp.concatenate([first, second], axis=1)
    out_down = scatter_dp(
        pair(collect_tensor(g_down[::2], 1, 2), collect_tensor(g_down[1::2], 2, 1))
    )
    out_up = scatter_dp(pair(collect_tensor(g_up[::2], 1, 2), collect_tensor(g_up[1::2], 2, 1)))
    out_pack = scatter_dp(pair(collect_tensor(g_qk, 1, 2), collect_tensor(g_vp, 2, 1)))
    shard_qkv = out_pack[:, : 3 * qkv_cols].reshape(-1, 3, qkv_cols)
    shard_proj = out_pack[:, 3 * qkv_cols :].T
    shard_up = out_up
    shard_down = out_down.T

    grad_mod = jnp.concatenate([sums_a[0][:, :3], sums_b[0][:, :3]], axis=1)
    grad_mod = grad_mod.reshape(share, 6 * width).astype(BF16)

    grad_groups = jnp.transpose(grad_mod.reshape(share, ways, mod_cols), (1, 0, 2))
    grad_block = ordered(jnp.stack(send_tensor(grad_groups)))
    grad_all = share_dp(grad_block.reshape(micros * slots, mod_cols))
    shard_ada = dot(act_all, grad_all, "kgd,kgm->dm")
    ctx_terms = return_dp(dot(grad_all, mod_w, "kgm,dm->kgd").astype(BF16))
    ctx = jnp.transpose(ctx_terms, (1, 0, 2)).reshape(micros * slots, width)
    for axis, step in (("tensor", 1), ("tensor", 2), ("section", 1)):
        if axis == "section":
            ctx = after(ctx, out_pack, out_up, out_down)
        ctx = (ctx.astype(F32) + swap(ctx, axis, step).astype(F32)).astype(BF16)
    silu_back = jax.vjp(jax.nn.silu, cond.astype(F32))[1]
    cond_grad = silu_back(ctx.astype(F32).reshape(cond.shape))[0].astype(BF16)

    pack_sums = jnp.sum(sums_a[1], axis=0)
    parts = [
        by_xor(pack_sums[:ways, :qkv_cols].reshape(-1)),
        by_xor(pack_sums[ways:, :qkv_cols].reshape(-1)),
        jnp.sum(sums_a[0][:, 3], axis=0),
        by_xor(jnp.sum(sums_b[1], axis=0).reshape(-1)),
        jnp.sum(sums_b[0][:, 3], axis=0),
        jnp.sum(grad_mod.astype(F32), axis=0),
    ]
    bias_terms = jnp.concatenate([part.reshape(dps, ways, -1) for part in parts], axis=2)
    bias_terms = scatter_dp(bias_terms)[0]
    bias_out = sum(send_tensor(bias_terms))
    bias_pieces, start = [], 0
    for cut in cuts:
        bias_pieces.append(bias_out[start : start + cut])
        start += cut

    def handed_back(whole):
        split = jnp.transpose(whole.reshape(share, ways, tokens_own, width), (1, 0, 2, 3))
        arrivals = [split[0]] + [swap(split[j], "tensor", j) for j in range(1, ways)]
        return ordered(jnp.stack(arrivals)).reshape(latents.shape)

    layer_out = handed_back(output)
    input_grad = handed_back(grad_input)
    return (
        layer_out[None],
        input_grad[None],
        cond_grad,
        shard_qkv[None],
        shard_proj[None],
        shard_up[None],
        shard_down[None],
        shard_ada[None],
        jnp.stack(bias_pieces[:2])[None],
        bias_pieces[2][None],
        bias_pieces[3][None],
        bias_pieces[4][None],
        bias_pieces[5][None],
    )


def solution(mesh):
    both = ("dp", "tensor")
    return jax.shard_map(
        body,
        mesh=mesh,
        in_specs=(
            P(None, "dp", "tensor", None),
            P(None, "dp", None),
            P(None, "dp", "tensor", None),
            P(None, "dp"),
            P("section", "dp", None, "tensor"),
            P("section", "tensor", "dp"),
            P("section", "dp", "tensor"),
            P("section", "tensor", "dp"),
            P("section", "dp", "tensor"),
            P("section", None, both),
            P("section", both),
            P("section", both),
            P("section", both),
            P("section", both),
        ),
        out_specs=(
            P("section", None, "dp", "tensor", None),
            P("section", None, "dp", "tensor", None),
            P(None, "dp", None),
            P("section", "dp", None, "tensor"),
            P("section", "tensor", "dp"),
            P("section", "dp", "tensor"),
            P("section", "tensor", "dp"),
            P("section", "dp", "tensor"),
            P("section", None, both),
            P("section", both),
            P("section", both),
            P("section", both),
            P("section", both),
        ),
        check_vma=False,
    )
```

time: 833 us -> 618 us (0.74)
  Pallas kernels: 0 us -> 115 us
  matrix products: 108 us -> 2.49 us
  waiting for transfers between devices: 363 us -> 286 us
  local copies, waits for them, and re-layouts: 111 us -> 43 us
  other arithmetic: 84.9 us -> 18.1 us
  starting transfers between devices: 146 us -> 135 us
    pallas_call x0 -> x6, Pallas kernels: none -> 115 us  [the longest x4 91.2 us: over_latents(): pl.pallas_call(lambda *refs: kernel(refs), grid=(varying[0].shape[0],), i...]
    dot_general x22 -> x3, matrix products: 108 us -> 2.49 us  [dot(): return jnp.einsum(spec, lhs, rhs, preferred_element_type=F32)]
    ppermute x1, waiting for transfers between devices: 114 us -> 61.6 us  [body(): back = lax.ppermute(grad_second_in, 'section', [(1, 0)])]
    ppermute x48 -> x60, waiting for transfers between devices: 166 us -> 139 us  [swap(): return lax.ppermute(shard, axis, [(i, i ^ step) for i in range(peers)])]
    reduce_sum x11 -> x4, other arithmetic: 20.9 us -> 1.59 us  [the longest x1 0.79 us: body(): jnp.sum(sums_a[0][:, 3], axis=0)]
    concatenate x9 -> x3, other arithmetic: 18.1 us -> 0.29 us  [body(): pair = lambda first, second: jnp.concatenate([first, second], axis=1)]
    ppermute x36, starting transfers between devices: 85.1 us -> 68.1 us  [turned(): lax.ppermute(shard, axis, [(i, (i + by) % peers) for i in range(peers)])]
    slice x15 -> x8, local copies, waits for them, and re-layouts: 19.8 us -> 3.56 us  [the longest x2 1.55 us: body(): grad_mod = jnp.concatenate([sums_a[0][:, :3], sums_b[0][:, :3]], axis=1)]
  transfers between devices with their start and end apart: 86 -> 98, of which waited for: 33 -> 47; matrix products, arithmetic and copies ran while one was open for 14% -> 6% of each run, Pallas kernels for 0% -> 4%
where the time goes in v2:
time: 618 us; the launch traced here: 610 us
  waiting for transfers between devices  286 us (46%)
  starting transfers between devices  135 us (22%)
  Pallas kernels  115 us (19%)
  local copies, waits for them, and re-layouts  43 us (7%)
  other arithmetic  18.1 us (3%)
  loops' own time  8.08 us (1%)
    ppermute x60, waiting for transfers between devices, swap(): return lax.ppermute(shard, axis, [(i, i ^ step) for i in range(peers)])  139 us
    pallas_call x4, Pallas kernels, over_latents(): pl.pallas_call(lambda *refs: kernel(refs), grid=(varying[0].shape[0],), i...  91.2 us
    ppermute x36, waiting for transfers between devices, turned(): lax.ppermute(shard, axis, [(i, (i + by) % peers) for i in range(peers)])  83.3 us
    ppermute x36, starting transfers between devices, turned(): lax.ppermute(shard, axis, [(i, (i + by) % peers) for i in range(peers)])  68.1 us
    ppermute x60, starting transfers between devices, swap(): return lax.ppermute(shard, axis, [(i, i ^ step) for i in range(peers)])  64.7 us
    ppermute x1, waiting for transfers between devices, body(): back = lax.ppermute(grad_second_in, 'section', [(1, 0)])  61.6 us
    pallas_call x2, Pallas kernels, at_once(): pl.pallas_call(lambda *refs: kernel(refs), in_specs=[pl.BlockSpec(memory_...  23.6 us
    another operation x20, local copies, waits for them, and re-layouts  14 us
  transfers between devices with their start and end apart: 98, of which 47 were waited for; matrix products, arithmetic and copies ran while one was open for 6% of the time, Pallas kernels for 4%

profile of v2, /device:TPU:0, one launch (start us, length us, event | category | flops | bytes accessed | tf_op | source)
XLA Modules:
  0.0 610.4 jit_solution(4656021379213341776)
XLA Ops:
  37.0 8.5 %collective-permute-done.8 = f32[12,1152]{1,0:T(8,128)S(1)} collective-permute-done((f32[12,1152]{1,0:T(8,128)}, f32[12,1152]{1,0:T(8,128)S(1)}, u32[]{:S(2)}, u32[]{:S(2)}) %collective-permute-start.8) | collective-permute-done | bytes 55328 | tf_op jit(solution)/shard_map/ppermute | solution.py:23
  45.5 10.2 %collective-permute-done.7 = f32[12,1152]{1,0:T(8,128)} collective-permute-done((f32[12,1152]{1,0:T(8,128)S(1)}, f32[12,1152]{1,0:T(8,128)}, u32[]{:S(2)}, u32[]{:S(2)}) %collective-permute-start.7) | collective-permute-done | bytes 55328 | tf_op jit(solution)/shard_map/ppermute | solution.py:23
  85.4 16.4 %collective-permute-done.27 = bf16[192,768]{1,0:T(8,128)(2,1)S(1)} collective-permute-done((bf16[192,768]{1,0:T(8,128)(2,1)S(1)}, bf16[192,768]{1,0:T(8,128)(2,1)S(1)}, u32[]{:S(2)}, u32[]{:S(2)}) %collective-permute-start.27) | collective-permute-done | bytes 294944 | tf_op jit(solution)/shard_map/ppermute | solution.py:23
  108.0 8.1 %collective-permute-done.21 = bf16[768,384]{1,0:T(8,128)(2,1)S(1)} collective-permute-done((bf16[768,384]{1,0:T(8,128)(2,1)S(1)}, bf16[768,384]{1,0:T(8,128)(2,1)S(1)}, u32[]{:S(2)}, u32[]{:S(2)}) %collective-permute-start.21) | collective-permute-done | bytes 589856 | tf_op jit(solution)/shard_map/ppermute | solution.py:18
  142.1 8.4 %collective-permute-done.38 = bf16[192,768]{1,0:T(8,128)(2,1)S(1)} collective-permute-done((bf16[192,768]{1,0:T(8,128)(2,1)S(1)}, bf16[192,768]{1,0:T(8,128)(2,1)S(1)}, u32[]{:S(2)}, u32[]{:S(2)}) %collective-permute-start.38) | collective-permute-done | bytes 294944 | tf_op jit(solution)/shard_map/ppermute | solution.py:23
  157.6 10.9 %collective-permute-done.31 = bf16[768,384]{1,0:T(8,128)(2,1)S(1)} collective-permute-done((bf16[768,384]{1,0:T(8,128)(2,1)S(1)}, bf16[768,384]{1,0:T(8,128)(2,1)S(1)}, u32[]{:S(2)}, u32[]{:S(2)}) %collective-permute-start.31) | collective-permute-done | bytes 589856 | tf_op jit(solution)/shard_map/ppermute | solution.py:18
  170.7 10.4 %collective-permute-done.35 = bf16[768,384]{1,0:T(8,128)(2,1)S(1)} collective-permute-done((bf16[768,384]{1,0:T(8,128)(2,1)S(1)}, bf16[768,384]{1,0:T(8,128)(2,1)S(1)}, u32[]{:S(2)}, u32[]{:S(2)}) %collective-permute-start.35) | collective-permute-done | bytes 589856 | tf_op jit(solution)/shard_map/ppermute | solution.py:18
  183.3 10.5 %collective-permute-done.39 = bf16[768,384]{1,0:T(8,128)(2,1)} collective-permute-done((bf16[768,384]{1,0:T(8,128)(2,1)}, bf16[768,384]{1,0:T(8,128)(2,1)}, u32[]{:S(2)}, u32[]{:S(2)}) %collective-permute-start.39) | collective-permute-done | bytes 589856 | tf_op jit(solution)/shard_map/ppermute | solution.py:18
  197.1 24.7 %conditional.5 = ((bf16[3,256,768]{2,1,0:T(8,128)(2,1)}, bf16[3,4,256,384]{3,2,1,0:T(8,128)(2,1)}, bf16[3,4,256,192]{3,2,1,0:T(8,128)(2,1)}, bf16[3,4,256,384]{3...) conditional(s32[]{:T(128)} %convert_element_type.255, () %tuple.58, ...), branch_computations={%region_0.1_spmd, %region_1.2_spmd} | conditional | flops 4529848320 | bytes 27199496 | solution.py:569
  197.3 24.5 %attend_forward.3 = (bf16[3,256,768]{2,1,0:T(8,128)(2,1)}, bf16[3,4,256,384]{3,2,1,0:T(8,128)(2,1)}, bf16[3,4,256,192]{3,2,1,0:T(8,128)(2,1)}, bf16[3,4,256,384]...) custom-call(bf16[3,256,768]{2,1,0:T(8,128)(2,1)S(1)} %get-tuple-element.2, ...), custom_call_target="tpu_custom_call" | custom-call | flops 4529848320 | bytes 27199488 | tf_op jit(solution)/shard_map/cond/branch_1_fun/attend_forward/pallas_call | solution.py:320
  221.9 18.6 %conditional.6 = ((bf16[3,256,3072]{2,1,0:T(8,128)(2,1)}, bf16[3,256,3072]{2,1,0:T(8,128)(2,1)}, bf16[3,256,768]{2,1,0:T(8,128)(2,1)}, bf16[3,256,768]{2,1,0:T(8,128)(2,1)S(1)})) conditional(s32[]{:T(128)} %convert_element_type.255, () %tuple.57, (bf16[3,256,768]{2,1,0:T(8,128)(2,1)}, f32[3,256,768]{2,1,0:T(8,128)}, f32[3,6,768]{2,1,0:T(8,128)S(1)}, ...), branch_computations={%region_2.3_spmd, %region_3.4_spmd} | conditional | flops 7247757312 | bytes 38999076 | solution.py:569
  222.7 17.7 %lift_forward.3 = (bf16[3,256,3072]{2,1,0:T(8,128)(2,1)}, bf16[3,256,3072]{2,1,0:T(8,128)(2,1)}, bf16[3,256,768]{2,1,0:T(8,128)(2,1)}, bf16[3,256,768]{2,1,0:T(8,128)(2,1)S(1)}) custom-call(bf16[3,256,768]{2,1,0:T(8,128)(2,1)} %get-tuple-element.295.refs_0_, f32[3,256,768]{2,1,0:T(8,128)} %get-tuple-element.296.refs_1_, ...), custom_call_target="tpu_custom_call" | custom-call | flops 7247757312 | bytes 36639744 | tf_op jit(solution)/shard_map/cond/branch_1_fun/lift_forward/pallas_call | solution.py:320
  244.2 20.6 %conditional.7 = (bf16[3,256,768]{2,1,0:T(8,128)(2,1)S(1)}, bf16[3,256,768]{2,1,0:T(8,128)(2,1)}, bf16[3,256,768]{2,1,0:T(8,128)(2,1)}, bf16[3,4,256,384]{3,2,1,...) conditional(s32[]{:T(128)} %convert_element_type.255, ...), branch_computations={%region_4.5_spmd, %region_5.6_spmd} | conditional | flops 24461770752 | bytes 166727168 | solution.py:592
  279.5 61.6 %collective-permute-done.49 = bf16[3,256,768]{2,1,0:T(8,128)(2,1)S(1)} collective-permute-done((bf16[3,256,768]{2,1,0:T(8,128)(2,1)}, bf16[3,256,768]{2,1,0:T(8,128)(2,1)S(1)}, u32[]{:S(2)}, u32[]{:S(2)}) %collective-permute-start.49) | collective-permute-done | bytes 1179680 | tf_op jit(solution)/shard_map/ppermute | solution.py:595
  341.1 33.7 %conditional.8 = (f32[3,256,768]{2,1,0:T(8,128)S(1)}, f32[3,4,768]{2,1,0:T(4,128)}, f32[3,8,384]{2,1,0:T(8,128)S(1)}, bf16[768,384]{1,0:T(8,128)(2,1)}, bf16[768...) conditional(s32[]{:T(128)} %convert_element_type.255, ...), branch_computations={%region_6.7_spmd, %region_7.8_spmd} | conditional | flops 14495514624 | bytes 59111604 | solution.py:569
  342.3 18.9 %lift_backward.4 = (bf16[3,256,768]{2,1,0:T(8,128)(2,1)S(1)}, bf16[3,256,3072]{2,1,0:T(8,128)(2,1)}, f32[3,256,768]{2,1,0:T(8,128)S(1)}, f32[3,4,768]{2,1,0:T(4,128)}, f32[3,8,384]{2,1,0:T(8,128)S(1)}) custom-call(bf16[3,256,768]{2,1,0:T(8,128)(2,1)} %copy-done.43, bf16[3,256,768]{2,1,0:T(8,128)(2,1)} %get-tuple-element.395.refs_1_, ...), custom_call_target="tpu_custom_call" | custom-call | flops 7247757312 | bytes 33159168 | tf_op jit(solution)/shard_map/cond/branch_1_fun/lift_backward/pallas_call | solution.py:320
  361.3 13.6 %lift_weights.3 = (bf16[768,384]{1,0:T(8,128)(2,1)}, bf16[768,384]{1,0:T(8,128)(2,1)}, bf16[768,384]{1,0:T(8,128)(2,1)}, bf16[768,384]{1,0:T(8,128)(2,1)S(1)}, b...) custom-call(bf16[3,256,768]{2,1,0:T(8,128)(2,1)} %get-tuple-element., ...), custom_call_target="tpu_custom_call" | custom-call | flops 7247757312 | bytes 21233664 | tf_op jit(solution)/shard_map/cond/branch_1_fun/lift_weights/pallas_call | solution.py:338
  374.9 40.7 %conditional.9 = (bf16[3,256,768]{2,1,0:T(8,128)(2,1)}, f32[3,4,768]{2,1,0:T(4,128)}, f32[3,8,384]{2,1,0:T(8,128)S(1)}, bf16[768,384]{1,0:T(8,128)(2,1)}, bf16[7...) conditional(s32[]{:T(128)} %convert_element_type.255, ...), branch_computations={%region_8.9_spmd, %region_9.10_spmd} | conditional | flops 10871635968 | bytes 55572624 | solution.py:569
  375.3 30.1 %attend_backward.4 = (bf16[3,256,768]{2,1,0:T(8,128)(2,1)S(1)}, bf16[3,4,256,384]{3,2,1,0:T(8,128)(2,1)S(1)}, bf16[3,4,256,384]{3,2,1,0:T(8,128)(2,1)}, bf16[3,2...) custom-call(f32[3,256,768]{2,1,0:T(8,128)S(1)} %get-tuple-element.454.refs_0_, ...), custom_call_target="tpu_custom_call" | custom-call | flops 5435817984 | bytes 27260928 | tf_op jit(solution)/shard_map/cond/branch_1_fun/attend_backward/pallas_call | solution.py:320
  405.4 10.0 %attend_weights.3 = (bf16[768,384]{1,0:T(8,128)(2,1)}, bf16[768,384]{1,0:T(8,128)(2,1)}, bf16[768,384]{1,0:T(8,128)(2,1)}, bf16[768,384]{1,0:T(8,128)(2,1)}, bf1...) custom-call(bf16[3,256,768]{2,1,0:T(8,128)(2,1)S(1)} %copy-done.5, ...), custom_call_target="tpu_custom_call" | custom-call | flops 5435817984 | bytes 14155776 | tf_op jit(solution)/shard_map/cond/branch_1_fun/attend_weights/pallas_call | solution.py:338
  470.8 12.8 %collective-permute-done.62 = bf16[12,768]{1,0:T(8,128)(2,1)S(1)} collective-permute-done((bf16[12,768]{1,0:T(8,128)(2,1)S(1)}, bf16[12,768]{1,0:T(8,128)(2,1)S(1)}, u32[]{:S(2)}, u32[]{:S(2)}) %collective-permute-start.62) | collective-permute-done | bytes 18464 | tf_op jit(solution)/shard_map/ppermute | solution.py:18
  505.1 12.4 %collective-permute-done.83 = bf16[768,384]{1,0:T(8,128)(2,1)S(1)} collective-permute-done((bf16[768,384]{1,0:T(8,128)(2,1)}, bf16[768,384]{1,0:T(8,128)(2,1)S(1)}, u32[]{:S(2)}, u32[]{:S(2)}) %collective-permute-start.83) | collective-permute-done | bytes 589856 | tf_op jit(solution)/shard_map/ppermute | solution.py:18
  519.0 10.4 %collective-permute-done.86 = bf16[768,384]{1,0:T(8,128)(2,1)S(1)} collective-permute-done((bf16[768,384]{1,0:T(8,128)(2,1)S(1)}, bf16[768,384]{1,0:T(8,128)(2,1)S(1)}, u32[]{:S(2)}, u32[]{:S(2)}) %collective-permute-start.86) | collective-permute-done | bytes 589856 | tf_op jit(solution)/shard_map/ppermute | solution.py:18
  534.1 8.0 %collective-permute-done.84 = bf16[768,384]{1,0:T(8,128)(2,1)S(1)} collective-permute-done((bf16[768,384]{1,0:T(8,128)(2,1)S(1)}, bf16[768,384]{1,0:T(8,128)(2,1)S(1)}, u32[]{:S(2)}, u32[]{:S(2)}) %collective-permute-start.84) | collective-permute-done | bytes 589856 | tf_op jit(solution)/shard_map/ppermute | solution.py:18
  (507 shorter events, 296.5 us)
Async XLA Ops:
  22.5 46.8 %collective-permute-start.19 = (bf16[192,768]{0,1:T(8,128)(2,1)S(1)}, bf16[192,768]{0,1:T(8,128)(2,1)S(1)}, u32[]{:S(2)}, u32[]{:S(2)}) collective-permute-start(bf16[192,768]{0,1:T(8,128)(2,1)S(1)} %copy-done.29), channel_id=1, source_target_pairs={{0,8},{4,12},{8,0},{12,4},{1,9},{5,13},{9,1},{13,5},{2,10},{6,14},... | collective-permute-start | bytes 884744 | tf_op jit(solution)/shard_map/ppermute | solution.py:23
  25.3 43.1 %collective-permute-start.18 = (bf16[192,768]{0,1:T(8,128)(2,1)S(1)}, bf16[192,768]{0,1:T(8,128)(2,1)S(1)}, u32[]{:S(2)}, u32[]{:S(2)}) collective-permute-start(bf16[192,768]{0,1:T(8,128)(2,1)S(1)} %copy-done.29), channel_id=1, source_target_pairs={{0,4},{4,8},{8,12},{12,0},{1,5},{5,9},{9,13},{13,1},{2,6},{6,10},{... | collective-permute-start | bytes 884744 | tf_op jit(solution)/shard_map/ppermute | solution.py:23
  80.8 27.1 %collective-permute-start.29 = (bf16[192,768]{1,0:T(8,128)(2,1)S(1)}, bf16[192,768]{1,0:T(8,128)(2,1)S(1)}, u32[]{:S(2)}, u32[]{:S(2)}) collective-permute-start(bf16[192,768]{1,0:T(8,128)(2,1)S(1)} %bitcast.245), channel_id=1, source_target_pairs={{0,12},{4,0},{8,4},{12,8},{1,13},{5,1},{9,5},{13,9},{2,14},{6,2},{... | collective-permute-start | bytes 884744 | tf_op jit(solution)/shard_map/ppermute | solution.py:23
  84.5 40.9 %collective-permute-start.24 = (bf16[768,384]{1,0:T(8,128)(2,1)S(1)}, bf16[768,384]{1,0:T(8,128)(2,1)S(1)}, u32[]{:S(2)}, u32[]{:S(2)}) collective-permute-start(bf16[768,384]{1,0:T(8,128)(2,1)S(1)} %get-tuple-element.684), channel_id=1, source_target_pairs={{0,1},{1,0},{2,3},{3,2},{4,5},{5,4},{6,7},{7,6},{8,9},{9,8},{10,11... | collective-permute-start | bytes 1769480 | tf_op jit(solution)/shard_map/ppermute | solution.py:18
  107.2 31.9 %collective-permute-start.22 = (bf16[768,384]{1,0:T(8,128)(2,1)S(1)}, bf16[768,384]{1,0:T(8,128)(2,1)S(1)}, u32[]{:S(2)}, u32[]{:S(2)}) collective-permute-start(bf16[768,384]{1,0:T(8,128)(2,1)S(1)} %get-tuple-element.685), channel_id=1, source_target_pairs={{0,2},{1,3},{2,0},{3,1},{4,6},{5,7},{6,4},{7,5},{8,10},{9,11},{10,... | collective-permute-start | bytes 1769480 | tf_op jit(solution)/shard_map/ppermute | solution.py:18
  153.8 28.7 %collective-permute-start.42 = (bf16[768,384]{1,0:T(8,128)(2,1)}, bf16[768,384]{1,0:T(8,128)(2,1)}, u32[]{:S(2)}, u32[]{:S(2)}) collective-permute-start(bf16[768,384]{1,0:T(8,128)(2,1)} %get-tuple-element.567), channel_id=1, source_target_pairs={{0,2},{1,3},{2,0},{3,1},{4,6},{5,7},{6,4},{7,5},{8,10},{9,11},{10,... | collective-permute-start | bytes 1769480 | tf_op jit(solution)/shard_map/ppermute | solution.py:18
  155.9 37.9 %collective-permute-start.39 = (bf16[768,384]{1,0:T(8,128)(2,1)}, bf16[768,384]{1,0:T(8,128)(2,1)}, u32[]{:S(2)}, u32[]{:S(2)}) collective-permute-start(bf16[768,384]{1,0:T(8,128)(2,1)} %get-tuple-element.566), channel_id=1, source_target_pairs={{0,1},{1,0},{2,3},{3,2},{4,5},{5,4},{6,7},{7,6},{8,9},{9,8},{10,11... | collective-permute-start | bytes 1769480 | tf_op jit(solution)/shard_map/ppermute | solution.py:18
  168.4 53.4 %collective-permute-start.40 = (bf16[768,384]{1,0:T(8,128)(2,1)}, bf16[768,384]{1,0:T(8,128)(2,1)}, u32[]{:S(2)}, u32[]{:S(2)}) collective-permute-start(bf16[768,384]{1,0:T(8,128)(2,1)} %get-tuple-element.567), channel_id=1, source_target_pairs={{0,1},{1,0},{2,3},{3,2},{4,5},{5,4},{6,7},{7,6},{8,9},{9,8},{10,11... | collective-permute-start | bytes 1769480 | tf_op jit(solution)/shard_map/ppermute | solution.py:18
  169.8 52.1 %collective-permute-start.41 = (bf16[768,384]{1,0:T(8,128)(2,1)}, bf16[768,384]{1,0:T(8,128)(2,1)}, u32[]{:S(2)}, u32[]{:S(2)}) collective-permute-start(bf16[768,384]{1,0:T(8,128)(2,1)} %get-tuple-element.566), channel_id=1, source_target_pairs={{0,2},{1,3},{2,0},{3,1},{4,6},{5,7},{6,4},{7,5},{8,10},{9,11},{10,... | collective-permute-start | bytes 1769480 | tf_op jit(solution)/shard_map/ppermute | solution.py:18
  181.1 40.8 %collective-permute-start.34 = (bf16[768,384]{1,0:T(8,128)(2,1)}, bf16[768,384]{1,0:T(8,128)(2,1)}, u32[]{:S(2)}, u32[]{:S(2)}) collective-permute-start(bf16[768,384]{1,0:T(8,128)(2,1)} %collective-permute-done.30), channel_id=1, source_target_pairs={{0,2},{1,3},{2,0},{3,1},{4,6},{5,7},{6,4},{7,5},{8,10},{9,11},{10,... | collective-permute-start | bytes 1769480 | tf_op jit(solution)/shard_map/ppermute | solution.py:18
  182.5 39.3 %collective-permute-start.44 = (bf16[768,384]{1,0:T(8,128)(2,1)}, bf16[768,384]{1,0:T(8,128)(2,1)}, u32[]{:S(2)}, u32[]{:S(2)}) collective-permute-start(bf16[768,384]{1,0:T(8,128)(2,1)} %collective-permute-done.42), channel_id=1, source_target_pairs={{0,1},{1,0},{2,3},{3,2},{4,5},{5,4},{6,7},{7,6},{8,9},{9,8},{10,11... | collective-permute-start | bytes 1769480 | tf_op jit(solution)/shard_map/ppermute | solution.py:18
  193.8 28.1 %collective-permute-start.43 = (bf16[768,384]{1,0:T(8,128)(2,1)}, bf16[768,384]{1,0:T(8,128)(2,1)}, u32[]{:S(2)}, u32[]{:S(2)}) collective-permute-start(bf16[768,384]{1,0:T(8,128)(2,1)} %collective-permute-done.39), channel_id=1, source_target_pairs={{0,2},{1,3},{2,0},{3,1},{4,6},{5,7},{6,4},{7,5},{8,10},{9,11},{10,... | collective-permute-start | bytes 1769480 | tf_op jit(solution)/shard_map/ppermute | solution.py:18
  264.9 76.2 %collective-permute-start.49 = (bf16[3,256,768]{2,1,0:T(8,128)(2,1)}, bf16[3,256,768]{2,1,0:T(8,128)(2,1)S(1)}, u32[]{:S(2)}, u32[]{:S(2)}) collective-permute-start(bf16[3,256,768]{2,1,0:T(8,128)(2,1)} %get-tuple-element.575), channel_id=1, source_target_pairs={{16,0},{17,1},{18,2},{19,3},{20,4},{21,5},{22,6},{23,7},{24,8},{25... | collective-permute-start | bytes 3538952 | tf_op jit(solution)/shard_map/ppermute | solution.py:595
  436.6 51.8 %collective-permute-start.50 = (bf16[3,64,768]{2,1,0:T(8,128)(2,1)}, bf16[3,64,768]{2,1,0:T(8,128)(2,1)}, u32[]{:S(2)}, u32[]{:S(2)}) collective-permute-start(bf16[3,64,768]{2,1,0:T(8,128)(2,1)} %get-tuple-element.669), channel_id=1, source_target_pairs={{0,1},{1,0},{2,3},{3,2},{4,5},{5,4},{6,7},{7,6},{8,9},{9,8},{10,11... | collective-permute-start | bytes 884744 | tf_op jit(solution)/shard_map/ppermute | solution.py:18
  438.3 52.3 %collective-permute-start.52 = (bf16[3,64,768]{2,1,0:T(8,128)(2,1)}, bf16[3,64,768]{2,1,0:T(8,128)(2,1)}, u32[]{:S(2)}, u32[]{:S(2)}) collective-permute-start(bf16[3,64,768]{2,1,0:T(8,128)(2,1)} %get-tuple-element.670), channel_id=1, source_target_pairs={{0,3},{1,2},{2,1},{3,0},{4,7},{5,6},{6,5},{7,4},{8,11},{9,10},{10,... | collective-permute-start | bytes 884744 | tf_op jit(solution)/shard_map/ppermute | solution.py:18
  464.7 25.9 %collective-permute-start.51 = (bf16[3,64,768]{2,1,0:T(8,128)(2,1)S(1)}, bf16[3,64,768]{2,1,0:T(8,128)(2,1)}, u32[]{:S(2)}, u32[]{:S(2)}) collective-permute-start(bf16[3,64,768]{2,1,0:T(8,128)(2,1)S(1)} %get-tuple-element.671), channel_id=1, source_target_pairs={{0,2},{1,3},{2,0},{3,1},{4,6},{5,7},{6,4},{7,5},{8,10},{9,11},{10,... | collective-permute-start | bytes 884744 | tf_op jit(solution)/shard_map/ppermute | solution.py:18
  466.6 29.2 %collective-permute-start.65 = (bf16[768,384]{1,0:T(8,128)(2,1)}, bf16[768,384]{1,0:T(8,128)(2,1)S(1)}, u32[]{:S(2)}, u32[]{:S(2)}) collective-permute-start(bf16[768,384]{1,0:T(8,128)(2,1)} %get-tuple-element.599), channel_id=1, source_target_pairs={{0,1},{1,0},{2,3},{3,2},{4,5},{5,4},{6,7},{7,6},{8,9},{9,8},{10,11... | collective-permute-start | bytes 1769480 | tf_op jit(solution)/shard_map/ppermute | solution.py:18
  488.4 41.9 %collective-permute-start.74 = (bf16[768,384]{1,0:T(8,128)(2,1)S(1)}, bf16[768,384]{1,0:T(8,128)(2,1)S(1)}, u32[]{:S(2)}, u32[]{:S(2)}) collective-permute-start(bf16[768,384]{1,0:T(8,128)(2,1)S(1)} %copy-done.64), channel_id=1, source_target_pairs={{0,1},{1,0},{2,3},{3,2},{4,5},{5,4},{6,7},{7,6},{8,9},{9,8},{10,11... | collective-permute-start | bytes 1769480 | tf_op jit(solution)/shard_map/ppermute | solution.py:18
  490.6 41.2 %collective-permute-start.77 = (bf16[768,384]{1,0:T(8,128)(2,1)S(1)}, bf16[768,384]{1,0:T(8,128)(2,1)S(1)}, u32[]{:S(2)}, u32[]{:S(2)}) collective-permute-start(bf16[768,384]{1,0:T(8,128)(2,1)S(1)} %copy-done.65), channel_id=1, source_target_pairs={{0,2},{1,3},{2,0},{3,1},{4,6},{5,7},{6,4},{7,5},{8,10},{9,11},{10,... | collective-permute-start | bytes 1769480 | tf_op jit(solution)/shard_map/ppermute | solution.py:18
  490.6 26.9 %collective-permute-start.83 = (bf16[768,384]{1,0:T(8,128)(2,1)}, bf16[768,384]{1,0:T(8,128)(2,1)S(1)}, u32[]{:S(2)}, u32[]{:S(2)}) collective-permute-start(bf16[768,384]{1,0:T(8,128)(2,1)} %get-tuple-element.615), channel_id=1, source_target_pairs={{0,1},{1,0},{2,3},{3,2},{4,5},{5,4},{6,7},{7,6},{8,9},{9,8},{10,11... | collective-permute-start | bytes 1769480 | tf_op jit(solution)/shard_map/ppermute | solution.py:18
  495.8 33.6 %collective-permute-start.86 = (bf16[768,384]{1,0:T(8,128)(2,1)S(1)}, bf16[768,384]{1,0:T(8,128)(2,1)S(1)}, u32[]{:S(2)}, u32[]{:S(2)}) collective-permute-start(bf16[768,384]{1,0:T(8,128)(2,1)S(1)} %copy-done.68), channel_id=1, source_target_pairs={{0,2},{1,3},{2,0},{3,1},{4,6},{5,7},{6,4},{7,5},{8,10},{9,11},{10,... | collective-permute-start | bytes 1769480 | tf_op jit(solution)/shard_map/ppermute | solution.py:18
  504.3 28.6 %collective-permute-start.82 = (bf16[768,384]{1,0:T(8,128)(2,1)S(1)}, bf16[768,384]{1,0:T(8,128)(2,1)S(1)}, u32[]{:S(2)}, u32[]{:S(2)}) collective-permute-start(bf16[768,384]{1,0:T(8,128)(2,1)S(1)} %copy-done.66), channel_id=1, source_target_pairs={{0,1},{1,0},{2,3},{3,2},{4,5},{5,4},{6,7},{7,6},{8,9},{9,8},{10,11... | collective-permute-start | bytes 1769480 | tf_op jit(solution)/shard_map/ppermute | solution.py:18
  517.4 25.6 %collective-permute-start.85 = (bf16[768,384]{1,0:T(8,128)(2,1)S(1)}, bf16[768,384]{1,0:T(8,128)(2,1)S(1)}, u32[]{:S(2)}, u32[]{:S(2)}) collective-permute-start(bf16[768,384]{1,0:T(8,128)(2,1)S(1)} %copy-done.67), channel_id=1, source_target_pairs={{0,2},{1,3},{2,0},{3,1},{4,6},{5,7},{6,4},{7,5},{8,10},{9,11},{10,... | collective-permute-start | bytes 1769480 | tf_op jit(solution)/shard_map/ppermute | solution.py:18
  531.8 27.9 %collective-permute-start.64 = (bf16[768,384]{1,0:T(8,128)(2,1)S(1)}, bf16[768,384]{1,0:T(8,128)(2,1)S(1)}, u32[]{:S(2)}, u32[]{:S(2)}) collective-permute-start(bf16[768,384]{1,0:T(8,128)(2,1)S(1)} %copy-done.69), channel_id=1, source_target_pairs={{0,1},{1,0},{2,3},{3,2},{4,5},{5,4},{6,7},{7,6},{8,9},{9,8},{10,11... | collective-permute-start | bytes 1769480 | tf_op jit(solution)/shard_map/ppermute | solution.py:18
  (140 other events, 2274.7 us)

commit v3 on v2

v3 whole, which is shorter than its diff:
```python
import functools
import math

import jax
import jax.numpy as jnp
from jax import lax
from jax.experimental import pallas as pl
from jax.experimental.pallas import tpu as pltpu
from jax.sharding import PartitionSpec as P

HEAD_DIM = 64
BF16 = jnp.bfloat16
F32 = jnp.float32


def swap(shard, axis, step):
    peers = lax.axis_size(axis)
    return lax.ppermute(shard, axis, [(i, i ^ step) for i in range(peers)])


def turned(shard, axis, by):
    peers = lax.axis_size(axis)
    return lax.ppermute(shard, axis, [(i, (i + by) % peers) for i in range(peers)])


def pick(blocks, index):
    return lax.dynamic_index_in_dim(blocks, index, 0, keepdims=False)


def direct_dp():
    return lax.axis_size("dp") == 4


def gather_dp(shard):
    peers = lax.axis_size("dp")
    if not direct_dp():
        return lax.all_gather(shard, "dp")
    place = lax.axis_index("dp")
    whole = jnp.zeros((peers,) + shard.shape, shard.dtype)
    for k in range(peers):
        piece = shard if k == 0 else turned(shard, "dp", k)
        whole = lax.dynamic_update_index_in_dim(whole, piece, (place - k) % peers, 0)
    return whole


def ordered(blocks):
    own = lax.axis_index("tensor")
    return jnp.stack([pick(blocks, b ^ own) for b in range(blocks.shape[0])])


def send_tensor(blocks):
    own = lax.axis_index("tensor")
    return [pick(blocks, own)] + [
        swap(pick(blocks, own ^ j), "tensor", j) for j in range(1, lax.axis_size("tensor"))
    ]


def spread_tensor(own, first, second):
    near = swap(own, "tensor", first)
    side = swap(own, "tensor", second)
    far = swap(near, "tensor", second)
    pieces = {0: own, first: near, second: side, first ^ second: far}
    return [pieces[j] for j in range(4)]


def first_hop(sent, kept, step):
    near = swap(sent, "tensor", step)
    rest = kept.shape[0] // 2
    return near, (kept[rest:].astype(F32) + near[rest:].astype(F32)).astype(BF16)


def second_hop(kept, near, onward, step):
    far = swap(onward, "tensor", step)
    rest = kept.shape[0] // 2
    return (kept[:rest].astype(F32) + near[:rest].astype(F32) + far.astype(F32)).astype(BF16)


def scatter_rows(parts):
    peers = lax.axis_size("dp")
    if not direct_dp():
        whole = jnp.concatenate(parts)
        return lax.psum_scatter(whole, "dp", scatter_dimension=1, tiled=True).astype(F32)
    place = lax.axis_index("dp")
    rows = parts[0].shape[1] // peers
    block = lambda at: jnp.concatenate(
        [lax.dynamic_slice_in_dim(part, at * rows, rows, 1) for part in parts]
    )
    total = block(place).astype(F32)
    for k in range(1, peers):
        total = total + turned(block((place + k) % peers), "dp", k).astype(F32)
    return total


VMEM_BYTES = 50 * 1024 * 1024
GELU_A = 0.7978845608028654
GELU_B = 0.044715


def dot(lhs, rhs, spec):
    return jnp.einsum(spec, lhs, rhs, preferred_element_type=F32)


def mm(lhs, rhs):
    return jnp.dot(lhs, rhs, preferred_element_type=F32)


def mm_nt(lhs, rhs):
    return lax.dot_general(lhs, rhs, (((1,), (1,)), ((), ())), preferred_element_type=F32)


def mm_tn(lhs, rhs):
    return lax.dot_general(lhs, rhs, (((0,), (0,)), ((), ())), preferred_element_type=F32)


def norm_parts(features):
    centred = features - jnp.mean(features, axis=-1, keepdims=True)
    spread = jnp.mean(centred * centred, axis=-1, keepdims=True)
    rate = lax.rsqrt(spread + 1e-06)
    return centred * rate, rate


def norm_back(unit, rate, grad):
    lean = jnp.mean(grad, axis=-1, keepdims=True)
    tilt = jnp.mean(grad * unit, axis=-1, keepdims=True)
    return rate * (grad - lean - unit * tilt)


def token_sum(part):
    return jnp.sum(part, axis=0, keepdims=True)


def head_cols(block, start, head):
    return block[:, start + head * HEAD_DIM : start + (head + 1) * HEAD_DIM]


def attend_kernel(ways, heads, refs):
    x_ref, mod_ref, bqk_ref, bv_ref, bproj_ref = refs[:5]
    pack_w = refs[5 : 5 + ways]
    na_ref, qk_ref, v_ref, att_ref, branch_ref, middle_ref, nb_ref = refs[5 + ways :]
    cols = heads * HEAD_DIM
    width = x_ref.shape[2]
    scale = HEAD_DIM**-0.5
    x = x_ref[0].astype(F32)
    shift_a, scale_a, gate_a = (mod_ref[0, i : i + 1, :] for i in range(3))
    shift_b, scale_b = (mod_ref[0, i : i + 1, :] for i in (3, 4))
    normed = (norm_parts(x)[0] * (1.0 + scale_a) + shift_a).astype(BF16)
    na_ref[0] = normed
    branch = jnp.zeros_like(x) + bproj_ref[...]
    for j in range(ways):
        qk = (mm(normed, pack_w[j][:width, : 2 * cols]) + bqk_ref[j : j + 1, :]).astype(BF16)
        value = (mm(normed, pack_w[j][:width, 2 * cols : 3 * cols]) + bv_ref[j : j + 1, :]).astype(BF16)
        qk_ref[0, j] = qk
        v_ref[0, j] = value
        outs = [jnp.zeros((x.shape[0], cols), F32)]
        for h in range(heads):
            query = head_cols(qk, 0, h) * jnp.asarray(scale, BF16)
            scores = mm_nt(query, head_cols(qk, cols, h))
            raised = jnp.exp(scores - jnp.max(scores, axis=-1, keepdims=True))
            total = jnp.sum(raised, axis=-1, keepdims=True)
            outs.append(mm(raised.astype(BF16), head_cols(value, 0, h)) * (1.0 / total))
        padded = jnp.concatenate(outs, axis=1).astype(BF16)
        att_ref[0, j] = padded
        branch = branch + mm_nt(padded, pack_w[j][:width, 2 * cols :])
    branch_ref[0] = branch.astype(BF16)
    middle = x + gate_a * branch
    middle_ref[0] = middle
    nb_ref[0] = (norm_parts(middle)[0] * (1.0 + scale_b) + shift_b).astype(BF16)


def lift_kernel(pieces, refs):
    nb_ref, middle_ref, mod_ref, bup_ref, bdown_ref = refs[:5]
    both_w = refs[5 : 5 + pieces]
    lifted_ref, hidden_ref, second_ref, out_ref = refs[5 + pieces :]
    normed = nb_ref[0]
    middle = middle_ref[0]
    gate_b = mod_ref[0, 5:6, :]
    second = jnp.zeros_like(middle) + bdown_ref[...]
    for c in range(pieces):
        part = both_w[c].shape[2]
        lifted = mm(normed, both_w[c][0]) + bup_ref[c : c + 1, :]
        turn = jnp.tanh(GELU_A * (lifted + GELU_B * lifted * lifted * lifted))
        hidden = (0.5 * lifted * (1.0 + turn)).astype(BF16)
        lifted_ref[0, :, c * part : (c + 1) * part] = lifted.astype(BF16)
        hidden_ref[0, :, c * part : (c + 1) * part] = hidden
        second = second + mm_nt(hidden, both_w[c][1])
    second_ref[0] = second.astype(BF16)
    out_ref[0] = (middle + gate_b * second).astype(BF16)


def lift_back_kernel(pieces, refs):
    g_ref, second_ref, lifted_ref, middle_ref, mod_ref = refs[:5]
    both_w = refs[5 : 5 + pieces]
    gs_ref, gl_ref, gm_ref, sums_ref, lift_sums_ref = refs[5 + pieces :]
    grad = g_ref[0].astype(F32)
    scale_b, gate_b = mod_ref[0, 4:5, :], mod_ref[0, 5:6, :]
    grad_second = (gate_b * grad).astype(BF16)
    gs_ref[0] = grad_second
    normed = jnp.zeros_like(grad)
    for c in range(pieces):
        part = both_w[c].shape[2]
        grad_hidden = mm(grad_second, both_w[c][1])
        v = lifted_ref[0, :, c * part : (c + 1) * part].astype(F32)
        square = v * v
        turn = jnp.tanh(GELU_A * v * (1.0 + GELU_B * square))
        slope = 0.5 * (1.0 + turn) + (0.5 * GELU_A) * v * (1.0 - turn * turn) * (
            1.0 + (3.0 * GELU_B) * square
        )
        grad_lifted = (grad_hidden * slope).astype(BF16)
        gl_ref[0, :, c * part : (c + 1) * part] = grad_lifted
        lift_sums_ref[0, c : c + 1, :] = token_sum(grad_lifted.astype(F32))
        normed = normed + mm_nt(grad_lifted, both_w[c][0])
    unit, rate = norm_parts(middle_ref[0])
    gm_ref[0] = grad + norm_back(unit, rate, normed * (1.0 + scale_b))
    sums_ref[0, 0:1, :] = token_sum(normed)
    sums_ref[0, 1:2, :] = token_sum(normed * unit)
    sums_ref[0, 2:3, :] = token_sum(grad * second_ref[0].astype(F32))
    sums_ref[0, 3:4, :] = token_sum(grad_second.astype(F32))


def attend_back_kernel(ways, heads, refs):
    gm_ref, branch_ref, qk_ref, v_ref, x_ref, mod_ref = refs[:6]
    pack_w = refs[6 : 6 + ways]
    gb_ref, gqk_ref, gv_ref, gi_ref, sums_ref, pack_sums_ref = refs[6 + ways :]
    cols = heads * HEAD_DIM
    width = gm_ref.shape[2]
    scale = HEAD_DIM**-0.5
    middle = gm_ref[0]
    scale_a, gate_a = mod_ref[0, 1:2, :], mod_ref[0, 2:3, :]
    grad_branch = (gate_a * middle).astype(BF16)
    gb_ref[0] = grad_branch
    normed = jnp.zeros_like(middle)
    for j in range(ways):
        grad_att = mm(grad_branch, pack_w[j][:width, 2 * cols :]).astype(BF16)
        qk = qk_ref[0, j]
        value = v_ref[0, j]
        grads_q, grads_k, grads_v = [], [], []
        for h in range(heads):
            query, key = head_cols(qk, 0, h), head_cols(qk, cols, h)
            grad_head = head_cols(grad_att, cols, h)
            scores = mm_nt(key, query * jnp.asarray(scale, BF16))
            raised = jnp.exp(scores - jnp.max(scores, axis=0, keepdims=True))
            probs = raised * (1.0 / jnp.sum(raised, axis=0, keepdims=True))
            grads_v.append(mm(probs.astype(BF16), grad_head))
            grad_probs = mm_nt(head_cols(value, 0, h), grad_head)
            total = jnp.sum(grad_probs * probs, axis=0, keepdims=True)
            grad_scores = (probs * (grad_probs - total)).astype(BF16)
            grads_k.append(mm(grad_scores, query) * scale)
            grads_q.append(mm_tn(grad_scores, key) * scale)
        grad_qk = jnp.concatenate(grads_q + grads_k, axis=1).astype(BF16)
        grads_v.append(jnp.zeros((middle.shape[0], cols), F32))
        grad_v = jnp.concatenate(grads_v, axis=1).astype(BF16)
        gqk_ref[0, j] = grad_qk
        gv_ref[0, j] = grad_v
        pack_sums_ref[0, j : j + 1, :] = token_sum(grad_qk.astype(F32))
        pack_sums_ref[0, ways + j : ways + j + 1, :] = token_sum(grad_v.astype(F32))
        normed = normed + mm_nt(grad_qk, pack_w[j][:width, : 2 * cols])
        normed = normed + mm_nt(grad_v, pack_w[j][:width, 2 * cols :])
    unit, rate = norm_parts(x_ref[0].astype(F32))
    gi_ref[0] = (middle + norm_back(unit, rate, normed * (1.0 + scale_a))).astype(BF16)
    sums_ref[0, 0:1, :] = token_sum(normed)
    sums_ref[0, 1:2, :] = token_sum(normed * unit)
    sums_ref[0, 2:3, :] = token_sum(middle * branch_ref[0].astype(F32))
    sums_ref[0, 3:4, :] = token_sum(grad_branch.astype(F32))


def flat_tokens(ref):
    return ref[...].reshape(ref.shape[0] * ref.shape[1], ref.shape[2])


SENT = {1: (1, 3), 2: (2, 3)}
KEPT = {1: (0, 2), 2: (0, 1)}


def lift_weights_kernel(refs):
    nb_ref, gl_ref, gs_ref, hidden_ref = refs[:4]
    outs = {1: refs[4:6], 2: refs[6:8]}
    part = refs[4].shape[2]
    for kind, (left_ref, right_ref) in enumerate(((gs_ref, hidden_ref), (nb_ref, gl_ref))):
        left = flat_tokens(left_ref).T
        for side, first in enumerate((1, 2)):
            for place, blocks in enumerate((SENT[first], KEPT[first])):
                for i, j in enumerate(blocks):
                    c = 2 * j + side
                    right = right_ref[:, :, c * part : (c + 1) * part]
                    right = right.reshape(right.shape[0] * right.shape[1], part)
                    outs[first][place][2 * i + kind] = mm(left, right).astype(BF16)


def attend_weights_kernel(refs):
    na_ref, gqk_ref, gv_ref, gb_ref, att_ref = refs[:5]
    outs = {1: refs[5:7], 2: refs[7:9]}
    latents = na_ref.shape[0]
    left_n = flat_tokens(na_ref).T
    left_b = flat_tokens(gb_ref).T
    over = lambda ref, j: jnp.concatenate([ref[g, j] for g in range(latents)], axis=0)
    for place in range(2):
        for i, j in enumerate((SENT, KEPT)[place][1]):
            outs[1][place][i] = mm(left_n, over(gqk_ref, j)).astype(BF16)
        for i, j in enumerate((SENT, KEPT)[place][2]):
            grad = mm(left_n, over(gv_ref, j)) + mm(left_b, over(att_ref, j))
            outs[2][place][i] = grad.astype(BF16)


def per_latent(shape):
    rank = len(shape)
    return pl.BlockSpec((1,) + tuple(shape[1:]), lambda g: (g,) + (0,) * (rank - 1))


def constant(shape):
    rank = len(shape)
    return pl.BlockSpec(tuple(shape), lambda g: (0,) * rank, pipeline_mode=pl.Buffered(1))


def over_latents(kernel, name, varying, fixed, outs, flops, run=None, others=()):
    flags = [] if run is None else [run]

    def whole(*refs):
        refs = refs[len(flags) :]
        ins, rest = refs[: len(varying)], refs[len(varying) : len(varying) + len(fixed)]
        kernel(ins + rest + refs[-len(outs) :])

    def flagged(*refs):
        flag = refs[0][0]

        @pl.when(flag == 1)
        def _():
            whole(*refs)

        if others:

            @pl.when(flag == 0)
            def _():
                start = 1 + len(varying) + len(fixed)
                for source, target in zip(refs[start : start + len(others)], refs[-len(outs) :]):
                    target[...] = source[...]

    return pl.pallas_call(
        flagged if flags else whole,
        grid=(varying[0].shape[0],),
        in_specs=[pl.BlockSpec(memory_space=pltpu.SMEM)] * len(flags)
        + [per_latent(a.shape) for a in varying]
        + [constant(a.shape) for a in fixed]
        + [per_latent(a.shape) for a in others],
        out_specs=[per_latent(shape) for shape, _ in outs],
        out_shape=[jax.ShapeDtypeStruct(shape, dtype) for shape, dtype in outs],
        compiler_params=pltpu.CompilerParams(vmem_limit_bytes=VMEM_BYTES),
        cost_estimate=pl.CostEstimate(
            flops=flops,
            bytes_accessed=sum(a.size * a.dtype.itemsize for a in varying + fixed)
            + sum(2 * math.prod(shape) for shape, _ in outs),
            transcendentals=0,
        ),
        name=name,
    )(*flags, *varying, *fixed, *others)


def at_once(kernel, name, inputs, out_shapes, flops):
    return pl.pallas_call(
        lambda *refs: kernel(refs),
        in_specs=[pl.BlockSpec(memory_space=pltpu.VMEM)] * len(inputs),
        out_specs=[pl.BlockSpec(memory_space=pltpu.VMEM)] * len(out_shapes),
        out_shape=[jax.ShapeDtypeStruct(shape, BF16) for shape in out_shapes],
        compiler_params=pltpu.CompilerParams(vmem_limit_bytes=VMEM_BYTES),
        cost_estimate=pl.CostEstimate(
            flops=flops,
            bytes_accessed=sum(a.size * a.dtype.itemsize for a in inputs)
            + sum(2 * math.prod(shape) for shape in out_shapes),
            transcendentals=0,
        ),
        name=name,
    )(*inputs)


def attend_forward(tokens_in, mod6, weights, biases):
    pack_w = weights[0]
    b_qk, b_v, b_proj = biases[:3]
    ways, cols = len(pack_w), b_v.shape[1]
    latents, tokens, width = tokens_in.shape
    whole = (latents, tokens, width)
    return over_latents(
        functools.partial(attend_kernel, ways, cols // HEAD_DIM),
        "attend_forward",
        [tokens_in, mod6],
        [b_qk, b_v, b_proj, *pack_w],
        [
            (whole, BF16),
            ((latents, ways, tokens, 2 * cols), BF16),
            ((latents, ways, tokens, cols), BF16),
            ((latents, ways, tokens, 2 * cols), BF16),
            (whole, BF16),
            (whole, F32),
            (whole, BF16),
        ],
        10 * latents * tokens * width * width,
    )


def lift_forward(normed_b, middle, mod6, weights, biases):
    both_w = weights[1]
    b_up, b_down = biases[3:]
    whole = middle.shape
    wide = whole[:2] + (b_up.size,)
    return over_latents(
        functools.partial(lift_kernel, len(both_w)),
        "lift_forward",
        [normed_b, middle, mod6],
        [b_up, b_down, *both_w],
        [(wide, BF16), (wide, BF16), (whole, BF16), (whole, BF16)],
        4 * math.prod(whole) * b_up.size,
    )


def layer_forward(tokens_in, mod6, weights, biases):
    normed_a, qk, value, attended, branch, middle, normed_b = attend_forward(
        tokens_in, mod6, weights, biases
    )
    lifted, hidden, second, output = lift_forward(normed_b, middle, mod6, weights, biases)
    saved_a = (normed_a, qk, value, attended, branch)
    saved_b = (middle, normed_b, lifted, hidden, second)
    return output, saved_a, saved_b


def lift_backward(grad_out, mod6, weights, saved_b, run, others=()):
    both_w = weights[1]
    middle, normed_b, lifted, hidden, second = saved_b
    latents, tokens, width = middle.shape
    grad_second, grad_lifted, grad_middle, sums, lift_sums = over_latents(
        functools.partial(lift_back_kernel, len(both_w)),
        "lift_backward",
        [grad_out, second, lifted, middle, mod6],
        both_w,
        [
            (middle.shape, BF16),
            (lifted.shape, BF16),
            (middle.shape, F32),
            ((latents, 4, width), F32),
            ((latents, len(both_w), both_w[0].shape[2]), F32),
        ],
        4 * middle.size * lifted.shape[2],
        run,
        others,
    )
    outs = (grad_second, grad_lifted, grad_middle, sums, lift_sums)
    return outs, (normed_b, grad_lifted, grad_second, hidden)


def attend_backward(grad_middle, tokens_in, mod6, weights, saved_a, run, others=()):
    pack_w = weights[0]
    normed_a, qk, value, attended, branch = saved_a
    latents, tokens, width = grad_middle.shape
    cols = value.shape[3]
    grad_branch, grad_qk, grad_v, grad_input, sums, pack_sums = over_latents(
        functools.partial(attend_back_kernel, len(pack_w), cols // HEAD_DIM),
        "attend_backward",
        [grad_middle, branch, qk, value, tokens_in, mod6],
        pack_w,
        [
            (grad_middle.shape, BF16),
            (qk.shape, BF16),
            (qk.shape, BF16),
            (grad_middle.shape, BF16),
            ((latents, 4, width), F32),
            ((latents, 2 * len(pack_w), 2 * cols), F32),
        ],
        16 * grad_middle.size * width,
        run,
        others,
    )
    outs = (grad_branch, grad_qk, grad_v, grad_input, sums, pack_sums)
    return outs, (normed_a, grad_qk, grad_v, grad_branch, attended)


def lift_weights(kept):
    normed_b, grad_lifted = kept[:2]
    width, wide = normed_b.shape[2], grad_lifted.shape[2]
    shape = (4, width, wide // 8)
    return at_once(lift_weights_kernel, "lift_weights", kept, [shape] * 4, 4 * normed_b.size * wide)


def attend_weights(kept):
    normed_a, grad_qk = kept[:2]
    shape = (2, normed_a.shape[2], grad_qk.shape[3])
    flops = 6 * normed_a.size * grad_qk.shape[1] * grad_qk.shape[3]
    return at_once(attend_weights_kernel, "attend_weights", kept, [shape] * 4, flops)


def after(value, *others):
    return lax.optimization_barrier((value, others))[0]


def body(
    latents,
    cond,
    cotangent,
    live,
    w_qkv,
    w_proj,
    w_up,
    w_down,
    w_ada,
    bias_qv,
    bias_proj,
    bias_up,
    bias_down,
    bias_ada,
):
    micros, slots, tokens_own, width = latents.shape
    ways = lax.axis_size("tensor")
    dps = lax.axis_size("dp")
    share = micros * slots // ways
    own_t = lax.axis_index("tensor")
    is_first = lax.axis_index("section") == 0
    qkv_cols = w_qkv.shape[3]
    hidden_cols = w_up.shape[2]
    mod_cols = w_ada.shape[2]
    mod_w = w_ada[0]

    source = jnp.where(is_first, latents, cotangent).reshape(ways, share, tokens_own, width)
    tokens_in = jnp.concatenate(send_tensor(source), axis=1)

    half = hidden_cols // 2
    pair_cols = 2 * qkv_cols
    rows = width // dps
    pack_shard = jnp.concatenate(
        [w_qkv[0, :, 0], w_qkv[0, :, 1], w_qkv[0, :, 2], w_proj[0].T], axis=1
    )
    bias_shard = jnp.concatenate(
        [bias_qv[0, 0], bias_qv[0, 1], bias_proj[0], bias_up[0], bias_down[0], bias_ada[0]]
    )
    cuts = [bias_qv.shape[2]] * 2 + [b.shape[1] for b in (bias_proj, bias_up, bias_down, bias_ada)]
    bias_size = sum(cuts)
    latent_count = micros * slots
    act = jax.nn.silu(cond.astype(F32)).astype(BF16).reshape(latent_count, width)
    riders = jnp.concatenate([jnp.pad(bias_shard, (0, width - bias_size))[None], act])
    riders = jnp.pad(riders, ((0, -riders.shape[0] % 16), (0, 0)))
    first_kind = gather_dp(jnp.concatenate([pack_shard, riders]))
    bias_dp = first_kind[:, rows, :bias_size].reshape(-1)
    bias_dp = jnp.pad(bias_dp, (0, -bias_dp.shape[0] % (16 * 2 * pair_cols)))
    pack_own = jnp.concatenate(
        [first_kind[:, :rows].reshape(width, 2 * pair_cols), bias_dp.reshape(-1, 2 * pair_cols)]
    )
    act_all = lax.dynamic_slice_in_dim(
        first_kind[:, rows + 1 : rows + 1 + latent_count],
        lax.axis_index("dp") * rows,
        rows,
        2,
    )
    pack_own = after(pack_own, tokens_in)
    pack_w = [pack_own] + [swap(pack_own, "tensor", j) for j in range(1, ways)]
    second_kind = gather_dp(after(jnp.stack([w_up[0], w_down[0].T]), pack_own))
    mod_terms = dot(after(act_all, second_kind), mod_w, "kgd,dm->kgm")
    mod_block = jnp.sum(lax.all_to_all(mod_terms, "dp", 0, 0), axis=0)
    mod_block = lax.all_to_all(mod_block.reshape(ways, share, mod_cols), "tensor", 0, 0)
    both_own = jnp.transpose(second_kind, (1, 0, 2, 3)).reshape(2, width, hidden_cols)

    bias_rel = jnp.stack([part[width:].reshape(-1)[: dps * bias_size] for part in pack_w])
    bias_all = ordered(bias_rel).reshape(ways, dps, bias_size)
    bias_all = jnp.transpose(bias_all, (1, 0, 2)).astype(F32)
    full, start = [], 0
    for cut in cuts:
        full.append(bias_all[:, :, start : start + cut].reshape(-1))
        start += cut
    full_q, full_v, full_proj, full_up, full_down, full_ada = full
    by_xor = lambda vector: ordered(vector.reshape(ways, -1)).reshape(-1)
    bias_qk = by_xor(full_q).reshape(ways, -1)
    bias_qk = jnp.concatenate([bias_qk, jnp.zeros_like(bias_qk)], axis=1)
    biases = (
        bias_qk,
        by_xor(full_v).reshape(ways, -1),
        full_proj[None],
        by_xor(full_up).reshape(2 * ways, -1),
        full_down[None],
    )

    modulate = jnp.transpose(mod_block, (1, 0, 2)).reshape(share, ways * mod_cols) + full_ada
    mod6 = modulate.reshape(share, 6, width)

    both_a = spread_tensor(after(both_own[:, :, :half], pack_w), 1, 2)
    both_b = spread_tensor(after(both_own[:, :, half:], pack_w), 2, 1)
    weights = (pack_w, [piece for pair in zip(both_a, both_b) for piece in pair])

    slot_mask = (lax.broadcasted_iota(jnp.int32, (micros, slots), 1) < live).astype(F32)
    own_mask = pick(slot_mask.reshape(ways, share), own_t)

    on_first = jnp.where(is_first, 1, 0).astype(jnp.int32).reshape(1)

    def handed_back(whole):
        split = jnp.transpose(whole.reshape(share, ways, tokens_own, width), (1, 0, 2, 3))
        arrivals = [split[0]] + [swap(split[j], "tensor", j) for j in range(1, ways)]
        return ordered(jnp.stack(arrivals)).reshape(latents.shape)

    output_first = layer_forward(tokens_in, mod6, weights, biases)[0]
    arrived = lax.ppermute(output_first, "section", [(0, 1)])
    incoming = jnp.where(is_first, tokens_in, arrived)
    output, saved_a, saved_b = layer_forward(incoming, mod6, weights, biases)

    grad_out = tokens_in * own_mask[:, None, None].astype(BF16)
    lift_1, _ = lift_backward(grad_out, mod6, weights, saved_b, 1 - on_first)
    attend_1, _ = attend_backward(lift_1[2], incoming, mod6, weights, saved_a, 1 - on_first)
    back = lax.ppermute(attend_1[3], "section", [(1, 0)])

    layer_out = handed_back(output)
    back = after(back, layer_out)
    lift_outs, kept_b = lift_backward(back, mod6, weights, saved_b, on_first, lift_1)
    lift_slabs = lift_weights(kept_b)
    attend_outs, kept_a = attend_backward(
        after(lift_outs[2], lift_slabs), incoming, mod6, weights, saved_a, on_first, attend_1
    )
    sums_b = lift_outs[3:]
    grad_input, sums_a = attend_outs[3], attend_outs[4:]
    attend_slabs = attend_weights(kept_a)
    near_a, onward_a = first_hop(*lift_slabs[:2], 1)
    near_b, onward_b = first_hop(*lift_slabs[2:], 2)
    sums_a, sums_b = after((sums_a, sums_b), onward_a, onward_b)

    grad_mod = jnp.concatenate([sums_a[0][:, :3], sums_b[0][:, :3]], axis=1)
    grad_mod = grad_mod.reshape(share, 6 * width).astype(BF16)

    pack_sums = jnp.sum(sums_a[1], axis=0)
    parts = [
        by_xor(pack_sums[:ways, :qkv_cols].reshape(-1)),
        by_xor(pack_sums[ways:, :qkv_cols].reshape(-1)),
        jnp.sum(sums_a[0][:, 3], axis=0),
        by_xor(jnp.sum(sums_b[1], axis=0).reshape(-1)),
        jnp.sum(sums_b[0][:, 3], axis=0),
        jnp.sum(grad_mod.astype(F32), axis=0),
    ]
    bias_terms = jnp.concatenate([part.reshape(dps, ways, -1) for part in parts], axis=2)
    bias_terms = jnp.transpose(bias_terms, (1, 0, 2)).reshape(ways, -1)
    grad_groups = jnp.transpose(grad_mod.reshape(share, ways, mod_cols), (1, 0, 2))
    grad_groups = grad_groups.reshape(ways, -1).astype(F32)
    mod_size = grad_groups.shape[1]
    arrivals = jnp.concatenate([grad_groups, bias_terms], axis=1)
    arrivals = lax.all_to_all(arrivals, "tensor", 0, 0)
    grad_block = arrivals[:, :mod_size].reshape(latent_count, mod_cols)
    bias_terms = jnp.sum(arrivals[:, mod_size:], axis=0).reshape(dps, bias_size)

    grad_block = jnp.broadcast_to(grad_block.reshape(1, -1), (dps, grad_block.size))
    shared = lax.all_to_all(jnp.concatenate([grad_block, bias_terms], axis=1), "dp", 0, 0)
    grad_all = shared[:, : -bias_size].reshape(dps, latent_count, mod_cols).astype(BF16)
    bias_out = jnp.sum(shared[:, -bias_size:], axis=0)

    lift_a = second_hop(lift_slabs[1], near_a, after(onward_a, arrivals), 2)
    lift_b = second_hop(lift_slabs[3], near_b, after(onward_b, arrivals), 1)
    near_a, onward_a = first_hop(after(attend_slabs[0], arrivals), attend_slabs[1], 1)
    near_b, onward_b = first_hop(after(attend_slabs[2], arrivals), attend_slabs[3], 2)
    out_lift = scatter_rows([lift_a, lift_b])
    sum_qk = second_hop(attend_slabs[1], near_a, onward_a, 2)
    sum_vp = second_hop(attend_slabs[3], near_b, onward_b, 1)
    out_attend = scatter_rows(after([sum_qk, sum_vp], out_lift))
    shard_down = jnp.concatenate([out_lift[0], out_lift[2]], axis=1).T
    shard_up = jnp.concatenate([out_lift[1], out_lift[3]], axis=1)
    shard_qkv = jnp.concatenate([out_attend[0], out_attend[1][:, :qkv_cols]], axis=1)
    shard_qkv = shard_qkv.reshape(-1, 3, qkv_cols)
    shard_proj = out_attend[1][:, qkv_cols:].T

    shard_ada = dot(act_all, grad_all, "kgd,kgm->dm")
    ctx_terms = dot(after(grad_all, out_lift), mod_w, "kgm,dm->kgd").astype(BF16)
    ctx_terms = lax.all_to_all(ctx_terms, "dp", 0, 0)
    ctx = jnp.transpose(ctx_terms, (1, 0, 2)).reshape(latent_count, width)
    ctx, grad_input = after((ctx, grad_input), sum_qk, sum_vp)
    for axis, step in (("tensor", 1), ("tensor", 2), ("section", 1)):
        if axis == "section":
            ctx = after(ctx, out_attend, out_lift)
        ctx = (ctx.astype(F32) + swap(ctx, axis, step).astype(F32)).astype(BF16)
    silu_back = jax.vjp(jax.nn.silu, cond.astype(F32))[1]
    cond_grad = silu_back(ctx.astype(F32).reshape(cond.shape))[0].astype(BF16)
    bias_pieces, start = [], 0
    for cut in cuts:
        bias_pieces.append(bias_out[start : start + cut])
        start += cut

    input_grad = handed_back(grad_input)
    return (
        layer_out[None],
        input_grad[None],
        cond_grad,
        shard_qkv[None],
        shard_proj[None],
        shard_up[None],
        shard_down[None],
        shard_ada[None],
        jnp.stack(bias_pieces[:2])[None],
        bias_pieces[2][None],
        bias_pieces[3][None],
        bias_pieces[4][None],
        bias_pieces[5][None],
    )


def solution(mesh):
    both = ("dp", "tensor")
    return jax.shard_map(
        body,
        mesh=mesh,
        in_specs=(
            P(None, "dp", "tensor", None),
            P(None, "dp", None),
            P(None, "dp", "tensor", None),
            P(None, "dp"),
            P("section", "dp", None, "tensor"),
            P("section", "tensor", "dp"),
            P("section", "dp", "tensor"),
            P("section", "tensor", "dp"),
            P("section", "dp", "tensor"),
            P("section", None, both),
            P("section", both),
            P("section", both),
            P("section", both),
            P("section", both),
        ),
        out_specs=(
            P("section", None, "dp", "tensor", None),
            P("section", None, "dp", "tensor", None),
            P(None, "dp", None),
            P("section", "dp", None, "tensor"),
            P("section", "tensor", "dp"),
            P("section", "dp", "tensor"),
            P("section", "tensor", "dp"),
            P("section", "dp", "tensor"),
            P("section", None, both),
            P("section", both),
            P("section", both),
            P("section", both),
            P("section", both),
        ),
        check_vma=False,
    )
```

time: 618 us -> 544 us (0.88)
  waiting for transfers between devices: 286 us -> 187 us
  Pallas kernels: 115 us -> 176 us
  starting transfers between devices: 135 us -> 107 us
  other arithmetic: 18.1 us -> 36.1 us
  local copies, waits for them, and re-layouts: 43 us -> 27.3 us
  loops' own time: 8.08 us -> 0 us
    ppermute x60 -> x29, waiting for transfers between devices: 139 us -> 81 us  [swap(): return lax.ppermute(shard, axis, [(i, i ^ step) for i in range(peers)])]
    pallas_call x4 -> x8, Pallas kernels: 91.2 us -> 149 us  [over_latents(): pl.pallas_call(flagged if flags else whole, grid=(varying[0].shape[0],),...]
    ppermute x60 -> x29, starting transfers between devices: 64.7 us -> 32.6 us  [swap(): return lax.ppermute(shard, axis, [(i, i ^ step) for i in range(peers)])]
    all_to_all x0 -> x5, starting transfers between devices: none -> 32 us  [the longest x1 16.9 us: body(): mod_block = jnp.sum(lax.all_to_all(mod_terms, 'dp', 0, 0), axis=0)]
    ppermute x36 -> x12, waiting for transfers between devices: 83.3 us -> 51.4 us  [turned(): lax.ppermute(shard, axis, [(i, (i + by) % peers) for i in range(peers)])]
    ppermute x36 -> x12, starting transfers between devices: 68.1 us -> 38.6 us  [turned(): lax.ppermute(shard, axis, [(i, (i + by) % peers) for i in range(peers)])]
    ppermute x1, waiting for transfers between devices: 61.6 us -> 37 us  [body(): back = lax.ppermute(attend_1[3], 'section', [(1, 0)])]
    all_to_all x0 -> x5, waiting for transfers between devices: none -> 16 us  [the longest x1 8.52 us: body(): mod_block = jnp.sum(lax.all_to_all(mod_terms, 'dp', 0, 0), axis=0)]
  transfers between devices with their start and end apart: 98 -> 48, of which waited for: 47 -> 20; matrix products, arithmetic and copies ran while one was open for 6% -> 9% of each run, Pallas kernels for 4% -> 12%
where the time goes in v3:
time: 544 us; the launch traced here: 540 us
  waiting for transfers between devices  187 us (34%)
  Pallas kernels  176 us (32%)
  starting transfers between devices  107 us (20%)
  other arithmetic  36.1 us (7%)
  local copies, waits for them, and re-layouts  27.3 us (5%)
    pallas_call x8, Pallas kernels, over_latents(): pl.pallas_call(flagged if flags else whole, grid=(varying[0].shape[0],),...  149 us
    ppermute x29, waiting for transfers between devices, swap(): return lax.ppermute(shard, axis, [(i, i ^ step) for i in range(peers)])  81 us
    ppermute x12, waiting for transfers between devices, turned(): lax.ppermute(shard, axis, [(i, (i + by) % peers) for i in range(peers)])  51.4 us
    ppermute x12, starting transfers between devices, turned(): lax.ppermute(shard, axis, [(i, (i + by) % peers) for i in range(peers)])  38.6 us
    ppermute x1, waiting for transfers between devices, body(): back = lax.ppermute(attend_1[3], 'section', [(1, 0)])  37 us
    ppermute x29, starting transfers between devices, swap(): return lax.ppermute(shard, axis, [(i, i ^ step) for i in range(peers)])  32.6 us
    pallas_call x2, Pallas kernels, at_once(): pl.pallas_call(lambda *refs: kernel(refs), in_specs=[pl.BlockSpec(memory_...  27.4 us
    all_to_all x1, starting transfers between devices, body(): mod_block = jnp.sum(lax.all_to_all(mod_terms, 'dp', 0, 0), axis=0)  16.9 us
  transfers between devices with their start and end apart: 48, of which 20 were waited for; matrix products, arithmetic and copies ran while one was open for 9% of the time, Pallas kernels for 12%

profile of v3, /device:TPU:0, one launch (start us, length us, event | category | flops | bytes accessed | tf_op | source)
XLA Modules:
  0.0 539.7 jit_solution(4969296370194679885)
XLA Ops:
  23.3 10.5 %collective-permute-done.4 = bf16[208,768]{1,0:T(8,128)(2,1)S(1)} collective-permute-done((bf16[208,768]{1,0:T(8,128)(2,1)}, bf16[208,768]{1,0:T(8,128)(2,1)S(1)}, u32[]{:S(2)}, u32[]{:S(2)}) %collective-permute-start.4) | collective-permute-done | bytes 319520 | tf_op jit(solution)/shard_map/ppermute | solution.py:23
  35.3 7.3 %collective-permute-start.6 = (bf16[2,192,768]{2,1,0:T(8,128)(2,1)}, bf16[2,192,768]{2,1,0:T(8,128)(2,1)}, u32[]{:S(2)}, u32[]{:S(2)}) collective-permute-start(bf16[2,192,768]{2,1,0:T(8,128)(2,1)} %pad_maximum_fusion.5), channel_id=1, source_target_pairs={{0,4},{4,8},{8,12},{12,0},{1,5},{5,9},{9,13},{13,1},{2,6},{6,10},{... | collective-permute-start | bytes 1769480 | tf_op jit(solution)/shard_map/ppermute | solution.py:23
  49.3 9.1 %collective-permute-done.6 = bf16[2,192,768]{2,1,0:T(8,128)(2,1)} collective-permute-done((bf16[2,192,768]{2,1,0:T(8,128)(2,1)}, bf16[2,192,768]{2,1,0:T(8,128)(2,1)}, u32[]{:S(2)}, u32[]{:S(2)}) %collective-permute-start.6) | collective-permute-done | bytes 589856 | tf_op jit(solution)/shard_map/ppermute | solution.py:23
  61.0 19.9 %collective-permute-done.7 = bf16[2,192,768]{2,1,0:T(8,128)(2,1)S(1)} collective-permute-done((bf16[2,192,768]{2,1,0:T(8,128)(2,1)}, bf16[2,192,768]{2,1,0:T(8,128)(2,1)S(1)}, u32[]{:S(2)}, u32[]{:S(2)}) %collective-permute-start.7) | collective-permute-done | bytes 589856 | tf_op jit(solution)/shard_map/ppermute | solution.py:23
  82.0 16.9 %all-to-all-start = ((f32[4,12,1152]{2,1,0:T(8,128)}), f32[4,12,1152]{2,1,0:T(8,128)}, u32[]{:S(2)}, u32[]{:S(2)}) async-start(f32[4,12,1152]{2,1,0:T(8,128)} %fusion.1), calls=%async_computation | async-start | bytes 589824 | tf_op jit(solution)/shard_map/all_to_all | solution.py:552
  99.7 8.5 %all-to-all-done = f32[4,12,1152]{2,1,0:T(8,128)} async-done(((f32[4,12,1152]{2,1,0:T(8,128)}), f32[4,12,1152]{2,1,0:T(8,128)}, u32[]{:S(2)}, u32[]{:S(2)}) %all-to-all-start) | async-done | bytes 221216 | tf_op jit(solution)/shard_map/all_to_all | solution.py:552
  126.0 22.0 %collective-permute-done.15.refs_10_.refs_11_ = bf16[2,768,384]{2,1,0:T(8,128)(2,1)S(1)} collective-permute-done((bf16[2,768,384]{2,1,0:T(8,128)(2,1)}, bf16[2,768,384]{2,1,0:T(8,128)(2,1)S(1)}, u32[]{:S(2)}, u32[]{:S(2)}) %collective-permute-start.15) | collective-permute-done | bytes 1179680 | tf_op jit(solution)/shard_map/ppermute | solution.py:18
  148.9 25.2 %collective-permute-done.12.refs_7_.refs_8_ = bf16[2,768,384]{2,1,0:T(8,128)(2,1)} collective-permute-done((bf16[2,768,384]{2,1,0:T(8,128)(2,1)}, bf16[2,768,384]{2,1,0:T(8,128)(2,1)}, u32[]{:S(2)}, u32[]{:S(2)}) %collective-permute-start.12) | collective-permute-done | bytes 1179680 | tf_op jit(solution)/shard_map/ppermute | solution.py:18
  176.1 22.1 %attend_forward.2 = (bf16[3,256,768]{2,1,0:T(8,128)(2,1)}, bf16[3,4,256,384]{3,2,1,0:T(8,128)(2,1)}, bf16[3,4,256,192]{3,2,1,0:T(8,128)(2,1)}, bf16[3,4,256,384]...) custom-call(bf16[3,256,768]{2,1,0:T(8,128)(2,1)} %pad_maximum_fusion., ...), custom_call_target="tpu_custom_call" | custom-call | flops 4529848320 | bytes 16680960 | tf_op jit(solution)/shard_map/attend_forward/pallas_call | solution.py:337
  198.2 17.5 %lift_forward.2 = (bf16[3,256,3072]{2,1,0:T(8,128)(2,1)}, bf16[3,256,3072]{2,1,0:T(8,128)(2,1)}, bf16[3,256,768]{2,1,0:T(8,128)(2,1)}, bf16[3,256,768]{2,1,0:T(8,128)(2,1)S(1)}) custom-call(bf16[3,256,768]{2,1,0:T(8,128)(2,1)S(1)} %get-tuple-element.81.refs_0_, f32[3,256,768]{2,1,0:T(8,128)} %get-tuple-element.82.refs_1_, ...), custom_call_target="tpu_custom_call" | custom-call | flops 7247757312 | bytes 24843264 | tf_op jit(solution)/shard_map/lift_forward/pallas_call | solution.py:337
  221.2 21.6 %attend_forward.3 = (bf16[3,256,768]{2,1,0:T(8,128)(2,1)S(1)}, bf16[3,4,256,384]{3,2,1,0:T(8,128)(2,1)}, bf16[3,4,256,192]{3,2,1,0:T(8,128)(2,1)}, bf16[3,4,256,...) custom-call(bf16[3,256,768]{2,1,0:T(8,128)(2,1)} %get-tuple-element., ...), custom_call_target="tpu_custom_call" | custom-call | flops 4529848320 | bytes 16680960 | tf_op jit(solution)/shard_map/attend_forward/pallas_call | solution.py:337
  243.8 17.7 %lift_forward.3 = (bf16[3,256,3072]{2,1,0:T(8,128)(2,1)}, bf16[3,256,3072]{2,1,0:T(8,128)(2,1)}, bf16[3,256,768]{2,1,0:T(8,128)(2,1)S(1)}, bf16[3,256,768]{2,1,0:T(8,128)(2,1)S(1)}) custom-call(bf16[3,256,768]{2,1,0:T(8,128)(2,1)S(1)} %get-tuple-element.86.refs_0_, f32[3,256,768]{2,1,0:T(8,128)} %get-tuple-element.87.refs_1_.refs_4_, ...), custom_call_target="tpu_custom_call" | custom-call | flops 7247757312 | bytes 24843264 | tf_op jit(solution)/shard_map/lift_forward/pallas_call | solution.py:337
  261.6 9.8 %lift_backward.2 = (bf16[3,256,768]{2,1,0:T(8,128)(2,1)S(1)}, bf16[3,256,3072]{2,1,0:T(8,128)(2,1)}, f32[3,256,768]{2,1,0:T(8,128)}, f32[3,4,768]{2,1,0:T(4,128)S(1)}, f32[3,8,384]{2,1,0:T(8,128)S(1)}) custom-call(s32[1]{0:T(128)S(6)} %sub.23.refs_0_, bf16[3,256,768]{2,1,0:T(8,128)(2,1)S(1)} %get-tuple-element.219.refs_1_, ...), custom_call_target="tpu_custom_call" | custom-call | flops 7247757312 | bytes 26044416 | tf_op jit(solution)/shard_map/lift_backward/pallas_call | solution.py:337
  272.4 7.4 %attend_backward.2 = (bf16[3,256,768]{2,1,0:T(8,128)(2,1)S(1)}, bf16[3,4,256,384]{3,2,1,0:T(8,128)(2,1)}, bf16[3,4,256,384]{3,2,1,0:T(8,128)(2,1)}, bf16[3,256,7...) custom-call(s32[1]{0:T(128)S(6)} %sub.23.refs_0_, ...), custom_call_target="tpu_custom_call" | custom-call | flops 7247757312 | bytes 20244480 | tf_op jit(solution)/shard_map/attend_backward/pallas_call | solution.py:337
  282.2 37.0 %collective-permute-done.22.refs_1_ = bf16[3,256,768]{2,1,0:T(8,128)(2,1)S(1)} collective-permute-done((bf16[3,256,768]{2,1,0:T(8,128)(2,1)S(1)}, bf16[3,256,768]{2,1,0:T(8,128)(2,1)S(1)}, u32[]{:S(2)}, u32[]{:S(2)}) %collective-permute-start.22) | collective-permute-done | bytes 1179680 | tf_op jit(solution)/shard_map/ppermute | solution.py:600
  319.2 21.2 %lift_backward.3 = (bf16[3,256,768]{2,1,0:T(8,128)(2,1)S(1)}, bf16[3,256,3072]{2,1,0:T(8,128)(2,1)}, f32[3,256,768]{2,1,0:T(8,128)}, f32[3,4,768]{2,1,0:T(4,128)S(1)}, f32[3,8,384]{2,1,0:T(8,128)S(1)}) custom-call(s32[1]{0:T(128)} %bitcast.45.refs_0_, bf16[3,256,768]{2,1,0:T(8,128)(2,1)S(1)} %collective-permute-done.22.refs_1_, ...), custom_call_target="tpu_custom_call" | custom-call | flops 7247757312 | bytes 26044416 | tf_op jit(solution)/shard_map/lift_backward/pallas_call | solution.py:337
  340.4 15.2 %lift_weights.1 = (bf16[4,768,384]{2,1,0:T(8,128)(2,1)}, bf16[4,768,384]{2,1,0:T(8,128)(2,1)}, bf16[4,768,384]{2,1,0:T(8,128)(2,1)}, bf16[4,768,384]{2,1,0:T(8,128)(2,1)}) custom-call(bf16[3,256,768]{2,1,0:T(8,128)(2,1)S(1)} %get-tuple-element.86.refs_0_, bf16[3,256,3072]{2,1,0:T(8,128)(2,1)} %get-tuple-element.102.refs_1_, ...), custom_call_target="tpu_custom_call" | custom-call | flops 7247757312 | bytes 21233664 | tf_op jit(solution)/shard_map/lift_weights/pallas_call | solution.py:358
  361.2 31.6 %attend_backward.3 = (bf16[3,256,768]{2,1,0:T(8,128)(2,1)S(1)}, bf16[3,4,256,384]{3,2,1,0:T(8,128)(2,1)}, bf16[3,4,256,384]{3,2,1,0:T(8,128)(2,1)}, bf16[3,256,7...) custom-call(s32[1]{0:T(128)} %bitcast.45.refs_0_, ...), custom_call_target="tpu_custom_call" | custom-call | flops 7247757312 | bytes 20244480 | tf_op jit(solution)/shard_map/attend_backward/pallas_call | solution.py:337
  392.8 14.0 %collective-permute-done.24 = bf16[4,768,384]{2,1,0:T(8,128)(2,1)} collective-permute-done((bf16[4,768,384]{2,1,0:T(8,128)(2,1)}, bf16[4,768,384]{2,1,0:T(8,128)(2,1)}, u32[]{:S(2)}, u32[]{:S(2)}) %collective-permute-start.24) | collective-permute-done | bytes 2359328 | tf_op jit(solution)/shard_map/ppermute | solution.py:18
  428.8 12.3 %attend_weights.1 = (bf16[2,768,384]{2,1,0:T(8,128)(2,1)}, bf16[2,768,384]{2,1,0:T(8,128)(2,1)S(1)}, bf16[2,768,384]{2,1,0:T(8,128)(2,1)}, bf16[2,768,384]{2,1,0:T(8,128)(2,1)}) custom-call(bf16[3,256,768]{2,1,0:T(8,128)(2,1)} %copy-done.7, bf16[3,4,256,384]{3,2,1,0:T(8,128)(2,1)} %get-tuple-element.128.refs_1_, ...), custom_call_target="tpu_custom_call" | custom-call | flops 5435817984 | bytes 14155776 | tf_op jit(solution)/shard_map/attend_weights/pallas_call | solution.py:358
  446.5 5.0 collective-permute-done.25
  463.9 6.7 %collective-permute-done.32 = bf16[2,768,384]{2,1,0:T(8,128)(2,1)} collective-permute-done((bf16[2,768,384]{2,1,0:T(8,128)(2,1)}, bf16[2,768,384]{2,1,0:T(8,128)(2,1)}, u32[]{:S(2)}, u32[]{:S(2)}) %collective-permute-start.32) | collective-permute-done | bytes 1179680 | tf_op jit(solution)/shard_map/ppermute | solution.py:18
  474.6 11.8 %collective-permute-done.28 = bf16[4,192,384]{2,1,0:T(8,128)(2,1)S(1)} collective-permute-done((bf16[4,192,384]{2,1,0:T(8,128)(2,1)S(1)}, bf16[4,192,384]{2,1,0:T(8,128)(2,1)S(1)}, u32[]{:S(2)}, u32[]{:S(2)}) %collective-permute-start.28) | collective-permute-done | bytes 589856 | tf_op jit(solution)/shard_map/ppermute | solution.py:23
  491.2 13.8 %collective-permute-start.39 = (bf16[2,192,384]{2,1,0:T(8,128)(2,1)}, bf16[2,192,384]{2,1,0:T(8,128)(2,1)}, u32[]{:S(2)}, u32[]{:S(2)}) collective-permute-start(bf16[2,192,384]{2,1,0:T(8,128)(2,1)} %pad_maximum_fusion.11), channel_id=1, source_target_pairs={{0,4},{4,8},{8,12},{12,0},{1,5},{5,9},{9,13},{13,1},{2,6},{6,10},{... | collective-permute-start | bytes 884744 | tf_op jit(solution)/shard_map/ppermute | solution.py:23
  (320 shorter events, 153.3 us)
Async XLA Ops:
  42.6 38.3 %collective-permute-start.7 = (bf16[2,192,768]{2,1,0:T(8,128)(2,1)}, bf16[2,192,768]{2,1,0:T(8,128)(2,1)S(1)}, u32[]{:S(2)}, u32[]{:S(2)}) collective-permute-start(bf16[2,192,768]{2,1,0:T(8,128)(2,1)} %pad_maximum_fusion.5), channel_id=1, source_target_pairs={{0,8},{4,12},{8,0},{12,4},{1,9},{5,13},{9,1},{13,5},{2,10},{6,14},... | collective-permute-start | bytes 1769480 | tf_op jit(solution)/shard_map/ppermute | solution.py:23
  44.2 36.7 %collective-permute-start.8 = (bf16[2,192,768]{2,1,0:T(8,128)(2,1)}, bf16[2,192,768]{2,1,0:T(8,128)(2,1)S(1)}, u32[]{:S(2)}, u32[]{:S(2)}) collective-permute-start(bf16[2,192,768]{2,1,0:T(8,128)(2,1)} %pad_maximum_fusion.5), channel_id=1, source_target_pairs={{0,12},{4,0},{8,4},{12,8},{1,13},{5,1},{9,5},{13,9},{2,14},{6,2},{... | collective-permute-start | bytes 1769480 | tf_op jit(solution)/shard_map/ppermute | solution.py:23
  44.9 73.9 %collective-permute-start.10 = (bf16[784,768]{1,0:T(8,128)(2,1)}, bf16[784,768]{1,0:T(8,128)(2,1)}, u32[]{:S(2)}, u32[]{:S(2)}) collective-permute-start(bf16[784,768]{1,0:T(8,128)(2,1)} %pad_maximum_fusion.refs_5_.refs_7_), channel_id=1, source_target_pairs={{0,2},{1,3},{2,0},{3,1},{4,6},{5,7},{6,4},{7,5},{8,10},{9,11},{10,... | collective-permute-start | bytes 3612680 | tf_op jit(solution)/shard_map/ppermute | solution.py:18
  46.5 72.4 %collective-permute-start.11 = (bf16[784,768]{1,0:T(8,128)(2,1)}, bf16[784,768]{1,0:T(8,128)(2,1)}, u32[]{:S(2)}, u32[]{:S(2)}) collective-permute-start(bf16[784,768]{1,0:T(8,128)(2,1)} %pad_maximum_fusion.refs_5_.refs_7_), channel_id=1, source_target_pairs={{0,3},{1,2},{2,1},{3,0},{4,7},{5,6},{6,5},{7,4},{8,11},{9,10},{10,... | collective-permute-start | bytes 3612680 | tf_op jit(solution)/shard_map/ppermute | solution.py:18
  58.4 60.5 %collective-permute-start.9 = (bf16[784,768]{1,0:T(8,128)(2,1)}, bf16[784,768]{1,0:T(8,128)(2,1)}, u32[]{:S(2)}, u32[]{:S(2)}) collective-permute-start(bf16[784,768]{1,0:T(8,128)(2,1)} %pad_maximum_fusion.refs_5_.refs_7_), channel_id=1, source_target_pairs={{0,1},{1,0},{2,3},{3,2},{4,5},{5,4},{6,7},{7,6},{8,9},{9,8},{10,11... | collective-permute-start | bytes 3612680 | tf_op jit(solution)/shard_map/ppermute | solution.py:18
  82.0 26.3 %all-to-all-start = ((f32[4,12,1152]{2,1,0:T(8,128)}), f32[4,12,1152]{2,1,0:T(8,128)}, u32[]{:S(2)}, u32[]{:S(2)}) async-start(f32[4,12,1152]{2,1,0:T(8,128)} %fusion.1), calls=%async_computation | async-start | bytes 589824 | tf_op jit(solution)/shard_map/all_to_all | solution.py:552
  118.9 29.2 %collective-permute-start.15 = (bf16[2,768,384]{2,1,0:T(8,128)(2,1)}, bf16[2,768,384]{2,1,0:T(8,128)(2,1)S(1)}, u32[]{:S(2)}, u32[]{:S(2)}) collective-permute-start(bf16[2,768,384]{2,1,0:T(8,128)(2,1)} %get-tuple-element.84.refs_6_.refs_7_), channel_id=1, source_target_pairs={{0,2},{1,3},{2,0},{3,1},{4,6},{5,7},{6,4},{7,5},{8,10},{9,11},{10,... | collective-permute-start | bytes 3538952 | tf_op jit(solution)/shard_map/ppermute | solution.py:18
  119.6 78.6 %collective-permute-start.13 = (bf16[2,768,384]{2,1,0:T(8,128)(2,1)}, bf16[2,768,384]{2,1,0:T(8,128)(2,1)}, u32[]{:S(2)}, u32[]{:S(2)}) collective-permute-start(bf16[2,768,384]{2,1,0:T(8,128)(2,1)} %get-tuple-element.84.refs_6_.refs_7_), channel_id=1, source_target_pairs={{0,1},{1,0},{2,3},{3,2},{4,5},{5,4},{6,7},{7,6},{8,9},{9,8},{10,11... | collective-permute-start | bytes 3538952 | tf_op jit(solution)/shard_map/ppermute | solution.py:18
  120.2 53.9 %collective-permute-start.12 = (bf16[2,768,384]{2,1,0:T(8,128)(2,1)}, bf16[2,768,384]{2,1,0:T(8,128)(2,1)}, u32[]{:S(2)}, u32[]{:S(2)}) collective-permute-start(bf16[2,768,384]{2,1,0:T(8,128)(2,1)} %get-tuple-element.83.refs_5_.refs_6_), channel_id=1, source_target_pairs={{0,1},{1,0},{2,3},{3,2},{4,5},{5,4},{6,7},{7,6},{8,9},{9,8},{10,11... | collective-permute-start | bytes 3538952 | tf_op jit(solution)/shard_map/ppermute | solution.py:18
  121.6 76.6 %collective-permute-start.14 = (bf16[2,768,384]{2,1,0:T(8,128)(2,1)}, bf16[2,768,384]{2,1,0:T(8,128)(2,1)}, u32[]{:S(2)}, u32[]{:S(2)}) collective-permute-start(bf16[2,768,384]{2,1,0:T(8,128)(2,1)} %get-tuple-element.83.refs_5_.refs_6_), channel_id=1, source_target_pairs={{0,2},{1,3},{2,0},{3,1},{4,6},{5,7},{6,4},{7,5},{8,10},{9,11},{10,... | collective-permute-start | bytes 3538952 | tf_op jit(solution)/shard_map/ppermute | solution.py:18
  148.0 50.1 %collective-permute-start.17 = (bf16[2,768,384]{2,1,0:T(8,128)(2,1)S(1)}, bf16[2,768,384]{2,1,0:T(8,128)(2,1)}, u32[]{:S(2)}, u32[]{:S(2)}) collective-permute-start(bf16[2,768,384]{2,1,0:T(8,128)(2,1)S(1)} %collective-permute-done.15.refs_10_.refs_11_), channel_id=1, source_target_pairs={{0,1},{1,0},{2,3},{3,2},{4,5},{5,4},{6,7},{7,6},{8,9},{9,8},{10,11... | collective-permute-start | bytes 3538952 | tf_op jit(solution)/shard_map/ppermute | solution.py:18
  280.8 38.4 %collective-permute-start.22 = (bf16[3,256,768]{2,1,0:T(8,128)(2,1)S(1)}, bf16[3,256,768]{2,1,0:T(8,128)(2,1)S(1)}, u32[]{:S(2)}, u32[]{:S(2)}) collective-permute-start(bf16[3,256,768]{2,1,0:T(8,128)(2,1)S(1)} %get-tuple-element.95.refs_14_), channel_id=1, source_target_pairs={{16,0},{17,1},{18,2},{19,3},{20,4},{21,5},{22,6},{23,7},{24,8},{25... | collective-permute-start | bytes 3538952 | tf_op jit(solution)/shard_map/ppermute | solution.py:600
  355.6 51.2 %collective-permute-start.24 = (bf16[4,768,384]{2,1,0:T(8,128)(2,1)}, bf16[4,768,384]{2,1,0:T(8,128)(2,1)}, u32[]{:S(2)}, u32[]{:S(2)}) collective-permute-start(bf16[4,768,384]{2,1,0:T(8,128)(2,1)} %get-tuple-element.107), channel_id=1, source_target_pairs={{0,2},{1,3},{2,0},{3,1},{4,6},{5,7},{6,4},{7,5},{8,10},{9,11},{10,... | collective-permute-start | bytes 7077896 | tf_op jit(solution)/shard_map/ppermute | solution.py:18
  356.3 53.2 %collective-permute-start.23 = (bf16[4,768,384]{2,1,0:T(8,128)(2,1)}, bf16[4,768,384]{2,1,0:T(8,128)(2,1)}, u32[]{:S(2)}, u32[]{:S(2)}) collective-permute-start(bf16[4,768,384]{2,1,0:T(8,128)(2,1)} %get-tuple-element.105), channel_id=1, source_target_pairs={{0,1},{1,0},{2,3},{3,2},{4,5},{5,4},{6,7},{7,6},{8,9},{9,8},{10,11... | collective-permute-start | bytes 7077896 | tf_op jit(solution)/shard_map/ppermute | solution.py:18
  357.8 59.6 %collective-permute-start.19 = (bf16[3,64,768]{2,1,0:T(8,128)(2,1)}, bf16[3,64,768]{2,1,0:T(8,128)(2,1)S(1)}, u32[]{:S(2)}, u32[]{:S(2)}) collective-permute-start(bf16[3,64,768]{2,1,0:T(8,128)(2,1)} %get-tuple-element.228), channel_id=1, source_target_pairs={{0,1},{1,0},{2,3},{3,2},{4,5},{5,4},{6,7},{7,6},{8,9},{9,8},{10,11... | collective-permute-start | bytes 884744 | tf_op jit(solution)/shard_map/ppermute | solution.py:18
  359.2 58.2 %collective-permute-start.20 = (bf16[3,64,768]{2,1,0:T(8,128)(2,1)S(1)}, bf16[3,64,768]{2,1,0:T(8,128)(2,1)S(1)}, u32[]{:S(2)}, u32[]{:S(2)}) collective-permute-start(bf16[3,64,768]{2,1,0:T(8,128)(2,1)S(1)} %get-tuple-element.227), channel_id=1, source_target_pairs={{0,2},{1,3},{2,0},{3,1},{4,6},{5,7},{6,4},{7,5},{8,10},{9,11},{10,... | collective-permute-start | bytes 884744 | tf_op jit(solution)/shard_map/ppermute | solution.py:18
  360.6 56.8 %collective-permute-start.21 = (bf16[3,64,768]{2,1,0:T(8,128)(2,1)S(1)}, bf16[3,64,768]{2,1,0:T(8,128)(2,1)}, u32[]{:S(2)}, u32[]{:S(2)}) collective-permute-start(bf16[3,64,768]{2,1,0:T(8,128)(2,1)S(1)} %get-tuple-element.226), channel_id=1, source_target_pairs={{0,3},{1,2},{2,1},{3,0},{4,7},{5,6},{6,5},{7,4},{8,11},{9,10},{10,... | collective-permute-start | bytes 884744 | tf_op jit(solution)/shard_map/ppermute | solution.py:18
  422.8 28.8 %collective-permute-start.25 = (bf16[2,768,384]{2,1,0:T(8,128)(2,1)}, bf16[2,768,384]{2,1,0:T(8,128)(2,1)}, u32[]{:S(2)}, u32[]{:S(2)}) collective-permute-start(bf16[2,768,384]{2,1,0:T(8,128)(2,1)} %add_convert_fusion.3), channel_id=1, source_target_pairs={{0,2},{1,3},{2,0},{3,1},{4,6},{5,7},{6,4},{7,5},{8,10},{9,11},{10,... | collective-permute-start | bytes 3538952 | tf_op jit(solution)/shard_map/ppermute | solution.py:18
  428.5 25.7 %collective-permute-start.26 = (bf16[2,768,384]{2,1,0:T(8,128)(2,1)}, bf16[2,768,384]{2,1,0:T(8,128)(2,1)}, u32[]{:S(2)}, u32[]{:S(2)}) collective-permute-start(bf16[2,768,384]{2,1,0:T(8,128)(2,1)} %add_convert_fusion.2), channel_id=1, source_target_pairs={{0,1},{1,0},{2,3},{3,2},{4,5},{5,4},{6,7},{7,6},{8,9},{9,8},{10,11... | collective-permute-start | bytes 3538952 | tf_op jit(solution)/shard_map/ppermute | solution.py:18
  441.1 29.4 %collective-permute-start.32 = (bf16[2,768,384]{2,1,0:T(8,128)(2,1)}, bf16[2,768,384]{2,1,0:T(8,128)(2,1)}, u32[]{:S(2)}, u32[]{:S(2)}) collective-permute-start(bf16[2,768,384]{2,1,0:T(8,128)(2,1)} %get-tuple-element.137), channel_id=1, source_target_pairs={{0,2},{1,3},{2,0},{3,1},{4,6},{5,7},{6,4},{7,5},{8,10},{9,11},{10,... | collective-permute-start | bytes 3538952 | tf_op jit(solution)/shard_map/ppermute | solution.py:18
  442.8 30.2 %collective-permute-start.30 = (bf16[2,768,384]{2,1,0:T(8,128)(2,1)}, bf16[2,768,384]{2,1,0:T(8,128)(2,1)}, u32[]{:S(2)}, u32[]{:S(2)}) collective-permute-start(bf16[2,768,384]{2,1,0:T(8,128)(2,1)} %get-tuple-element.134), channel_id=1, source_target_pairs={{0,1},{1,0},{2,3},{3,2},{4,5},{5,4},{6,7},{7,6},{8,9},{9,8},{10,11... | collective-permute-start | bytes 3538952 | tf_op jit(solution)/shard_map/ppermute | solution.py:18
  458.1 28.3 %collective-permute-start.28 = (bf16[4,192,384]{2,1,0:T(8,128)(2,1)S(1)}, bf16[4,192,384]{2,1,0:T(8,128)(2,1)S(1)}, u32[]{:S(2)}, u32[]{:S(2)}) collective-permute-start(bf16[4,192,384]{2,1,0:T(8,128)(2,1)S(1)} %pad_maximum_fusion.7), channel_id=1, source_target_pairs={{0,8},{4,12},{8,0},{12,4},{1,9},{5,13},{9,1},{13,5},{2,10},{6,14},... | collective-permute-start | bytes 1769480 | tf_op jit(solution)/shard_map/ppermute | solution.py:23
  459.3 27.1 %collective-permute-start.29 = (bf16[4,192,384]{2,1,0:T(8,128)(2,1)S(1)}, bf16[4,192,384]{2,1,0:T(8,128)(2,1)S(1)}, u32[]{:S(2)}, u32[]{:S(2)}) collective-permute-start(bf16[4,192,384]{2,1,0:T(8,128)(2,1)S(1)} %pad_maximum_fusion.8), channel_id=1, source_target_pairs={{0,12},{4,0},{8,4},{12,8},{1,13},{5,1},{9,5},{13,9},{2,14},{6,2},{... | collective-permute-start | bytes 1769480 | tf_op jit(solution)/shard_map/ppermute | solution.py:23
  491.2 36.1 %collective-permute-start.39 = (bf16[2,192,384]{2,1,0:T(8,128)(2,1)}, bf16[2,192,384]{2,1,0:T(8,128)(2,1)}, u32[]{:S(2)}, u32[]{:S(2)}) collective-permute-start(bf16[2,192,384]{2,1,0:T(8,128)(2,1)} %pad_maximum_fusion.11), channel_id=1, source_target_pairs={{0,4},{4,8},{8,12},{12,0},{1,5},{5,9},{9,13},{13,1},{2,6},{6,10},{... | collective-permute-start | bytes 884744 | tf_op jit(solution)/shard_map/ppermute | solution.py:23
  (55 other events, 834.3 us)

commit v4 on v3

--- a/solution.py
+++ b/solution.py
@@ -91,7 +91,7 @@
     return total
 
 
-VMEM_BYTES = 50 * 1024 * 1024
+VMEM_BYTES = 34 * 1024 * 1024
 GELU_A = 0.7978845608028654
 GELU_B = 0.044715
 
@@ -548,9 +548,10 @@
     pack_own = after(pack_own, tokens_in)
     pack_w = [pack_own] + [swap(pack_own, "tensor", j) for j in range(1, ways)]
     second_kind = gather_dp(after(jnp.stack([w_up[0], w_down[0].T]), pack_own))
-    mod_terms = dot(after(act_all, second_kind), mod_w, "kgd,dm->kgm")
-    mod_block = jnp.sum(lax.all_to_all(mod_terms, "dp", 0, 0), axis=0)
-    mod_block = lax.all_to_all(mod_block.reshape(ways, share, mod_cols), "tensor", 0, 0)
+    mod_terms = dot(after(act_all, pack_own), mod_w, "kgd,dm->kgm")
+    mod_terms = mod_terms.reshape(dps * ways, share, mod_cols)
+    mod_block = lax.all_to_all(mod_terms, ("dp", "tensor"), 0, 0)
+    mod_block = jnp.sum(mod_block.reshape(dps, ways, share, mod_cols), axis=0)
     both_own = jnp.transpose(second_kind, (1, 0, 2, 3)).reshape(2, width, hidden_cols)
 
     bias_rel = jnp.stack([part[width:].reshape(-1)[: dps * bias_size] for part in pack_w])
@@ -596,11 +597,11 @@
 
     grad_out = tokens_in * own_mask[:, None, None].astype(BF16)
     lift_1, _ = lift_backward(grad_out, mod6, weights, saved_b, 1 - on_first)
-    attend_1, _ = attend_backward(lift_1[2], incoming, mod6, weights, saved_a, 1 - on_first)
+    layer_out = handed_back(output)
+    grad_middle, layer_out = lax.optimization_barrier((lift_1[2], layer_out))
+    attend_1, _ = attend_backward(grad_middle, incoming, mod6, weights, saved_a, 1 - on_first)
     back = lax.ppermute(attend_1[3], "section", [(1, 0)])
 
-    layer_out = handed_back(output)
-    back = after(back, layer_out)
     lift_outs, kept_b = lift_backward(back, mod6, weights, saved_b, on_first, lift_1)
     lift_slabs = lift_weights(kept_b)
     attend_outs, kept_a = attend_backward(
@@ -611,7 +612,7 @@
     attend_slabs = attend_weights(kept_a)
     near_a, onward_a = first_hop(*lift_slabs[:2], 1)
     near_b, onward_b = first_hop(*lift_slabs[2:], 2)
-    sums_a, sums_b = after((sums_a, sums_b), onward_a, onward_b)
+    sums_a, sums_b = after((sums_a, sums_b), onward_a, onward_b, attend_slabs)
 
     grad_mod = jnp.concatenate([sums_a[0][:, :3], sums_b[0][:, :3]], axis=1)
     grad_mod = grad_mod.reshape(share, 6 * width).astype(BF16)
@@ -647,7 +648,7 @@
     out_lift = scatter_rows([lift_a, lift_b])
     sum_qk = second_hop(attend_slabs[1], near_a, onward_a, 2)
     sum_vp = second_hop(attend_slabs[3], near_b, onward_b, 1)
-    out_attend = scatter_rows(after([sum_qk, sum_vp], out_lift))
+    out_attend = scatter_rows([sum_qk, sum_vp])
     shard_down = jnp.concatenate([out_lift[0], out_lift[2]], axis=1).T
     shard_up = jnp.concatenate([out_lift[1], out_lift[3]], axis=1)
     shard_qkv = jnp.concatenate([out_attend[0], out_attend[1][:, :qkv_cols]], axis=1)

time: 544 us -> 535 us (0.983)
  starting transfers between devices: 107 us -> 76.6 us
  local copies, waits for them, and re-layouts: 27.3 us -> 51.3 us
  Pallas kernels: 176 us -> 157 us
  blocking collectives: 0 us -> 7.71 us
  waiting for transfers between devices: 187 us -> 194 us
    unnamed x68 -> x114, local copies, waits for them, and re-layouts: 7.6 us -> 30.6 us
    all_to_all x3 -> x1, starting transfers between devices: 24.1 us -> 4.98 us  [body(): mod_block = lax.all_to_all(mod_terms, ('dp', 'tensor'), 0, 0)]
    pallas_call x8, Pallas kernels: 149 us -> 137 us  [over_latents(): pl.pallas_call(flagged if flags else whole, grid=(varying[0].shape[0],),...]
    ppermute x29, waiting for transfers between devices: 81 us -> 92.5 us  [swap(): return lax.ppermute(shard, axis, [(i, i ^ step) for i in range(peers)])]
    ppermute x12, starting transfers between devices: 38.6 us -> 28.1 us  [turned(): lax.ppermute(shard, axis, [(i, (i + by) % peers) for i in range(peers)])]
    all_to_all x0 -> x1, blocking collectives: none -> 7.71 us  [body(): arrivals = lax.all_to_all(arrivals, 'tensor', 0, 0)]
    pallas_call x2, Pallas kernels: 27.4 us -> 20.2 us  [at_once(): pl.pallas_call(lambda *refs: kernel(refs), in_specs=[pl.BlockSpec(memory_...]
    all_to_all x3 -> x1, waiting for transfers between devices: 14.9 us -> 11.8 us  [body(): mod_block = lax.all_to_all(mod_terms, ('dp', 'tensor'), 0, 0)]
  transfers between devices with their start and end apart: 48 -> 46, of which waited for: 20 -> 23; matrix products, arithmetic and copies ran while one was open for 9% -> 9% of each run, Pallas kernels for 12% -> 13%
where the time goes in v4:
time: 535 us; the launch traced here: 530 us
  waiting for transfers between devices  194 us (36%)
  Pallas kernels  157 us (29%)
  starting transfers between devices  76.6 us (14%)
  local copies, waits for them, and re-layouts  51.3 us (10%)
  other arithmetic  38.3 us (7%)
  blocking collectives  7.71 us (1%)
    pallas_call x8, Pallas kernels, over_latents(): pl.pallas_call(flagged if flags else whole, grid=(varying[0].shape[0],),...  137 us
    ppermute x29, waiting for transfers between devices, swap(): return lax.ppermute(shard, axis, [(i, i ^ step) for i in range(peers)])  92.5 us
    ppermute x12, waiting for transfers between devices, turned(): lax.ppermute(shard, axis, [(i, (i + by) % peers) for i in range(peers)])  48.7 us
    ppermute x1, waiting for transfers between devices, body(): back = lax.ppermute(attend_1[3], 'section', [(1, 0)])  34.9 us
    ppermute x29, starting transfers between devices, swap(): return lax.ppermute(shard, axis, [(i, i ^ step) for i in range(peers)])  32.5 us
    unnamed x114, local copies, waits for them, and re-layouts  30.6 us
    ppermute x12, starting transfers between devices, turned(): lax.ppermute(shard, axis, [(i, (i + by) % peers) for i in range(peers)])  28.1 us
    pallas_call x2, Pallas kernels, at_once(): pl.pallas_call(lambda *refs: kernel(refs), in_specs=[pl.BlockSpec(memory_...  20.2 us
  transfers between devices with their start and end apart: 46, of which 23 were waited for; matrix products, arithmetic and copies ran while one was open for 9% of the time, Pallas kernels for 13%

profile of v4, /device:TPU:0, one launch (start us, length us, event | category | flops | bytes accessed | tf_op | source)
XLA Modules:
  0.0 530.0 jit_solution(15086503231002297495)
XLA Ops:
  23.0 10.8 %collective-permute-done.4 = bf16[208,768]{1,0:T(8,128)(2,1)S(1)} collective-permute-done((bf16[208,768]{1,0:T(8,128)(2,1)}, bf16[208,768]{1,0:T(8,128)(2,1)S(1)}, u32[]{:S(2)}, u32[]{:S(2)}) %collective-permute-start.4) | collective-permute-done | bytes 319520 | tf_op jit(solution)/shard_map/ppermute | solution.py:23
  35.3 7.3 %collective-permute-start.9 = (bf16[2,192,768]{2,1,0:T(8,128)(2,1)}, bf16[2,192,768]{2,1,0:T(8,128)(2,1)S(1)}, u32[]{:S(2)}, u32[]{:S(2)}) collective-permute-start(bf16[2,192,768]{2,1,0:T(8,128)(2,1)} %pad_maximum_fusion.5), channel_id=1, source_target_pairs={{0,4},{4,8},{8,12},{12,0},{1,5},{5,9},{9,13},{13,1},{2,6},{6,10},{... | collective-permute-start | bytes 1769480 | tf_op jit(solution)/shard_map/ppermute | solution.py:23
  43.8 5.0 all-to-all-start
  61.3 11.8 %all-to-all-done = f32[16,3,1152]{2,1,0:T(4,128)} async-done(((f32[16,3,1152]{2,1,0:T(4,128)}), f32[16,3,1152]{2,1,0:T(4,128)}, u32[]{:S(2)}, u32[]{:S(2)}) %all-to-all-start) | async-done | bytes 221216 | tf_op jit(solution)/shard_map/all_to_all | solution.py:553
  76.0 11.3 %collective-permute-done.10 = bf16[2,192,768]{2,1,0:T(8,128)(2,1)} collective-permute-done((bf16[2,192,768]{2,1,0:T(8,128)(2,1)}, bf16[2,192,768]{2,1,0:T(8,128)(2,1)}, u32[]{:S(2)}, u32[]{:S(2)}) %collective-permute-start.10) | collective-permute-done | bytes 589856 | tf_op jit(solution)/shard_map/ppermute | solution.py:23
  93.6 14.0 %collective-permute-done.7.refs_7_.refs_9_ = bf16[784,768]{1,0:T(8,128)(2,1)} collective-permute-done((bf16[784,768]{1,0:T(8,128)(2,1)}, bf16[784,768]{1,0:T(8,128)(2,1)}, u32[]{:S(2)}, u32[]{:S(2)}) %collective-permute-start.7) | collective-permute-done | bytes 1204256 | tf_op jit(solution)/shard_map/ppermute | solution.py:18
  114.3 23.9 %collective-permute-done.12.refs_7_.refs_8_ = bf16[2,768,384]{2,1,0:T(8,128)(2,1)} collective-permute-done((bf16[2,768,384]{2,1,0:T(8,128)(2,1)S(1)}, bf16[2,768,384]{2,1,0:T(8,128)(2,1)}, u32[]{:S(2)}, u32[]{:S(2)}) %collective-permute-start.12) | collective-permute-done | bytes 1179680 | tf_op jit(solution)/shard_map/ppermute | solution.py:18
  143.1 21.6 %attend_forward.2 = (bf16[3,256,768]{2,1,0:T(8,128)(2,1)}, bf16[3,4,256,384]{3,2,1,0:T(8,128)(2,1)}, bf16[3,4,256,192]{3,2,1,0:T(8,128)(2,1)}, bf16[3,4,256,384]...) custom-call(bf16[3,256,768]{2,1,0:T(8,128)(2,1)S(1)} %copy-done.10, ...), custom_call_target="tpu_custom_call" | custom-call | flops 4529848320 | bytes 16680960 | tf_op jit(solution)/shard_map/attend_forward/pallas_call | solution.py:337
  164.9 24.0 %collective-permute-done.16.refs_11_.refs_12_ = bf16[2,768,384]{2,1,0:T(8,128)(2,1)} collective-permute-done((bf16[2,768,384]{2,1,0:T(8,128)(2,1)}, bf16[2,768,384]{2,1,0:T(8,128)(2,1)}, u32[]{:S(2)}, u32[]{:S(2)}) %collective-permute-start.16) | collective-permute-done | bytes 1179680 | tf_op jit(solution)/shard_map/ppermute | solution.py:18
  188.9 16.7 %lift_forward.2 = (bf16[3,256,3072]{2,1,0:T(8,128)(2,1)}, bf16[3,256,3072]{2,1,0:T(8,128)(2,1)}, bf16[3,256,768]{2,1,0:T(8,128)(2,1)}, bf16[3,256,768]{2,1,0:T(8,128)(2,1)}) custom-call(bf16[3,256,768]{2,1,0:T(8,128)(2,1)S(1)} %get-tuple-element.79.refs_0_, f32[3,256,768]{2,1,0:T(8,128)S(1)} %get-tuple-element.80.refs_1_, ...), custom_call_target="tpu_custom_call" | custom-call | flops 7247757312 | bytes 24843264 | tf_op jit(solution)/shard_map/lift_forward/pallas_call | solution.py:337
  211.3 20.1 %attend_forward.3 = (bf16[3,256,768]{2,1,0:T(8,128)(2,1)S(1)}, bf16[3,4,256,384]{3,2,1,0:T(8,128)(2,1)S(1)}, bf16[3,4,256,192]{3,2,1,0:T(8,128)(2,1)S(1)}, bf16[...) custom-call(bf16[3,256,768]{2,1,0:T(8,128)(2,1)S(1)} %get-tuple-elem, ...), custom_call_target="tpu_custom_call" | custom-call | flops 4529848320 | bytes 16680960 | tf_op jit(solution)/shard_map/attend_forward/pallas_call | solution.py:337
  233.7 18.5 %lift_forward.3 = (bf16[3,256,3072]{2,1,0:T(8,128)(2,1)S(1)}, bf16[3,256,3072]{2,1,0:T(8,128)(2,1)}, bf16[3,256,768]{2,1,0:T(8,128)(2,1)S(1)}, bf16[3,256,768]{2,1,0:T(8,128)(2,1)S(1)}) custom-call(bf16[3,256,768]{2,1,0:T(8,128)(2,1)S(1)} %get-tuple-element.85.refs_0_, f32[3,256,768]{2,1,0:T(8,128)S(1)} %get-tuple-element.86.refs_1_.refs_4_, ...), custom_call_target="tpu_custom_call" | custom-call | flops 7247757312 | bytes 24843264 | tf_op jit(solution)/shard_map/lift_forward/pallas_call | solution.py:337
  258.1 7.7 %lift_backward.2 = (bf16[3,256,768]{2,1,0:T(8,128)(2,1)S(1)}, bf16[3,256,3072]{2,1,0:T(8,128)(2,1)}, f32[3,256,768]{2,1,0:T(8,128)S(1)}, f32[3,4,768]{2,1,0:T(4,128)S(1)}, f32[3,8,384]{2,1,0:T(8,128)S(1)}) custom-call(s32[1]{0:T(128)S(6)} %sub.20.refs_0_, bf16[3,256,768]{2,1,0:T(8,128)(2,1)S(1)} %get-tuple-element.239.refs_1_, ...), custom_call_target="tpu_custom_call" | custom-call | flops 7247757312 | bytes 26044416 | tf_op jit(solution)/shard_map/lift_backward/pallas_call | solution.py:337
  266.8 4.7 collective-permute-done.20
  281.3 34.9 %collective-permute-done.22.refs_1_ = bf16[3,256,768]{2,1,0:T(8,128)(2,1)S(1)} collective-permute-done((bf16[3,256,768]{2,1,0:T(8,128)(2,1)S(1)}, bf16[3,256,768]{2,1,0:T(8,128)(2,1)S(1)}, u32[]{:S(2)}, u32[]{:S(2)}) %collective-permute-start.22) | collective-permute-done | bytes 1179680 | tf_op jit(solution)/shard_map/ppermute | solution.py:603
  317.5 19.9 %lift_backward.3 = (bf16[3,256,768]{2,1,0:T(8,128)(2,1)S(1)}, bf16[3,256,3072]{2,1,0:T(8,128)(2,1)}, f32[3,256,768]{2,1,0:T(8,128)S(1)}, f32[3,4,768]{2,1,0:T(4,128)S(1)}, f32[3,8,384]{2,1,0:T(8,128)S(1)}) custom-call(s32[1]{0:T(128)} %bitcast.refs_0_, bf16[3,256,768]{2,1,0:T(8,128)(2,1)S(1)} %collective-permute-done.22.refs_1_, ...), custom_call_target="tpu_custom_call" | custom-call | flops 7247757312 | bytes 26044416 | tf_op jit(solution)/shard_map/lift_backward/pallas_call | solution.py:337
  341.1 12.7 %lift_weights.1 = (bf16[4,768,384]{2,1,0:T(8,128)(2,1)}, bf16[4,768,384]{2,1,0:T(8,128)(2,1)S(1)}, bf16[4,768,384]{2,1,0:T(8,128)(2,1)}, bf16[4,768,384]{2,1,0:T(8,128)(2,1)S(1)}) custom-call(bf16[3,256,768]{2,1,0:T(8,128)(2,1)S(1)} %copy-done.37, bf16[3,256,3072]{2,1,0:T(8,128)(2,1)S(1)} %copy-done.15, bf16[3,256,768]{2,1,0:T(8,128)(2,1)S(1)} %get-tuple-element.103.refs_2_, ...), custom_call_target="tpu_custom_call" | custom-call | flops 7247757312 | bytes 21233664 | tf_op jit(solution)/shard_map/lift_weights/pallas_call | solution.py:358
  359.0 29.6 %attend_backward.3 = (bf16[3,256,768]{2,1,0:T(8,128)(2,1)S(1)}, bf16[3,4,256,384]{3,2,1,0:T(8,128)(2,1)S(1)}, bf16[3,4,256,384]{3,2,1,0:T(8,128)(2,1)S(1)}, bf16...) custom-call(s32[1]{0:T(128)} %bitcast.refs_0_, f32[3,256,768]{2,1,0:T(8,128)S(1)} %copy-done.17, ...), custom_call_target="tpu_custom_call" | custom-call | flops 7247757312 | bytes 20244480 | tf_op jit(solution)/shard_map/attend_backward/pallas_call | solution.py:337
  392.6 7.5 %attend_weights.1 = (bf16[2,768,384]{2,1,0:T(8,128)(2,1)S(1)}, bf16[2,768,384]{2,1,0:T(8,128)(2,1)S(1)}, bf16[2,768,384]{2,1,0:T(8,128)(2,1)S(1)}, bf16[2,768,384]{2,1,0:T(8,128)(2,1)S(1)}) custom-call(bf16[3,256,768]{2,1,0:T(8,128)(2,1)S(1)} %copy-done.35, bf16[3,4,256,384]{3,2,1,0:T(8,128)(2,1)S(1)} %get-tuple-element.120.refs_1_, ...), custom_call_target="tpu_custom_call" | custom-call | flops 5435817984 | bytes 14155776 | tf_op jit(solution)/shard_map/attend_weights/pallas_call | solution.py:358
  408.5 7.7 %all_to_all.34 = f32[4,1,6144]{2,1,0:T(1,128)S(1)} all-to-all(f32[4,1,6144]{2,1,0:T(1,128)S(1)} %all_to_all.23), channel_id=1, replica_groups=mesh['section'=2,'dp'=4,'tensor'=4] {'tensor'}, dimensions={0} | all-to-all | bytes 196608 | tf_op jit(solution)/shard_map/all_to_all | solution.py:635
  424.9 4.7 all-to-all-done.2
  432.4 8.2 %collective-permute-done.26 = bf16[2,768,384]{2,1,0:T(8,128)(2,1)} collective-permute-done((bf16[2,768,384]{2,1,0:T(8,128)(2,1)}, bf16[2,768,384]{2,1,0:T(8,128)(2,1)}, u32[]{:S(2)}, u32[]{:S(2)}) %collective-permute-start.26) | collective-permute-done | bytes 1179680 | tf_op jit(solution)/shard_map/ppermute | solution.py:18
  454.4 10.0 %collective-permute-done.32 = bf16[2,768,384]{2,1,0:T(8,128)(2,1)} collective-permute-done((bf16[2,768,384]{2,1,0:T(8,128)(2,1)}, bf16[2,768,384]{2,1,0:T(8,128)(2,1)}, u32[]{:S(2)}, u32[]{:S(2)}) %collective-permute-start.32) | collective-permute-done | bytes 1179680 | tf_op jit(solution)/shard_map/ppermute | solution.py:18
  469.8 22.6 %collective-permute-done.28 = bf16[4,192,384]{2,1,0:T(8,128)(2,1)S(1)} collective-permute-done((bf16[4,192,384]{2,1,0:T(8,128)(2,1)S(1)}, bf16[4,192,384]{2,1,0:T(8,128)(2,1)S(1)}, u32[]{:S(2)}, u32[]{:S(2)}) %collective-permute-start.28) | collective-permute-done | bytes 589856 | tf_op jit(solution)/shard_map/ppermute | solution.py:23
  (365 shorter events, 172.7 us)
Async XLA Ops:
  35.3 22.9 %collective-permute-start.9 = (bf16[2,192,768]{2,1,0:T(8,128)(2,1)}, bf16[2,192,768]{2,1,0:T(8,128)(2,1)S(1)}, u32[]{:S(2)}, u32[]{:S(2)}) collective-permute-start(bf16[2,192,768]{2,1,0:T(8,128)(2,1)} %pad_maximum_fusion.5), channel_id=1, source_target_pairs={{0,4},{4,8},{8,12},{12,0},{1,5},{5,9},{9,13},{13,1},{2,6},{6,10},{... | collective-permute-start | bytes 1769480 | tf_op jit(solution)/shard_map/ppermute | solution.py:23
  43.8 29.3 %all-to-all-start = ((f32[16,3,1152]{2,1,0:T(4,128)}), f32[16,3,1152]{2,1,0:T(4,128)}, u32[]{:S(2)}, u32[]{:S(2)}) async-start(f32[16,3,1152]{2,1,0:T(4,128)} %copy.102), calls=%async_computation | async-start | bytes 589824 | tf_op jit(solution)/shard_map/all_to_all | solution.py:553
  48.8 38.5 %collective-permute-start.10 = (bf16[2,192,768]{2,1,0:T(8,128)(2,1)}, bf16[2,192,768]{2,1,0:T(8,128)(2,1)}, u32[]{:S(2)}, u32[]{:S(2)}) collective-permute-start(bf16[2,192,768]{2,1,0:T(8,128)(2,1)} %pad_maximum_fusion.5), channel_id=1, source_target_pairs={{0,8},{4,12},{8,0},{12,4},{1,9},{5,13},{9,1},{13,5},{2,10},{6,14},... | collective-permute-start | bytes 1769480 | tf_op jit(solution)/shard_map/ppermute | solution.py:23
  51.6 41.2 %collective-permute-start.8 = (bf16[784,768]{1,0:T(8,128)(2,1)}, bf16[784,768]{1,0:T(8,128)(2,1)}, u32[]{:S(2)}, u32[]{:S(2)}) collective-permute-start(bf16[784,768]{1,0:T(8,128)(2,1)} %pad_maximum_fusion.refs_5_.refs_7_), channel_id=1, source_target_pairs={{0,3},{1,2},{2,1},{3,0},{4,7},{5,6},{6,5},{7,4},{8,11},{9,10},{10,... | collective-permute-start | bytes 3612680 | tf_op jit(solution)/shard_map/ppermute | solution.py:18
  53.9 53.7 %collective-permute-start.7 = (bf16[784,768]{1,0:T(8,128)(2,1)}, bf16[784,768]{1,0:T(8,128)(2,1)}, u32[]{:S(2)}, u32[]{:S(2)}) collective-permute-start(bf16[784,768]{1,0:T(8,128)(2,1)} %pad_maximum_fusion.refs_5_.refs_7_), channel_id=1, source_target_pairs={{0,2},{1,3},{2,0},{3,1},{4,6},{5,7},{6,4},{7,5},{8,10},{9,11},{10,... | collective-permute-start | bytes 3612680 | tf_op jit(solution)/shard_map/ppermute | solution.py:18
  54.5 53.9 %collective-permute-start.6 = (bf16[784,768]{1,0:T(8,128)(2,1)}, bf16[784,768]{1,0:T(8,128)(2,1)}, u32[]{:S(2)}, u32[]{:S(2)}) collective-permute-start(bf16[784,768]{1,0:T(8,128)(2,1)} %pad_maximum_fusion.refs_5_.refs_7_), channel_id=1, source_target_pairs={{0,1},{1,0},{2,3},{3,2},{4,5},{5,4},{6,7},{7,6},{8,9},{9,8},{10,11... | collective-permute-start | bytes 3612680 | tf_op jit(solution)/shard_map/ppermute | solution.py:18
  59.0 29.4 %collective-permute-start.11 = (bf16[2,192,768]{2,1,0:T(8,128)(2,1)}, bf16[2,192,768]{2,1,0:T(8,128)(2,1)}, u32[]{:S(2)}, u32[]{:S(2)}) collective-permute-start(bf16[2,192,768]{2,1,0:T(8,128)(2,1)} %pad_maximum_fusion.5), channel_id=1, source_target_pairs={{0,12},{4,0},{8,4},{12,8},{1,13},{5,1},{9,5},{13,9},{2,14},{6,2},{... | collective-permute-start | bytes 1769480 | tf_op jit(solution)/shard_map/ppermute | solution.py:23
  109.2 29.0 %collective-permute-start.12 = (bf16[2,768,384]{2,1,0:T(8,128)(2,1)S(1)}, bf16[2,768,384]{2,1,0:T(8,128)(2,1)}, u32[]{:S(2)}, u32[]{:S(2)}) collective-permute-start(bf16[2,768,384]{2,1,0:T(8,128)(2,1)S(1)} %get-tuple-element.82.refs_5_.refs_6_), channel_id=1, source_target_pairs={{0,1},{1,0},{2,3},{3,2},{4,5},{5,4},{6,7},{7,6},{8,9},{9,8},{10,11... | collective-permute-start | bytes 3538952 | tf_op jit(solution)/shard_map/ppermute | solution.py:18
  110.6 29.0 %collective-permute-start.15 = (bf16[2,768,384]{2,1,0:T(8,128)(2,1)S(1)}, bf16[2,768,384]{2,1,0:T(8,128)(2,1)}, u32[]{:S(2)}, u32[]{:S(2)}) collective-permute-start(bf16[2,768,384]{2,1,0:T(8,128)(2,1)S(1)} %get-tuple-element.83.refs_6_.refs_7_), channel_id=1, source_target_pairs={{0,2},{1,3},{2,0},{3,1},{4,6},{5,7},{6,4},{7,5},{8,10},{9,11},{10,... | collective-permute-start | bytes 3538952 | tf_op jit(solution)/shard_map/ppermute | solution.py:18
  112.1 52.6 %collective-permute-start.13 = (bf16[2,768,384]{2,1,0:T(8,128)(2,1)S(1)}, bf16[2,768,384]{2,1,0:T(8,128)(2,1)}, u32[]{:S(2)}, u32[]{:S(2)}) collective-permute-start(bf16[2,768,384]{2,1,0:T(8,128)(2,1)S(1)} %get-tuple-element.83.refs_6_.refs_7_), channel_id=1, source_target_pairs={{0,1},{1,0},{2,3},{3,2},{4,5},{5,4},{6,7},{7,6},{8,9},{9,8},{10,11... | collective-permute-start | bytes 3538952 | tf_op jit(solution)/shard_map/ppermute | solution.py:18
  113.2 51.7 %collective-permute-start.14 = (bf16[2,768,384]{2,1,0:T(8,128)(2,1)S(1)}, bf16[2,768,384]{2,1,0:T(8,128)(2,1)}, u32[]{:S(2)}, u32[]{:S(2)}) collective-permute-start(bf16[2,768,384]{2,1,0:T(8,128)(2,1)S(1)} %get-tuple-element.82.refs_5_.refs_6_), channel_id=1, source_target_pairs={{0,2},{1,3},{2,0},{3,1},{4,6},{5,7},{6,4},{7,5},{8,10},{9,11},{10,... | collective-permute-start | bytes 3538952 | tf_op jit(solution)/shard_map/ppermute | solution.py:18
  138.3 50.7 %collective-permute-start.16 = (bf16[2,768,384]{2,1,0:T(8,128)(2,1)}, bf16[2,768,384]{2,1,0:T(8,128)(2,1)}, u32[]{:S(2)}, u32[]{:S(2)}) collective-permute-start(bf16[2,768,384]{2,1,0:T(8,128)(2,1)} %collective-permute-done.12.refs_7_.refs_8_), channel_id=1, source_target_pairs={{0,2},{1,3},{2,0},{3,1},{4,6},{5,7},{6,4},{7,5},{8,10},{9,11},{10,... | collective-permute-start | bytes 3538952 | tf_op jit(solution)/shard_map/ppermute | solution.py:18
  139.7 49.3 %collective-permute-start.17 = (bf16[2,768,384]{2,1,0:T(8,128)(2,1)}, bf16[2,768,384]{2,1,0:T(8,128)(2,1)}, u32[]{:S(2)}, u32[]{:S(2)}) collective-permute-start(bf16[2,768,384]{2,1,0:T(8,128)(2,1)} %collective-permute-done.15.refs_10_.refs_11_), channel_id=1, source_target_pairs={{0,1},{1,0},{2,3},{3,2},{4,5},{5,4},{6,7},{7,6},{8,9},{9,8},{10,11... | collective-permute-start | bytes 3538952 | tf_op jit(solution)/shard_map/ppermute | solution.py:18
  280.0 36.2 %collective-permute-start.22 = (bf16[3,256,768]{2,1,0:T(8,128)(2,1)S(1)}, bf16[3,256,768]{2,1,0:T(8,128)(2,1)S(1)}, u32[]{:S(2)}, u32[]{:S(2)}) collective-permute-start(bf16[3,256,768]{2,1,0:T(8,128)(2,1)S(1)} %get-tuple-element.96.refs_14_), channel_id=1, source_target_pairs={{16,0},{17,1},{18,2},{19,3},{20,4},{21,5},{22,6},{23,7},{24,8},{25... | collective-permute-start | bytes 3538952 | tf_op jit(solution)/shard_map/ppermute | solution.py:603
  353.8 47.4 %collective-permute-start.23 = (bf16[4,768,384]{2,1,0:T(8,128)(2,1)}, bf16[4,768,384]{2,1,0:T(8,128)(2,1)}, u32[]{:S(2)}, u32[]{:S(2)}) collective-permute-start(bf16[4,768,384]{2,1,0:T(8,128)(2,1)} %get-tuple-element.105), channel_id=1, source_target_pairs={{0,1},{1,0},{2,3},{3,2},{4,5},{5,4},{6,7},{7,6},{8,9},{9,8},{10,11... | collective-permute-start | bytes 7077896 | tf_op jit(solution)/shard_map/ppermute | solution.py:18
  354.4 50.3 %collective-permute-start.24 = (bf16[4,768,384]{2,1,0:T(8,128)(2,1)}, bf16[4,768,384]{2,1,0:T(8,128)(2,1)}, u32[]{:S(2)}, u32[]{:S(2)}) collective-permute-start(bf16[4,768,384]{2,1,0:T(8,128)(2,1)} %get-tuple-element.107), channel_id=1, source_target_pairs={{0,2},{1,3},{2,0},{3,1},{4,6},{5,7},{6,4},{7,5},{8,10},{9,11},{10,... | collective-permute-start | bytes 7077896 | tf_op jit(solution)/shard_map/ppermute | solution.py:18
  416.4 24.2 %collective-permute-start.26 = (bf16[2,768,384]{2,1,0:T(8,128)(2,1)}, bf16[2,768,384]{2,1,0:T(8,128)(2,1)}, u32[]{:S(2)}, u32[]{:S(2)}) collective-permute-start(bf16[2,768,384]{2,1,0:T(8,128)(2,1)} %add_convert_fusion.2), channel_id=1, source_target_pairs={{0,1},{1,0},{2,3},{3,2},{4,5},{5,4},{6,7},{7,6},{8,9},{9,8},{10,11... | collective-permute-start | bytes 3538952 | tf_op jit(solution)/shard_map/ppermute | solution.py:18
  421.8 23.6 %collective-permute-start.25 = (bf16[2,768,384]{2,1,0:T(8,128)(2,1)}, bf16[2,768,384]{2,1,0:T(8,128)(2,1)}, u32[]{:S(2)}, u32[]{:S(2)}) collective-permute-start(bf16[2,768,384]{2,1,0:T(8,128)(2,1)} %add_convert_fusion.3), channel_id=1, source_target_pairs={{0,2},{1,3},{2,0},{3,1},{4,6},{5,7},{6,4},{7,5},{8,10},{9,11},{10,... | collective-permute-start | bytes 3538952 | tf_op jit(solution)/shard_map/ppermute | solution.py:18
  422.2 44.7 %collective-permute-start.30 = (bf16[2,768,384]{2,1,0:T(8,128)(2,1)}, bf16[2,768,384]{2,1,0:T(8,128)(2,1)}, u32[]{:S(2)}, u32[]{:S(2)}) collective-permute-start(bf16[2,768,384]{2,1,0:T(8,128)(2,1)} %copy-done.18), channel_id=1, source_target_pairs={{0,1},{1,0},{2,3},{3,2},{4,5},{5,4},{6,7},{7,6},{8,9},{9,8},{10,11... | collective-permute-start | bytes 3538952 | tf_op jit(solution)/shard_map/ppermute | solution.py:18
  423.9 40.5 %collective-permute-start.32 = (bf16[2,768,384]{2,1,0:T(8,128)(2,1)}, bf16[2,768,384]{2,1,0:T(8,128)(2,1)}, u32[]{:S(2)}, u32[]{:S(2)}) collective-permute-start(bf16[2,768,384]{2,1,0:T(8,128)(2,1)} %copy-done.19), channel_id=1, source_target_pairs={{0,2},{1,3},{2,0},{3,1},{4,6},{5,7},{6,4},{7,5},{8,10},{9,11},{10,... | collective-permute-start | bytes 3538952 | tf_op jit(solution)/shard_map/ppermute | solution.py:18
  451.3 41.0 %collective-permute-start.28 = (bf16[4,192,384]{2,1,0:T(8,128)(2,1)S(1)}, bf16[4,192,384]{2,1,0:T(8,128)(2,1)S(1)}, u32[]{:S(2)}, u32[]{:S(2)}) collective-permute-start(bf16[4,192,384]{2,1,0:T(8,128)(2,1)S(1)} %pad_maximum_fusion.7), channel_id=1, source_target_pairs={{0,8},{4,12},{8,0},{12,4},{1,9},{5,13},{9,1},{13,5},{2,10},{6,14},... | collective-permute-start | bytes 1769480 | tf_op jit(solution)/shard_map/ppermute | solution.py:23
  451.5 40.9 %collective-permute-start.27 = (bf16[4,192,384]{2,1,0:T(8,128)(2,1)S(1)}, bf16[4,192,384]{2,1,0:T(8,128)(2,1)S(1)}, u32[]{:S(2)}, u32[]{:S(2)}) collective-permute-start(bf16[4,192,384]{2,1,0:T(8,128)(2,1)S(1)} %pad_maximum_fusion.6), channel_id=1, source_target_pairs={{0,4},{4,8},{8,12},{12,0},{1,5},{5,9},{9,13},{13,1},{2,6},{6,10},{... | collective-permute-start | bytes 1769480 | tf_op jit(solution)/shard_map/ppermute | solution.py:23
  465.6 32.8 %collective-permute-start.33 = (bf16[1,768,384]{2,1,0:T(8,128)(2,1)S(1)}, bf16[1,768,384]{2,1,0:T(8,128)(2,1)}, u32[]{:S(2)}, u32[]{:S(2)}) collective-permute-start(bf16[1,768,384]{2,1,0:T(8,128)(2,1)S(1)} %add_convert_fusion.5), channel_id=1, source_target_pairs={{0,1},{1,0},{2,3},{3,2},{4,5},{5,4},{6,7},{7,6},{8,9},{9,8},{10,11... | collective-permute-start | bytes 1769480 | tf_op jit(solution)/shard_map/ppermute | solution.py:18
  468.9 32.3 %collective-permute-start.31 = (bf16[1,768,384]{2,1,0:T(8,128)(2,1)}, bf16[1,768,384]{2,1,0:T(8,128)(2,1)}, u32[]{:S(2)}, u32[]{:S(2)}) collective-permute-start(bf16[1,768,384]{2,1,0:T(8,128)(2,1)} %add_convert_fusion.7), channel_id=1, source_target_pairs={{0,2},{1,3},{2,0},{3,1},{4,6},{5,7},{6,4},{7,5},{8,10},{9,11},{10,... | collective-permute-start | bytes 1769480 | tf_op jit(solution)/shard_map/ppermute | solution.py:18
  (76 other events, 800.9 us)
